TPU v7x, 32 devices: a whole 2x2x4 slice. The times are simulated.
32 devices in a mesh: dp: 4 (over z), mp: 8 (over y, x, core).
Axes of the slice: x: 2, y: 2, z: 4, core: 2. Of those that a mesh axis runs over, the one named last changes fastest.
Arguments:
- tokens: bfloat16 [4096, 8, 768], P('mp', 'dp'), may hold values from -6 to 6
- upstream: bfloat16 [4096, 8, 768], P('mp', 'dp'), may hold values from -6 to 6
- pieces: int32 [8], P('dp'), may hold values from 1 to 4, as said below
- layer_index: int32 [1], replicated, may hold values from 1 to 11
- mix_gain: float32 [768], replicated, may hold values from 0.5 to 1.5
- w_input: bfloat16 [768, 2, 384], P(None, None, 'mp'), may hold values from -0.21875 to 0.21875
- w_forget: bfloat16 [768, 384], P(None, 'mp'), may hold values from -0.21875 to 0.21875
- w_outgate: bfloat16 [768, 2, 384], P(None, None, 'mp'), may hold values from -0.21875 to 0.21875
- phase_angle: float32 [384], P('mp'), may hold values from -3.140625 to 3.140625
- lower_logits: float32 [12, 384], P(None, 'mp'), may hold values from -6 to 6
- out_gain: float32 [2, 384], P(None, 'mp'), may hold values from 0.5 to 1.5
- w_output: bfloat16 [2, 384, 768], P(None, 'mp'), may hold values from -0.21875 to 0.21875
- ffn_gain: float32 [768], replicated, may hold values from 0.5 to 1.5
- w_gate: bfloat16 [768, 1536], P(None, 'mp'), may hold values from -0.21875 to 0.21875
- w_up: bfloat16 [768, 1536], P(None, 'mp'), may hold values from -0.21875 to 0.21875
- w_down: bfloat16 [1536, 768], P('mp'), may hold values from -0.15625 to 0.15625
Outputs:
- result: bfloat16 [4096, 8, 768], P('mp', 'dp')
- grad_tokens: bfloat16 [4096, 8, 768], P('mp', 'dp')
- grad_mix_gain: float32 [768], replicated
- grad_w_input: float32 [768, 2, 384], P(None, None, 'mp')
- grad_w_forget: float32 [768, 384], P(None, 'mp')
- grad_w_outgate: float32 [768, 2, 384], P(None, None, 'mp')
- grad_phase: float32 [384], P('mp')
- grad_lower: float32 [12, 384], P(None, 'mp')
- grad_out_gain: float32 [2, 384], P(None, 'mp')
- grad_w_output: float32 [2, 384, 768], P(None, 'mp')
- grad_ffn_gain: float32 [768], replicated
- grad_w_gate: float32 [768, 1536], P(None, 'mp')
- grad_w_up: float32 [768, 1536], P(None, 'mp')
- grad_w_down: float32 [1536, 768], P('mp')
Inputs may be any that keep to these rules, and one draw needn't show every extreme that they name: `pieces`: each group of 4096 positions is one sequence (value 1) or four sequences of 1024 positions (value 4); the 2 groups of each dp index hold a group of value 1, and some group has value 4.
All inputs are finite; a program needn't handle non-finite values.
Results may differ from a plain program's by a relative error of at most 0.014.
Values may be sent and summed in bfloat16 or wider, within the bound.
No kernel may reach another device: no remote copies, remote signals or barrier semaphores. Data moves between devices by JAX's collectives and lax.ppermute only.
A program may use at most 320 MiB of HBM per device.

v0:
```python
import math

import jax
import jax.numpy as jnp
from jax import lax
from jax.sharding import PartitionSpec as P

EPSILON = 1e-06


def rms_scale(values, gain):
    return values * lax.rsqrt(jnp.mean(values * values, axis=-1, keepdims=True) + EPSILON) * gain


def combine(first_pair, second_pair):
    ar_one, ai_one, br_one, bi_one = first_pair
    ar_two, ai_two, br_two, bi_two = second_pair
    return (
        ar_two * ar_one - ai_two * ai_one,
        ar_two * ai_one + ai_two * ar_one,
        ar_two * br_one - ai_two * bi_one + br_two,
        ar_two * bi_one + ai_two * br_one + bi_two,
    )


def to_blocks(values, block_len):
    lead, chans, length = values.shape
    return jnp.transpose(values.reshape(lead, chans, length // block_len, block_len), (3, 0, 1, 2))


def from_blocks(values):
    block_len, lead, chans, count = values.shape
    return jnp.transpose(values, (1, 2, 3, 0)).reshape(lead, chans, count * block_len)


def blocked_scan(terms):
    length = terms[0].shape[-1]
    block_len = math.gcd(length, 16)
    blocked = tuple((to_blocks(term, block_len) for term in terms))
    shape = blocked[0].shape[1:]
    start = (
        jnp.ones(shape, jnp.float32),
        jnp.zeros(shape, jnp.float32),
        jnp.zeros(shape, jnp.float32),
        jnp.zeros(shape, jnp.float32),
    )

    def advance(carry, element):
        joined = combine(carry, element)
        return (joined, joined)

    totals, inner = lax.scan(advance, start, blocked)
    inclusive = lax.associative_scan(combine, totals, axis=2)
    firsts = (
        jnp.ones(shape[:2] + (1,), jnp.float32),
        jnp.zeros(shape[:2] + (1,), jnp.float32),
        jnp.zeros(shape[:2] + (1,), jnp.float32),
        jnp.zeros(shape[:2] + (1,), jnp.float32),
    )
    entering = tuple(
        (
            jnp.concatenate([first, whole[..., :-1]], axis=2)[None]
            for first, whole in zip(firsts, inclusive)
        )
    )
    joined = combine(entering, inner)
    return tuple((from_blocks(part) for part in joined))


def scan_terms(in_pre, forget_pre, lower_bound, phase_rows, keep_mask):
    bound_rows = lower_bound[None, :, None]
    decay = bound_rows + (1.0 - bound_rows) * jax.nn.sigmoid(forget_pre)
    activated = jax.nn.silu(in_pre)
    kept_decay = keep_mask[:, None, :] * decay
    return blocked_scan(
        (
            kept_decay * jnp.cos(phase_rows)[None, :, None],
            kept_decay * jnp.sin(phase_rows)[None, :, None],
            (1.0 - decay) * activated[:, 0],
            (1.0 - decay) * activated[:, 1],
        )
    )


def recurrence(in_pre, forget_pre, lower_bound, phase_rows, keep_mask):
    scanned = scan_terms(in_pre, forget_pre, lower_bound, phase_rows, keep_mask)
    return jnp.stack([scanned[2], scanned[3]], axis=1)


def lower_bound_of(logits, layer_mask):
    return jnp.sum(jax.nn.softmax(logits, axis=0) * layer_mask[:, None], axis=0)


def gated_of(state_part, gate_part, gain_part):
    return state_part * gain_part[None, :, :, None] * jax.nn.silu(gate_part)


def swiglu_back(gate_up, d_hidden):
    gate_pre = gate_up[..., 0, :]
    up_pre = gate_up[..., 1, :]
    sigma = jax.nn.sigmoid(gate_pre)
    d_gate = d_hidden * up_pre * sigma * (1.0 + gate_pre * (1.0 - sigma))
    d_up = d_hidden * gate_pre * sigma
    return jnp.stack([d_gate, d_up], axis=-2).astype(jnp.bfloat16)


def shards(
    tokens,
    upstream,
    pieces,
    layer_index,
    mix_gain,
    w_input,
    w_forget,
    w_outgate,
    phase_angle,
    lower_logits,
    out_gain,
    w_output,
    ffn_gain,
    w_gate,
    w_up,
    w_down,
):
    rows_dev, groups, width = tokens.shape
    mp_count = lax.axis_size("mp")
    seq_len = rows_dev * mp_count
    chan_all = w_input.shape[2] * mp_count
    tok_float = tokens.astype(jnp.float32)
    first_in, first_pull = jax.vjp(rms_scale, tok_float, mix_gain)
    normed = first_in.astype(jnp.bfloat16)
    w_mix = jnp.concatenate([w_input, w_outgate, w_forget[:, None, :]], axis=1)
    seq_span = seq_len // pieces
    layer_mask = (jnp.arange(lower_logits.shape[0], dtype=jnp.int32) < layer_index[0]).astype(
        jnp.float32
    )
    project = jnp.einsum(
        "tsd,dkc->skct",
        lax.all_gather(normed, "mp", axis=0, tiled=True),
        w_mix,
        preferred_element_type=jnp.float32,
    )
    positions = jnp.arange(seq_len, dtype=jnp.int32)
    keep_mask = (positions[None, :] % seq_span[:, None] != 0).astype(jnp.float32)
    lower_bound, bound_pull = jax.vjp(
        lambda logits: lower_bound_of(logits, layer_mask), lower_logits
    )

    def run_states(in_part, forget_part, bound_part, phase_part):
        return recurrence(in_part, forget_part, bound_part, phase_part, keep_mask)

    states, states_pull = jax.vjp(
        run_states, project[:, 0:2], project[:, 4], lower_bound, phase_angle
    )
    squares = lax.psum_scatter(
        jnp.sum(states * states, axis=(1, 2)), "mp", scatter_dimension=1, tiled=True
    )
    mean_square = jnp.transpose(squares) / (2.0 * chan_all)
    inv_rms = lax.rsqrt(mean_square + EPSILON)
    gated_float, gated_pull = jax.vjp(gated_of, states, project[:, 2:4], out_gain)
    gated = gated_float.astype(jnp.bfloat16)
    rows_part = gated
    mix_out = lax.psum_scatter(
        jnp.einsum("skct,kcd->tsd", rows_part, w_output, preferred_element_type=jnp.float32),
        "mp",
        scatter_dimension=0,
        tiled=True,
    )
    mid_stream = tok_float + inv_rms[..., None] * mix_out
    ffn_in, ffn_pull = jax.vjp(rms_scale, mid_stream, ffn_gain)
    ffn_normed = ffn_in.astype(jnp.bfloat16)
    w_both = jnp.stack([w_gate, w_up], axis=1)
    gate_up = jnp.einsum(
        "tsd,dkf->tskf",
        lax.all_gather(ffn_normed, "mp", axis=0, tiled=True),
        w_both,
        preferred_element_type=jnp.float32,
    )
    hidden = (jax.nn.silu(gate_up[:, :, 0]) * gate_up[:, :, 1]).astype(jnp.bfloat16)
    rows_part = hidden
    result = mid_stream + lax.psum_scatter(
        jnp.einsum("tsf,fd->tsd", rows_part, w_down, preferred_element_type=jnp.float32).astype(
            jnp.bfloat16
        ),
        "mp",
        scatter_dimension=0,
        tiled=True,
    ).astype(jnp.float32)
    part_up = lax.all_gather(upstream, "mp", axis=0, tiled=True)
    part_in = lax.all_gather(ffn_normed, "mp", axis=0, tiled=True)
    d_rows = swiglu_back(
        gate_up, jnp.einsum("tsd,fd->tsf", part_up, w_down, preferred_element_type=jnp.float32)
    )
    d_down = jnp.einsum("tsf,tsd->fd", hidden, part_up, preferred_element_type=jnp.float32)
    d_both = jnp.einsum("tsd,tskf->dkf", part_in, d_rows, preferred_element_type=jnp.float32)
    grad_down = d_down
    grad_both = d_both
    rows_part = d_rows
    d_ffn_in = lax.psum_scatter(
        jnp.einsum("tskf,dkf->tsd", rows_part, w_both, preferred_element_type=jnp.float32),
        "mp",
        scatter_dimension=0,
        tiled=True,
    )
    d_mid_norm, grad_ffn_gain = ffn_pull(d_ffn_in)
    d_mid = upstream.astype(jnp.float32) + d_mid_norm
    d_rms = jnp.sum(d_mid * mix_out, axis=-1)
    d_mix = (inv_rms[..., None] * d_mid).astype(jnp.bfloat16)
    d_square = (-0.5 * inv_rms * inv_rms * inv_rms * d_rms).astype(jnp.bfloat16)
    part_mix = lax.all_gather(d_mix, "mp", axis=0, tiled=True)
    part_square = lax.all_gather(d_square, "mp", axis=0, tiled=True)
    d_part = jnp.einsum("tsd,kcd->skct", part_mix, w_output, preferred_element_type=jnp.float32)
    d_gated = d_part
    d_squares = jnp.transpose(part_square.astype(jnp.float32))
    d_out = jnp.einsum("skct,tsd->kcd", gated, part_mix, preferred_element_type=jnp.float32)
    d_gated, d_squares, grad_output = (d_gated, d_squares, d_out)
    d_states_gate, d_outgate, grad_out_gain = gated_pull(d_gated)
    d_states = d_states_gate + d_squares[:, None, None, :] * states / chan_all
    d_in_pre, d_forget_pre, d_lower, grad_phase = states_pull(d_states)
    (grad_lower,) = bound_pull(d_lower)
    d_project = jnp.concatenate([d_in_pre, d_outgate, d_forget_pre[:, None]], axis=1).astype(
        jnp.bfloat16
    )
    rows_part = d_project
    d_normed = lax.psum_scatter(
        jnp.einsum("skct,dkc->tsd", rows_part, w_mix, preferred_element_type=jnp.float32).astype(
            jnp.bfloat16
        ),
        "mp",
        scatter_dimension=0,
        tiled=True,
    ).astype(jnp.float32)
    rows_part = d_project
    grad_mix = jnp.einsum(
        "tsd,skct->dkc",
        lax.all_gather(normed, "mp", axis=0, tiled=True),
        rows_part,
        preferred_element_type=jnp.float32,
    )
    d_tok_norm, grad_mix_gain = first_pull(d_normed)
    grad_tokens = (d_mid + d_tok_norm).astype(jnp.bfloat16)
    grad_mix, grad_output, grad_both, grad_down, grad_out_gain, grad_phase, grad_lower = lax.psum(
        (grad_mix, grad_output, grad_both, grad_down, grad_out_gain, grad_phase, grad_lower), "dp"
    )
    grad_mix_gain, grad_ffn_gain = lax.psum((grad_mix_gain, grad_ffn_gain), ("dp", "mp"))
    return (
        result.astype(jnp.bfloat16),
        grad_tokens,
        grad_mix_gain,
        grad_mix[:, 0:2],
        grad_mix[:, 4],
        grad_mix[:, 2:4],
        grad_phase,
        grad_lower,
        grad_out_gain,
        grad_output,
        grad_ffn_gain,
        grad_both[:, 0],
        grad_both[:, 1],
        grad_down,
    )


def solution(mesh):
    in_specs = (
        P("mp", "dp", None),
        P("mp", "dp", None),
        P("dp"),
        P(),
        P(),
        P(None, None, "mp"),
        P(None, "mp"),
        P(None, None, "mp"),
        P("mp"),
        P(None, "mp"),
        P(None, "mp"),
        P(None, "mp", None),
        P(),
        P(None, "mp"),
        P(None, "mp"),
        P("mp", None),
    )
    out_specs = (
        P("mp", "dp", None),
        P("mp", "dp", None),
        P(),
        P(None, None, "mp"),
        P(None, "mp"),
        P(None, None, "mp"),
        P("mp"),
        P(None, "mp"),
        P(None, "mp"),
        P(None, "mp", None),
        P(),
        P(None, "mp"),
        P(None, "mp"),
        P("mp", None),
    )
    return jax.shard_map(shards, mesh=mesh, in_specs=in_specs, out_specs=out_specs, check_vma=False)
```

profile of v0, /device:TPU:0, one launch (start us, length us, event | category | flops | bytes accessed | tf_op | source)
XLA Modules:
  0.0 1634.9 jit_solution(4589234935897195705)
XLA Ops:
  18.3 70.1 %all-gather.5.cloned.1.call-done = bf16[4096,2,768]{2,0,1:T(8,128)(2,1)} async-done(((bf16[512,2,768]{2,0,1:T(8,128)(2,1)}), bf16[4096,2,768]{2,0,1:T(8,128)(2,1)}) %all-gather.5.cloned.1.call-update) | async-done | bytes 12582928 | tf_op jit(solution)/shard_map/all_gather | solution.py:139
  116.1 9.3 multiply_bitcast_fusion
  148.5 34.8 %while.62 = (s32[]{:T(128)}, f32[2,48,256]{2,1,0:T(8,128)}, f32[2,48,256]{2,1,0:T(8,128)}, f32[2,48,256]{2,1,0:T(8,128)}, f32[2,48,256]{2,1,0:T(8,128)S(1)}, /*i...) while((s32[]{:T(128)}, f32[2,48,256]{2,1,0:T(8,128)}, ...), condition=%wide.region_5.6_spmd.clone, body=%wide.region_4.5_spmd.clone.sunk | while | flops 442371 | bytes 1966275 | solution.py:52
  458.4 10.7 convolution_bitcast_fusion
  469.2 30.5 %reduce-scatter.16.cloned.1.call-done = f32[512,2]{1,0:T(8,128)} async-done(((f32[4096,2]{1,0:T(8,128)}), f32[512,2]{1,0:T(8,128)}) %reduce-scatter.16.cloned.1.call-update) | async-done | bytes 4112
  500.8 159.9 %reduce-scatter.8.cloned.1.call-done = f32[512,2,768]{2,0,1:T(8,128)} async-done(((f32[4096,2,768]{2,0,1:T(8,128)}), f32[512,2,768]{2,0,1:T(8,128)}) %reduce-scatter.8.cloned.1.call-update) | async-done | bytes 3145744 | tf_op jit(solution)/shard_map/reduce_scatter | solution.py:163
  668.1 69.4 %all-gather.7.cloned.1.call-done = bf16[4096,2,768]{2,0,1:T(8,128)(2,1)} async-done(((bf16[512,2,768]{2,0,1:T(8,128)(2,1)}), bf16[4096,2,768]{2,0,1:T(8,128)(2,1)}) %all-gather.7.cloned.1.call-update) | async-done | bytes 12582928 | tf_op jit(solution)/shard_map/all_gather | solution.py:175
  737.5 11.3 fusion.15
  748.8 62.8 %all-gather.9.cloned.1.call-done = bf16[4096,2,768]{2,0,1:T(8,128)(2,1)} async-done(((bf16[512,2,768]{2,0,1:T(8,128)(2,1)}), bf16[4096,2,768]{2,0,1:T(8,128)(2,1)}) %all-gather.9.cloned.1.call-update) | async-done | bytes 12582928 | tf_op jit(solution)/shard_map/all_gather | solution.py:189
  811.6 15.8 fusion.59
  830.0 11.8 convolution_bitcast_fusion.1
  842.2 12.0 convolution_convert_fusion
  854.3 144.6 %reduce-scatter.12.cloned.1.call-done = f32[512,2,768]{2,0,1:T(8,128)} async-done(((f32[4096,2,768]{2,0,1:T(8,128)}), f32[512,2,768]{2,0,1:T(8,128)}) %reduce-scatter.12.cloned.1.call-update) | async-done | bytes 3145744 | tf_op jit(solution)/shard_map/reduce_scatter | solution.py:199
  1002.2 93.0 %reduce-scatter.10.cloned.1.call-done = bf16[512,2,768]{2,0,1:T(8,128)(2,1)} async-done(((bf16[4096,2,768]{2,0,1:T(8,128)(2,1)}), bf16[512,2,768]{2,0,1:T(8,128)(2,1)}) %reduce-scatter.10.cloned.1.call-update) | async-done | bytes 1572880 | tf_op jit(solution)/shard_map/reduce_scatter | solution.py:181
  1102.9 9.9 convolution_bitcast_fusion.2
  1112.9 10.8 fusion.65
  1132.7 40.0 %all-gather.11.cloned.1.call-done = bf16[4096,2,768]{2,0,1:T(8,128)(2,1)} async-done(((bf16[512,2,768]{2,0,1:T(8,128)(2,1)}), bf16[4096,2,768]{2,0,1:T(8,128)(2,1)}) %all-gather.11.cloned.1.call-update) | async-done | bytes 12582928 | tf_op jit(solution)/shard_map/all_gather | solution.py:210
  1218.7 101.8 %while.61 = (s32[]{:T(128)}, f32[2,48,256]{2,1,0:T(8,128)}, f32[2,48,256]{2,1,0:T(8,128)S(1)}, f32[2,48,256]{2,1,0:T(8,128)}, f32[2,48,256]{2,1,0:T(8,128)}, /*i...) while((s32[]{:T(128)}, f32[2,48,256]{2,1,0:T(8,128)}, ...), condition=%wide.region_19.20_spmd, body=%wide.region_18.19_spmd.sunk | while | flops 835587 | bytes 3932377 | solution.py:52
  1371.8 9.8 fusion.14
  1385.7 9.5 fusion.118
  1400.2 13.8 all-reduce.157
  1414.0 69.5 %all-reduce.161.cloned.1.call-done = (f32[768,5,48]{0,2,1:T(8,128)}, f32[2,48,768]{2,1,0:T(8,128)}, f32[768,2,192]{0,2,1:T(8,128)}, f32[192,768]{1,0:T(8,128)}) async-done(((f32[768,5,48]{0,2,1:T(8,128)}, f32[2,48,768]{2,1,0:T(8,128)}, f32[768,2,192]{0,2,1:T(8,128)}, f32[192,768]{1,0:T(8,128)}), (f32[768,5,48]{0,2,1:T(8,128)}, f32[2,48,768]{2,1,0:T(8,128)}, f32[768,2,192]{0,2,1:T(8,128)}, ...) | async-done | bytes 2801680 | tf_op jit(solution)/shard_map/psum | solution.py:242
  1489.3 88.9 %reduce-scatter.14.cloned.1.call-done = bf16[512,2,768]{2,0,1:T(8,128)(2,1)} async-done(((bf16[4096,2,768]{2,0,1:T(8,128)(2,1)}), bf16[512,2,768]{2,0,1:T(8,128)(2,1)}) %reduce-scatter.14.cloned.1.call-update) | async-done | bytes 1572880 | tf_op jit(solution)/shard_map/reduce_scatter | solution.py:225
  1586.7 39.4 %all-reduce.156 = (f32[768]{0:T(1024)}, f32[768]{0:T(1024)}) all-reduce(f32[768]{0:T(1024)S(1)} %get-tuple-element.823, f32[768]{0:T(1024)S(1)} %copy-done.121), channel_id=1, replica_groups=mesh['dp'=4,'mp'=8] {'dp','mp'}, use_global_device_ids=true, to_apply=%region_23.24 | all-reduce | flops 1536 | bytes 12288 | tf_op jit(solution)/shard_map/psum | solution.py:245
  (904 shorter events, 622.9 us)
Async XLA Ops:
  7.2 804.4 %copy-start = (bf16[192,768]{1,0:T(8,128)(2,1)S(1)}, bf16[192,768]{1,0:T(8,128)(2,1)}, u32[]{:S(2)}) copy-start(bf16[192,768]{1,0:T(8,128)(2,1)} %param.35) | copy-start | bytes 884740
  7.3 81.2 %all-gather.5.cloned.1.call-start = ((), (), s32[]{:S(2)}) async-start(), calls=%async_computation.5 | async-start | bytes 14155776 | tf_op jit(solution)/shard_map/all_gather | solution.py:139
  13.5 486.3 %reduce-scatter.16.cloned.1.call-start = ((), (), s32[]{:S(2)}) async-start(), calls=%async_computation.13 | async-start | bytes 2359296
  14.4 101.7 %copy-start.134 = (f32[48]{0:T(128)}, f32[48]{0:T(128)S(1)}, u32[]{:S(2)}) copy-start(f32[48]{0:T(128)S(1)} %multiply_reduce_fusion.11) | copy-start | bytes 580
  14.8 101.2 %copy-start.140 = (f32[48]{0:T(128)}, f32[48]{0:T(128)S(1)}, u32[]{:S(2)}) copy-start(f32[48]{0:T(128)S(1)} %broadcast_subtract_fusion) | copy-start | bytes 580
  15.0 101.0 %copy-start.130 = (f32[48]{0:T(128)}, f32[48]{0:T(128)S(1)}, u32[]{:S(2)}) copy-start(f32[48]{0:T(128)S(1)} %get-tuple-element.1221) | copy-start | bytes 580
  15.0 101.0 %copy-start.132 = (f32[48]{0:T(128)}, f32[48]{0:T(128)S(1)}, u32[]{:S(2)}) copy-start(f32[48]{0:T(128)S(1)} %get-tuple-element.1222) | copy-start | bytes 580
  183.3 250.0 %copy-start.13 = (f32[16,2,48,256]{3,2,1,0:T(8,128)}, f32[16,2,48,256]{3,2,1,0:T(8,128)S(1)}, u32[]{:S(2)}) copy-start(f32[16,2,48,256]{3,2,1,0:T(8,128)S(1)} %get-tuple-element.489) | copy-start | bytes 4718596
  183.3 250.0 %copy-start.15 = (f32[16,2,48,256]{3,2,1,0:T(8,128)}, f32[16,2,48,256]{3,2,1,0:T(8,128)S(1)}, u32[]{:S(2)}) copy-start(f32[16,2,48,256]{3,2,1,0:T(8,128)S(1)} %get-tuple-element.484) | copy-start | bytes 4718596
  215.9 169.1 %copy-start.40 = (f32[2,48,64]{1,2,0:T(8,128)}, f32[2,48,64]{1,2,0:T(8,128)S(1)}, u32[]{:S(2)}) copy-start(f32[2,48,64]{1,2,0:T(8,128)S(1)} %slice.543) | copy-start | bytes 73732
  239.3 160.8 %copy-start.59 = (f32[2,48,32]{1,2,0:T(8,128)}, f32[2,48,32]{1,2,0:T(8,128)S(1)}, u32[]{:S(2)}) copy-start(f32[2,48,32]{1,2,0:T(8,128)S(1)} %slice.555) | copy-start | bytes 36868
  258.5 150.9 %copy-start.73 = (f32[2,48,16]{1,2,0:T(8,128)}, f32[2,48,16]{1,2,0:T(8,128)S(1)}, u32[]{:S(2)}) copy-start(f32[2,48,16]{1,2,0:T(8,128)S(1)} %slice.563) | copy-start | bytes 18436
  458.4 202.3 %reduce-scatter.8.cloned.1.call-start = ((), (), s32[]{:S(2)}) async-start(), calls=%async_computation.6 | async-start | bytes 28311552 | tf_op jit(solution)/shard_map/reduce_scatter | solution.py:163
  469.2 268.4 %all-gather.7.cloned.1.call-start = ((), (), s32[]{:S(2)}) async-start(), calls=%async_computation.7 | async-start | bytes 14155776 | tf_op jit(solution)/shard_map/all_gather | solution.py:175
  500.8 162.9 %copy-start.111 = (f32[768]{0:T(1024)S(1)}, f32[768]{0:T(1024)}, u32[]{:S(2)}) copy-start(f32[768]{0:T(1024)} %param.32) | copy-start | bytes 9220
  665.2 146.4 %all-gather.9.cloned.1.call-start = ((), (), s32[]{:S(2)}) async-start(), calls=%async_computation.9 | async-start | bytes 14155776 | tf_op jit(solution)/shard_map/all_gather | solution.py:189
  668.1 330.8 %reduce-scatter.12.cloned.1.call-start = ((), (), s32[]{:S(2)}) async-start(), calls=%async_computation.10 | async-start | bytes 28311552 | tf_op jit(solution)/shard_map/reduce_scatter | solution.py:199
  841.9 253.4 %reduce-scatter.10.cloned.1.call-start = ((), (), s32[]{:S(2)}) async-start(), calls=%async_computation.8 | async-start | bytes 14155776 | tf_op jit(solution)/shard_map/reduce_scatter | solution.py:181
  854.2 318.5 %all-gather.11.cloned.1.call-start = ((), (), s32[]{:S(2)}) async-start(), calls=%async_computation.11 | async-start | bytes 14155776 | tf_op jit(solution)/shard_map/all_gather | solution.py:210
  1100.4 383.0 %all-reduce.161.cloned.1.call-start = ((), (), s32[]{:S(2)}) async-start(), calls=%async_computation.14 | async-start | bytes 5603328 | tf_op jit(solution)/shard_map/psum | solution.py:242
  1371.4 206.8 %reduce-scatter.14.cloned.1.call-start = ((), (), s32[]{:S(2)}) async-start(), calls=%async_computation.12 | async-start | bytes 14155776 | tf_op jit(solution)/shard_map/reduce_scatter | solution.py:225
  1399.9 178.3 %copy-start.4 = (bf16[512,2,768]{2,1,0:T(2,128)(2,1)S(1)}, bf16[512,2,768]{2,1,0:T(2,128)(2,1)}, u32[]{:S(2)}) copy-start(bf16[512,2,768]{2,1,0:T(2,128)(2,1)} %param.20) | copy-start | bytes 4718596
  1399.9 178.3 %copy-start.104 = (f32[512,2]{0,1:T(2,128)S(1)}, f32[512,2]{0,1:T(2,128)}, u32[]{:S(2)}) copy-start(f32[512,2]{0,1:T(2,128)} %copy-done.103) | copy-start | bytes 12292
  1399.9 178.3 %copy-start.112 = (f32[768]{0:T(1024)S(1)}, f32[768]{0:T(1024)}, u32[]{:S(2)}) copy-start(f32[768]{0:T(1024)} %param.24) | copy-start | bytes 9220
  (153 other events, 1645.6 us)
Sparse Core Ops, SparseCore 0:
  13.6 74.8 all-gather.4
  458.5 41.2 reduce-scatter.15
  503.8 156.8 reduce-scatter.7
  665.4 72.1 all-gather.6
  739.4 72.1 all-gather.8
  842.0 156.8 reduce-scatter.11
  1002.8 92.4 reduce-scatter.9
  1100.6 72.1 all-gather.10
  1371.6 111.8 all-reduce.160
  1486.8 91.3 reduce-scatter.13
where the time goes:
time: 1650 us; the launch traced here: 1630 us
  waiting for transfers between devices  829 us (50%)
  local copies, waits for them, and re-layouts  327 us (20%)
  other arithmetic  277 us (17%)
  matrix products  120 us (7%)
  blocking collectives  61.7 us (4%)
  between operations  18.5 us (1%)
    reduce_scatter x1, waiting for transfers between devices, shards(): lax.psum_scatter(jnp.einsum('skct,kcd->tsd', rows_part, w_output, preferr...  160 us
    reduce_scatter x1, waiting for transfers between devices, shards(): lax.psum_scatter(jnp.einsum('tskf,dkf->tsd', rows_part, w_both, preferred...  145 us
    slice x120, local copies, waits for them, and re-layouts, blocked_scan(): inclusive = lax.associative_scan(combine, totals, axis=2)  127 us
    dynamic_update_slice x64, other arithmetic, blocked_scan(): totals, inner = lax.scan(advance, start, blocked)  109 us
    reduce_scatter x1, waiting for transfers between devices, shards(): lax.psum_scatter(jnp.einsum('tsf,fd->tsd', rows_part, w_down, preferred_e...  93 us
    reduce_scatter x1, waiting for transfers between devices, shards(): lax.psum_scatter(jnp.einsum('skct,dkc->tsd', rows_part, w_mix, preferred_...  88.9 us
    all_gather x1, waiting for transfers between devices, shards(): lax.all_gather(normed, 'mp', axis=0, tiled=True)  70.1 us
    psum x1, waiting for transfers between devices, shards(): lax.psum((grad_mix, grad_output, grad_both, grad_down, grad_out_gain, gra...  69.5 us
  transfers between devices with their start and end apart: 10, of which 10 were waited for; matrix products, arithmetic and copies ran while one was open for 6% of the time, Pallas kernels for 0%

commit v1 on v0

v1 whole, which is shorter than its diff:
```python
import functools

import jax
import jax.numpy as jnp
from jax import lax
from jax.experimental import pallas as pl
from jax.experimental.pallas import tpu as pltpu
from jax.sharding import PartitionSpec as P

EPSILON = 1e-06
CHUNKS = 8
VMEM_BYTES = 48 * 1024 * 1024
F32 = jnp.float32
BF16 = jnp.bfloat16


def kernel_call(body, grid, in_specs, out_specs, out_shape, scratch=()):
    return pl.pallas_call(
        body,
        grid=grid,
        in_specs=in_specs,
        out_specs=out_specs,
        out_shape=out_shape,
        scratch_shapes=scratch,
        compiler_params=pltpu.CompilerParams(vmem_limit_bytes=VMEM_BYTES),
    )


def whole(shape):
    zeros = (0,) * len(shape)
    return pl.BlockSpec(shape, lambda *_: zeros)


def per_group(shape):
    zeros = (0,) * (len(shape) - 1)
    return pl.BlockSpec(shape, lambda g: (g,) + zeros)


SMEM_SPEC = pl.BlockSpec(memory_space=pltpu.SMEM)


def turn(cos, sin, re, im):
    return cos * re - sin * im, sin * re + cos * im


def back_turn(cos, sin, re, im):
    return cos * re + sin * im, cos * im - sin * re


def scan_local_body(steps, chans, pre, bound, angles, local, prods, decays, prefix, totals):
    low = bound[0:1, :]
    cos_one, sin_one = angles[0:1, :], angles[1:2, :]
    cos_chunk, sin_chunk = angles[2:3, :], angles[3:4, :]

    def step(j, carry):
        state_re, state_im, prod = carry
        rows = pl.ds(pl.multiple_of(j * CHUNKS, CHUNKS), CHUNKS)
        in_re = pre[rows, 0:chans]
        in_im = pre[rows, chans : 2 * chans]
        decay = low + (1.0 - low) * jax.nn.sigmoid(pre[rows, 2 * chans : 3 * chans])
        turned_re, turned_im = turn(cos_one, sin_one, state_re, state_im)
        state_re = decay * turned_re + (1.0 - decay) * (in_re * jax.nn.sigmoid(in_re))
        state_im = decay * turned_im + (1.0 - decay) * (in_im * jax.nn.sigmoid(in_im))
        prod = prod * decay
        local[rows, 0:chans] = state_re
        local[rows, chans : 2 * chans] = state_im
        prods[rows, :] = prod
        decays[rows, :] = decay
        return state_re, state_im, prod

    zeros = jnp.zeros((CHUNKS, chans), F32)
    end_re, end_im, prod = lax.fori_loop(0, steps, step, (zeros, zeros, zeros + 1.0), unroll=4)
    run, run_re, run_im = zeros[0:1] + 1.0, zeros[0:1], zeros[0:1]
    for s in range(CHUNKS):
        prefix[0, 0, s : s + 1, :] = run
        prefix[0, 1, s : s + 1, :] = run_re
        prefix[0, 2, s : s + 1, :] = run_im
        turned_re, turned_im = turn(cos_chunk, sin_chunk, run_re, run_im)
        run_re = prod[s : s + 1] * turned_re + end_re[s : s + 1]
        run_im = prod[s : s + 1] * turned_im + end_im[s : s + 1]
        run = run * prod[s : s + 1]
    totals[0] = zeros
    totals[0, 0:1, :] = run
    totals[0, 1:2, :] = run_re
    totals[0, 2:3, :] = run_im


def scan_local(pre, bound, angles, groups, chans):
    rows = pre.shape[0]
    per = rows // groups
    return kernel_call(
        functools.partial(scan_local_body, per // CHUNKS, chans),
        (groups,),
        [
            pl.BlockSpec((per, 3 * chans), lambda g: (g, 0)),
            whole((1, chans)),
            whole(angles.shape),
        ],
        [
            per_group((per, 2 * chans)),
            per_group((per, chans)),
            per_group((per, chans)),
            per_group((1, 3, CHUNKS, chans)),
            per_group((1, CHUNKS, chans)),
        ],
        [
            jax.ShapeDtypeStruct((rows, 2 * chans), F32),
            jax.ShapeDtypeStruct((rows, chans), F32),
            jax.ShapeDtypeStruct((rows, chans), F32),
            jax.ShapeDtypeStruct((groups, 3, CHUNKS, chans), F32),
            jax.ShapeDtypeStruct((groups, CHUNKS, chans), F32),
        ],
    )(pre, bound, angles)


def scan_finish_body(
    steps, chans, blocks, me, keep, gathered, local, prods, prefix, angles, table, states, entering
):
    g = pl.program_id(0)
    cos_dev, sin_dev = angles[4:5, :], angles[5:6, :]
    state_re = jnp.zeros((1, chans), F32)
    state_im = jnp.zeros((1, chans), F32)
    for d in range(blocks):
        kept = keep[g, d]
        turned_re, turned_im = turn(cos_dev, sin_dev, kept * state_re, kept * state_im)
        decay = gathered[d, 0, 0:1, :]
        earlier = d < me[0]
        state_re = jnp.where(earlier, decay * turned_re + gathered[d, 0, 1:2, :], state_re)
        state_im = jnp.where(earlier, decay * turned_im + gathered[d, 0, 2:3, :], state_im)
    kept = keep[g, me[0]]
    state_re, state_im = kept * state_re, kept * state_im
    cos_chunk, sin_chunk = angles[2:3, :], angles[3:4, :]
    for s in range(CHUNKS):
        run = prefix[0, 0, s : s + 1, :]
        entering[0, 0, s : s + 1, :] = run * state_re + prefix[0, 1, s : s + 1, :]
        entering[0, 1, s : s + 1, :] = run * state_im + prefix[0, 2, s : s + 1, :]
        state_re, state_im = turn(cos_chunk, sin_chunk, state_re, state_im)
    enter_re, enter_im = entering[0, 0], entering[0, 1]

    def step(j, carry):
        rows = pl.ds(pl.multiple_of(j * CHUNKS, CHUNKS), CHUNKS)
        prod = prods[rows, :]
        turned_re, turned_im = turn(
            table[pl.ds(j, 1), 0:chans], table[pl.ds(j, 1), chans : 2 * chans], enter_re, enter_im
        )
        states[rows, 0:chans] = local[rows, 0:chans] + prod * turned_re
        states[rows, chans : 2 * chans] = local[rows, chans : 2 * chans] + prod * turned_im
        return carry

    lax.fori_loop(0, steps, step, 0, unroll=4)


def scan_finish(me, keep, gathered, local, prods, prefix, angles, table, groups, chans):
    rows = prods.shape[0]
    per = rows // groups
    blocks = gathered.shape[0]
    return kernel_call(
        functools.partial(scan_finish_body, per // CHUNKS, chans, blocks),
        (groups,),
        [
            SMEM_SPEC,
            SMEM_SPEC,
            pl.BlockSpec((blocks, 1, CHUNKS, chans), lambda g: (0, g, 0, 0)),
            per_group((per, 2 * chans)),
            per_group((per, chans)),
            per_group((1, 3, CHUNKS, chans)),
            whole(angles.shape),
            whole(table.shape),
        ],
        [per_group((per, 2 * chans)), per_group((1, 2, CHUNKS, chans))],
        [
            jax.ShapeDtypeStruct((rows, 2 * chans), F32),
            jax.ShapeDtypeStruct((groups, 2, CHUNKS, chans), F32),
        ],
    )(me, keep, gathered, local, prods, prefix, angles, table)


def adjoint_local_body(steps, chans, d_states, decays, angles, local, prods, suffix, totals):
    cos_one, sin_one = angles[0:1, :], angles[1:2, :]
    cos_chunk, sin_chunk = angles[2:3, :], angles[3:4, :]

    def step(i, carry):
        flow_re, flow_im, prod = carry
        j = steps - 1 - i
        rows = pl.ds(pl.multiple_of(j * CHUNKS, CHUNKS), CHUNKS)
        grad_re = d_states[rows, 0:chans] + flow_re
        grad_im = d_states[rows, chans : 2 * chans] + flow_im
        local[rows, 0:chans] = grad_re
        local[rows, chans : 2 * chans] = grad_im
        prods[rows, :] = prod
        decay = decays[rows, :]
        turned_re, turned_im = back_turn(cos_one, sin_one, grad_re, grad_im)
        return decay * turned_re, decay * turned_im, prod * decay

    zeros = jnp.zeros((CHUNKS, chans), F32)
    end_re, end_im, prod = lax.fori_loop(0, steps, step, (zeros, zeros, zeros + 1.0), unroll=4)
    run, run_re, run_im = zeros[0:1] + 1.0, zeros[0:1], zeros[0:1]
    for s in reversed(range(CHUNKS)):
        suffix[0, 0, s : s + 1, :] = run
        suffix[0, 1, s : s + 1, :] = run_re
        suffix[0, 2, s : s + 1, :] = run_im
        turned_re, turned_im = back_turn(cos_chunk, sin_chunk, run_re, run_im)
        run_re = prod[s : s + 1] * turned_re + end_re[s : s + 1]
        run_im = prod[s : s + 1] * turned_im + end_im[s : s + 1]
        run = run * prod[s : s + 1]
    totals[0] = zeros
    totals[0, 0:1, :] = run
    totals[0, 1:2, :] = run_re
    totals[0, 2:3, :] = run_im


def adjoint_local(d_states, decays, angles, groups, chans):
    rows = decays.shape[0]
    per = rows // groups
    return kernel_call(
        functools.partial(adjoint_local_body, per // CHUNKS, chans),
        (groups,),
        [per_group((per, 2 * chans)), per_group((per, chans)), whole(angles.shape)],
        [
            per_group((per, 2 * chans)),
            per_group((per, chans)),
            per_group((1, 3, CHUNKS, chans)),
            per_group((1, CHUNKS, chans)),
        ],
        [
            jax.ShapeDtypeStruct((rows, 2 * chans), F32),
            jax.ShapeDtypeStruct((rows, chans), F32),
            jax.ShapeDtypeStruct((groups, 3, CHUNKS, chans), F32),
            jax.ShapeDtypeStruct((groups, CHUNKS, chans), F32),
        ],
    )(d_states, decays, angles)


def silu_slope(values, sigma):
    return sigma * (1.0 + values * (1.0 - sigma))


def adjoint_finish_body(
    steps,
    chans,
    blocks,
    me,
    keep,
    gathered,
    local,
    prods,
    suffix,
    pre,
    states,
    entering,
    bound,
    angles,
    table,
    d_pre,
    sums,
    leaving,
):
    g = pl.program_id(0)
    low = bound[0:1, :]
    cos_one, sin_one = angles[0:1, :], angles[1:2, :]
    cos_chunk, sin_chunk = angles[2:3, :], angles[3:4, :]
    cos_dev, sin_dev = angles[4:5, :], angles[5:6, :]
    flow_re = jnp.zeros((1, chans), F32)
    flow_im = jnp.zeros((1, chans), F32)
    for d in reversed(range(blocks)):
        kept = keep[g, d]
        turned_re, turned_im = back_turn(cos_dev, sin_dev, flow_re, flow_im)
        decay = gathered[d, 0, 0:1, :]
        later = d > me[0]
        flow_re = jnp.where(
            later, kept * (decay * turned_re + gathered[d, 0, 1:2, :]), flow_re
        )
        flow_im = jnp.where(
            later, kept * (decay * turned_im + gathered[d, 0, 2:3, :]), flow_im
        )
    for s in reversed(range(CHUNKS)):
        run = suffix[0, 0, s : s + 1, :]
        leaving[0, s : s + 1, :] = run * flow_re + suffix[0, 1, s : s + 1, :]
        leaving[1, s : s + 1, :] = run * flow_im + suffix[0, 2, s : s + 1, :]
        flow_re, flow_im = back_turn(cos_chunk, sin_chunk, flow_re, flow_im)
    leave_re, leave_im = leaving[0], leaving[1]

    def one(j, carry):
        last_re, last_im, phase_sum, bound_sum = carry
        rows = pl.ds(pl.multiple_of(j * CHUNKS, CHUNKS), CHUNKS)
        left = pl.ds(steps - 1 - j, 1)
        prod = prods[rows, :]
        turned_re, turned_im = back_turn(
            table[left, 0:chans], table[left, chans : 2 * chans], leave_re, leave_im
        )
        grad_re = local[rows, 0:chans] + prod * turned_re
        grad_im = local[rows, chans : 2 * chans] + prod * turned_im
        in_re = pre[rows, 0:chans]
        in_im = pre[rows, chans : 2 * chans]
        sigma_re = jax.nn.sigmoid(in_re)
        sigma_im = jax.nn.sigmoid(in_im)
        sigma = jax.nn.sigmoid(pre[rows, 2 * chans : 3 * chans])
        decay = low + (1.0 - low) * sigma
        cross_re = grad_re * last_re + grad_im * last_im
        cross_im = grad_im * last_re - grad_re * last_im
        along, across = back_turn(cos_one, sin_one, cross_re, cross_im)
        d_decay = along - (grad_re * in_re * sigma_re + grad_im * in_im * sigma_im)
        rest = 1.0 - decay
        d_re = grad_re * rest * silu_slope(in_re, sigma_re)
        d_im = grad_im * rest * silu_slope(in_im, sigma_im)
        d_low = d_decay * (1.0 - sigma)
        d_forget = d_low * (1.0 - low) * sigma
        carry = (
            states[rows, 0:chans],
            states[rows, chans : 2 * chans],
            phase_sum + decay * across,
            bound_sum + d_low,
        )
        return carry, (d_re, d_im, d_forget)

    def pair(i, carry):
        carry, first = one(2 * i, carry)
        carry, second = one(2 * i + 1, carry)
        rows = pl.ds(pl.multiple_of(i * 2 * CHUNKS, 2 * CHUNKS), 2 * CHUNKS)
        for k in range(3):
            d_pre[rows, k * chans : (k + 1) * chans] = jnp.concatenate(
                [first[k], second[k]], axis=0
            ).astype(BF16)
        return carry

    zeros = jnp.zeros((CHUNKS, chans), F32)
    _, _, phase_sum, bound_sum = lax.fori_loop(
        0, steps // 2, pair, (entering[0, 0], entering[0, 1], zeros, zeros), unroll=2
    )
    sums[0, 0] = phase_sum
    sums[0, 1] = bound_sum


def adjoint_finish(
    me, keep, gathered, local, prods, suffix, pre, states, entering, bound, angles, table, groups, chans
):
    rows = prods.shape[0]
    per = rows // groups
    blocks = gathered.shape[0]
    return kernel_call(
        functools.partial(adjoint_finish_body, per // CHUNKS, chans, blocks),
        (groups,),
        [
            SMEM_SPEC,
            SMEM_SPEC,
            pl.BlockSpec((blocks, 1, CHUNKS, chans), lambda g: (0, g, 0, 0)),
            per_group((per, 2 * chans)),
            per_group((per, chans)),
            per_group((1, 3, CHUNKS, chans)),
            pl.BlockSpec((per, 3 * chans), lambda g: (g, 0)),
            per_group((per, 2 * chans)),
            per_group((1, 2, CHUNKS, chans)),
            whole((1, chans)),
            whole(angles.shape),
            whole(table.shape),
        ],
        [per_group((per, 3 * chans)), per_group((1, 2, CHUNKS, chans))],
        [
            jax.ShapeDtypeStruct((rows, 3 * chans), BF16),
            jax.ShapeDtypeStruct((groups, 2, CHUNKS, chans), F32),
        ],
        [pltpu.VMEM((2, CHUNKS, chans), F32)],
    )(me, keep, gathered, local, prods, suffix, pre, states, entering, bound, angles, table)


def rms_rows(values):
    return lax.rsqrt(jnp.mean(values * values, axis=-1, keepdims=True) + EPSILON)


def rms_pull(values, inv, gain, d_out):
    scaled = d_out * gain
    dot = jnp.mean(scaled * values, axis=-1, keepdims=True)
    return inv * scaled - values * (inv * inv * inv * dot)


def nt(left, right):
    return lax.dot_general(left, right, (((1,), (1,)), ((), ())), preferred_element_type=F32)


def nn(left, right):
    return lax.dot_general(left, right, (((1,), (0,)), ((), ())), preferred_element_type=F32)


def tn(left, right):
    return lax.dot_general(left, right, (((0,), (0,)), ((), ())), preferred_element_type=F32)


def shards(
    tokens,
    upstream,
    pieces,
    layer_index,
    mix_gain,
    w_input,
    w_forget,
    w_outgate,
    phase_angle,
    lower_logits,
    out_gain,
    w_output,
    ffn_gain,
    w_gate,
    w_up,
    w_down,
):
    rows_dev, groups, width = tokens.shape
    blocks = lax.axis_size("mp")
    me = lax.axis_index("mp")
    seq_len = rows_dev * blocks
    chans_dev = w_input.shape[2]
    chans = chans_dev * blocks
    units_dev = w_gate.shape[1]
    units = units_dev * blocks
    steps = rows_dev // CHUNKS
    rows = rows_dev * groups

    def to_rows(values):
        return jnp.transpose(
            values.reshape(CHUNKS, steps, groups, width), (2, 1, 0, 3)
        ).reshape(rows, width)

    def from_rows(values):
        return jnp.transpose(
            values.reshape(groups, steps, CHUNKS, width), (2, 1, 0, 3)
        ).reshape(rows_dev, groups, width)

    mix_shard = jnp.concatenate(
        [
            jnp.transpose(w_input, (1, 2, 0)),
            jnp.transpose(w_forget)[None],
            jnp.transpose(w_outgate, (1, 2, 0)),
        ],
        axis=0,
    )
    w_mix = jnp.transpose(lax.all_gather(mix_shard, "mp", axis=0), (1, 0, 2, 3)).reshape(
        5 * chans, width
    )
    out_all = jnp.transpose(lax.all_gather(w_output, "mp", axis=0), (1, 0, 2, 3)).reshape(
        2 * chans, width
    )
    gate_all = lax.all_gather(jnp.transpose(w_gate), "mp", axis=0, tiled=True)
    up_all = lax.all_gather(jnp.transpose(w_up), "mp", axis=0, tiled=True)
    down_all = lax.all_gather(w_down, "mp", axis=0, tiled=True)
    layer_mask = (jnp.arange(lower_logits.shape[0], dtype=jnp.int32) < layer_index[0]).astype(F32)
    soft = jax.nn.softmax(lower_logits, axis=0)
    bound_own = jnp.sum(soft * layer_mask[:, None], axis=0)
    small = lax.all_gather(
        jnp.concatenate([bound_own[None], phase_angle[None], out_gain], axis=0), "mp", axis=0
    )
    small = jnp.transpose(small, (1, 0, 2)).reshape(4, chans)
    bound = small[0:1]
    phase = small[1:2]
    gain_row = small[2:4].reshape(1, 2 * chans)
    spans = phase * jnp.array([[1.0], [steps], [rows_dev]], F32)
    angles = jnp.stack([jnp.cos(spans), jnp.sin(spans)], axis=1).reshape(6, chans)
    lags = phase * jnp.arange(steps + 1, dtype=F32)[:, None]
    table = jnp.concatenate([jnp.cos(lags), jnp.sin(lags)], axis=1)
    table_one = table[1:]
    starts = jnp.arange(blocks, dtype=jnp.int32) * rows_dev
    keep = (starts[None, :] % (seq_len // pieces)[:, None] != 0).astype(F32)
    me_one = me[None].astype(jnp.int32)

    tok = to_rows(tokens).astype(F32)
    up_rows = to_rows(upstream)
    mix_row = mix_gain[None]
    inv_tok = rms_rows(tok)
    normed = (tok * inv_tok * mix_row).astype(BF16)
    pre = nt(normed, w_mix)
    local, prods, decays, prefix, totals = scan_local(pre, bound, angles, groups, chans)
    ends = lax.all_gather(totals, "mp", axis=0)
    states, entering = scan_finish(
        me_one, keep, ends, local, prods, prefix, angles, table_one, groups, chans
    )
    mean_square = jnp.mean(states * states, axis=-1, keepdims=True)
    inv_rms = lax.rsqrt(mean_square + EPSILON)
    gate_pre_out = pre[:, 3 * chans :]
    sigma_out = jax.nn.sigmoid(gate_pre_out)
    gated = (states * gain_row * gate_pre_out * sigma_out).astype(BF16)
    mix_out = nn(gated, out_all)
    mid = tok + inv_rms * mix_out
    inv_mid = rms_rows(mid)
    ffn_row = ffn_gain[None]
    ffn_normed = (mid * inv_mid * ffn_row).astype(BF16)

    gate_pre = nt(ffn_normed, gate_all)
    up_pre = nt(ffn_normed, up_all)
    sigma = jax.nn.sigmoid(gate_pre)
    hidden = (gate_pre * sigma * up_pre).astype(BF16)
    result = (mid + nn(hidden, down_all)).astype(BF16)
    d_hidden = nt(up_rows, down_all)
    d_gate = (d_hidden * up_pre * silu_slope(gate_pre, sigma)).astype(BF16)
    d_up = (d_hidden * gate_pre * sigma).astype(BF16)
    grad_down = tn(hidden, up_rows)
    grad_gate = tn(d_gate, ffn_normed)
    grad_up = tn(d_up, ffn_normed)
    d_ffn = nn(d_gate, gate_all) + nn(d_up, up_all)
    grad_ffn = jnp.stack(
        [part.astype(BF16).reshape(blocks, units_dev, width) for part in (grad_gate, grad_up, grad_down)],
        axis=1,
    )
    grad_ffn = lax.psum_scatter(grad_ffn, "mp", scatter_dimension=0, tiled=False)
    grad_ffn = lax.psum(grad_ffn, "dp").astype(F32)

    grad_ffn_gain = jnp.sum(d_ffn * mid * inv_mid, axis=0)
    d_mid = up_rows.astype(F32) + rms_pull(mid, inv_mid, ffn_row, d_ffn)
    d_mix = (inv_rms * d_mid).astype(BF16)
    d_square = -0.5 * inv_rms * inv_rms * inv_rms * jnp.sum(d_mid * mix_out, axis=-1, keepdims=True)
    d_gated = nt(d_mix, out_all)
    grad_out = tn(gated, d_mix).astype(BF16)
    silu_out = gate_pre_out * sigma_out
    d_states = d_gated * gain_row * silu_out + d_square * states / chans
    d_outgate = (d_gated * states * gain_row * silu_slope(gate_pre_out, sigma_out)).astype(BF16)
    grad_out_gain = jnp.sum(d_gated * states * silu_out, axis=0)
    back_local, back_prods, suffix, back_totals = adjoint_local(
        d_states, decays, angles, groups, chans
    )
    back_ends = lax.all_gather(back_totals, "mp", axis=0)
    d_scan, sums = adjoint_finish(
        me_one,
        keep,
        back_ends,
        back_local,
        back_prods,
        suffix,
        pre,
        states,
        entering,
        bound,
        angles,
        table[:-1],
        groups,
        chans,
    )
    d_project = jnp.concatenate([d_scan, d_outgate], axis=1)
    d_normed = nn(d_project, w_mix)
    grad_mix = tn(d_project, normed).astype(BF16)
    grad_tokens = d_mid + rms_pull(tok, inv_tok, mix_row, d_normed)
    grad_mix_gain = jnp.sum(d_normed * tok * inv_tok, axis=0)

    grad_rows = jnp.concatenate(
        [
            grad_mix.reshape(5, blocks, chans_dev, width),
            grad_out.reshape(2, blocks, chans_dev, width),
        ],
        axis=0,
    )
    grad_rows = jnp.transpose(grad_rows, (1, 0, 2, 3))
    grad_rows = lax.psum_scatter(grad_rows, "mp", scatter_dimension=0, tiled=False)
    grad_rows = lax.psum(grad_rows, "dp").astype(F32)
    sums = jnp.sum(sums, axis=(0, 2))
    flat = jnp.concatenate(
        [grad_mix_gain, grad_ffn_gain, grad_out_gain, sums[0], sums[1]], axis=0
    )
    flat = lax.psum(flat, ("dp", "mp"))
    own = me * chans_dev

    def own_part(offset):
        return lax.dynamic_slice(flat, (2 * width + offset * chans + own,), (chans_dev,))

    grad_gain = jnp.stack([own_part(0), own_part(1)], axis=0)
    d_bound = own_part(3)
    grad_lower = soft * (layer_mask[:, None] - bound_own[None]) * d_bound[None]
    return (
        from_rows(result),
        from_rows(grad_tokens.astype(BF16)),
        flat[0:width],
        jnp.transpose(grad_rows[0:2], (2, 0, 1)),
        jnp.transpose(grad_rows[2]),
        jnp.transpose(grad_rows[3:5], (2, 0, 1)),
        own_part(2),
        grad_lower,
        grad_gain,
        grad_rows[5:7],
        flat[width : 2 * width],
        jnp.transpose(grad_ffn[0]),
        jnp.transpose(grad_ffn[1]),
        grad_ffn[2],
    )


def solution(mesh):
    in_specs = (
        P("mp", "dp", None),
        P("mp", "dp", None),
        P("dp"),
        P(),
        P(),
        P(None, None, "mp"),
        P(None, "mp"),
        P(None, None, "mp"),
        P("mp"),
        P(None, "mp"),
        P(None, "mp"),
        P(None, "mp", None),
        P(),
        P(None, "mp"),
        P(None, "mp"),
        P("mp", None),
    )
    out_specs = (
        P("mp", "dp", None),
        P("mp", "dp", None),
        P(),
        P(None, None, "mp"),
        P(None, "mp"),
        P(None, None, "mp"),
        P("mp"),
        P(None, "mp"),
        P(None, "mp"),
        P(None, "mp", None),
        P(),
        P(None, "mp"),
        P(None, "mp"),
        P("mp", None),
    )
    return jax.shard_map(shards, mesh=mesh, in_specs=in_specs, out_specs=out_specs, check_vma=False)
```

time: 1650 us -> 433 us (0.26)
  waiting for transfers between devices: 829 us -> 179 us
  local copies, waits for them, and re-layouts: 327 us -> 26.4 us
  other arithmetic: 277 us -> 36.6 us
  matrix products: 120 us -> 77.9 us
  Pallas kernels: 0 us -> 17.7 us
    reduce_scatter x4 -> x2, waiting for transfers between devices: 486 us -> 97.9 us  [the longest x1 69 us: shards(): lax.psum_scatter(grad_ffn, 'mp', scatter_dimension=0, tiled=False)]
    all_gather x4 -> x5, waiting for transfers between devices: 242 us -> 65.4 us  [the longest x1 27 us: shards(): lax.all_gather(mix_shard, 'mp', axis=0)]
    slice x126 -> x7, local copies, waits for them, and re-layouts: 142 us -> 2.46 us  [the longest x1 1.72 us: shards(): grad_rows[5:7]]
    dynamic_update_slice x64 -> x0, other arithmetic: 109 us -> none  [blocked_scan(): totals, inner = lax.scan(advance, start, blocked)]
    psum x1, waiting for transfers between devices: 69.5 us -> 13.6 us  [shards(): grad_rows = lax.psum(grad_rows, 'dp').astype(F32)]
    pad x118 -> x0, local copies, waits for them, and re-layouts: 46.9 us -> none  [blocked_scan(): inclusive = lax.associative_scan(combine, totals, axis=2)]
    unnamed x353 -> x100, local copies, waits for them, and re-layouts: 49 us -> 4.55 us
    dot_general x12 -> x15, matrix products: 120 us -> 77.9 us  [the longest x5 36.9 us: nt(): lax.dot_general(left, right, (((1,), (1,)), ((), ())), preferred_element_...]
  transfers between devices with their start and end apart: 10 -> 8, of which waited for: 10 -> 6; matrix products, arithmetic and copies ran while one was open for 6% -> 21% of each run, Pallas kernels for 0% -> 2%
where the time goes in v1:
time: 433 us; the launch traced here: 425 us
  waiting for transfers between devices  179 us (41%)
  matrix products  77.9 us (18%)
  blocking collectives  70.6 us (16%)
  other arithmetic  36.6 us (8%)
  local copies, waits for them, and re-layouts  26.4 us (6%)
  Pallas kernels  17.7 us (4%)
  between operations  16 us (4%)
    reduce_scatter x1, waiting for transfers between devices, shards(): lax.psum_scatter(grad_ffn, 'mp', scatter_dimension=0, tiled=False)  69 us
    psum x1, blocking collectives, shards(): flat = lax.psum(flat, ('dp', 'mp'))  41.2 us
    dot_general x5, matrix products, nt(): lax.dot_general(left, right, (((1,), (1,)), ((), ())), preferred_element_...  36.9 us
    reduce_scatter x1, waiting for transfers between devices, shards(): lax.psum_scatter(grad_rows, 'mp', scatter_dimension=0, tiled=False)  28.9 us
    all_gather x1, waiting for transfers between devices, shards(): lax.all_gather(mix_shard, 'mp', axis=0)  27 us
    dot_general x5, matrix products, nn(): lax.dot_general(left, right, (((1,), (0,)), ((), ())), preferred_element_...  24.3 us
    all_gather x1, waiting for transfers between devices, shards(): down_all = lax.all_gather(w_down, 'mp', axis=0, tiled=True)  23.3 us
    dot_general x5, matrix products, tn(): lax.dot_general(left, right, (((0,), (0,)), ((), ())), preferred_element_...  16.8 us
  transfers between devices with their start and end apart: 8, of which 6 were waited for; matrix products, arithmetic and copies ran while one was open for 21% of the time, Pallas kernels for 2%

profile of v1, /device:TPU:0, one launch (start us, length us, event | category | flops | bytes accessed | tf_op | source)
XLA Modules:
  0.0 425.2 jit_solution(8292570316494859438)
XLA Ops:
  16.1 10.4 %all-gather.5 = f32[8,4,48]{2,1,0:T(4,128)S(1)} all-gather(f32[1,4,48]{2,1,0:T(4,128)S(1)} %maximum_bitcast_fusion), channel_id=3, replica_groups=mesh['dp'=4,'mp'=8] {'mp'}, dimensions={0}, use_global_device_ids=true | all-gather | bytes 6912 | tf_op jit(solution)/shard_map/all_gather | solution.py:447
  43.7 27.0 %all-gather.18.cloned.1.call-done = bf16[40,48,768]{2,1,0:T(8,128)(2,1)} async-done(((bf16[5,48,768]{2,1,0:T(8,128)(2,1)}), bf16[40,48,768]{2,1,0:T(8,128)(2,1)}) %all-gather.18.cloned.1.call-update) | async-done | bytes 2949136 | tf_op jit(solution)/shard_map/all_gather | solution.py:435
  74.4 5.5 %fusion.24.pre = f32[1024,1920]{1,0:T(8,128)} fusion(bf16[1024,768]{1,0:T(8,128)(2,1)S(1)} %bitcast.158, bf16[1920,768]{1,0:T(8,128)(2,1)S(1)} %bitcast.148), kind=kOutput, calls=%fused_computation.104 | convolution fusion | flops 3019898880 | bytes 12386304 | tf_op jit(solution)/shard_map/dot_general | solution.py:377
  80.0 4.7 %shard_map.275 = (f32[1024,768]{1,0:T(8,128)}, f32[1024,384]{1,0:T(8,128)S(1)}, f32[1024,384]{1,0:T(8,128)S(1)}, f32[2,3,8,384]{3,2,1,0:T(8,128)S(1)}, f32[2,8,384]{2,1,0:T(8,128)S(1)}) custom-call(f32[1024,1920]{1,0:T(8,128)} %fusion.24.pre, f32[1,384]{1,0:T(1,128)S(1)} %slice.57.bound, f32[6,384]{1,0:T(8,128)S(1)} %reshape.293.angles), custom_call_target="tpu_custom_call" | custom-call | tf_op jit(solution)/shard_map/pallas_call | solution.py:91
  85.9 9.8 %all-gather.2 = f32[16,8,384]{2,1,0:T(8,128)S(1)} all-gather(f32[2,8,384]{2,1,0:T(8,128)S(1)} %get-tuple-element.27), channel_id=4, replica_groups=mesh['dp'=4,'mp'=8] {'mp'}, dimensions={0}, use_global_device_ids=true | all-gather | bytes 221184 | tf_op jit(solution)/shard_map/all_gather | solution.py:470
  98.2 4.1 multiply_reduce_fusion.5
  102.5 4.1 multiply_reduce_fusion.4
  110.1 7.5 %fusion.26 = f32[1024,1536]{1,0:T(8,128)} fusion(bf16[1024,768]{1,0:T(8,128)(2,1)} %multiply_convert_fusion.5, bf16[1536,768]{1,0:T(8,128)(2,1)} %all-gather.14.cloned.1.call-done), kind=kOutput, calls=%fused_computation.106 | convolution fusion | flops 2415919104 | bytes 10223616 | tf_op jit(solution)/shard_map/dot_general | solution.py:377
  117.6 15.1 %all-gather.12.cloned.1.call-done = bf16[1536,768]{1,0:T(8,128)(2,1)} async-done(((bf16[192,768]{1,0:T(8,128)(2,1)}), bf16[1536,768]{1,0:T(8,128)(2,1)}) %all-gather.12.cloned.1.call-update) | async-done | bytes 2359312 | tf_op jit(solution)/shard_map/all_gather | solution.py:441
  132.7 7.5 %fusion.25 = f32[1024,1536]{1,0:T(8,128)} fusion(bf16[1024,768]{1,0:T(8,128)(2,1)} %multiply_convert_fusion.5, bf16[1536,768]{1,0:T(8,128)(2,1)} %all-gather.12.cloned.1.call-done), kind=kOutput, calls=%fused_computation.105 | convolution fusion | flops 2415919104 | bytes 10223616 | tf_op jit(solution)/shard_map/dot_general | solution.py:377
  140.2 23.3 %all-gather.16.cloned.1.call-done = bf16[1536,768]{1,0:T(8,128)(2,1)} async-done(((bf16[192,768]{1,0:T(8,128)(2,1)}), bf16[1536,768]{1,0:T(8,128)(2,1)}) %all-gather.16.cloned.1.call-update) | async-done | bytes 2359312 | tf_op jit(solution)/shard_map/all_gather | solution.py:443
  163.5 10.5 %multiply_convert_fusion = (bf16[1024,1536]{1,0:T(8,128)(2,1)S(1)}, bf16[1024,1536]{1,0:T(8,128)(2,1)S(1)}, bf16[1024,1536]{1,0:T(8,128)(2,1)}) fusion(f32[1024,1536]{1,0:T(8,128)} %fusion.25, f32[1024,1536]{1,0:T(8,128)} %fusion.26, bf16[1024,768]{1,0:T(8,128)(2,1)} %bitcast.142, bf16[1536,768]{1,0:T(8,128)(2,1)} %all-gather.16.cloned.1.call-done), kind=kOutput, calls=%fused_computation.1 | convolution fusion | flops 2441084928 | bytes 25952256 | tf_op jit(solution)/shard_map/dot_general | solution.py:377
  177.4 5.0 %multiply_reduce_fusion.1 = (f32[768]{0:T(1024)S(1)}, f32[1024]{0:T(1024)S(1)}, f32[1024,768]{1,0:T(8,128)S(1)}) fusion(f32[1024,768]{1,0:T(8,128)} %get-tuple-element.53, f32[1024]{0:T(1024)S(1)} %add_rsqrt_fusion.1, f32[768]{0:T(1024)S(1)} %copy-done.33, f32[1024,768]{1,0:T(8,128)S(1)} %fusion.27, bf16[1024,1536]{1,0:T(8,128)(2,1)S(1)} %get-tuple-element.59, ...), kind=kOutput, calls=%fused_computation.31 | convolution fusion | flops 2421422336 | bytes 14956544 | tf_op jit(solution)/shard_map/dot_general | solution.py:381
  187.9 5.8 %multiply_add_fusion = (f32[1024,768]{1,0:T(8,128)}, bf16[1024,768]{1,0:T(8,128)(2,1)S(1)}, f32[768]{0:T(1024)S(1)}) fusion(f32[1024,768]{1,0:T(8,128)S(1)} %get-tuple-element.31.states, f32[1024]{0:T(1024)S(1)} %fusion.18, f32[768]{0:T(1024)S(1)} %copy-done.30, f32[1024,1920]{1,0:T(8,128)} %fusion.24.pre, bf16[768,768]{1,0:T(8,128)(2,1)S(1)} %bitcast.146, ...), kind=kOutput, calls=%fused_computation.33 | convolution fusion | flops 1224473856 | bytes 15349760 | tf_op jit(solution)/shard_map/dot_general | solution.py:377
  197.4 9.2 %all-gather.4 = f32[16,8,384]{2,1,0:T(8,128)S(1)} all-gather(f32[2,8,384]{2,1,0:T(8,128)S(1)} %get-tuple-element.33), channel_id=6, replica_groups=mesh['dp'=4,'mp'=8] {'mp'}, dimensions={0}, use_global_device_ids=true | all-gather | bytes 221184 | tf_op jit(solution)/shard_map/all_gather | solution.py:517
  206.7 6.9 %shard_map.278 = (bf16[1024,1152]{1,0:T(8,128)(2,1)S(1)}, f32[2,2,8,384]{3,2,1,0:T(8,128)S(1)}) custom-call(s32[1]{0:T(128)} %bitcast.3.me, f32[2,8]{1,0:T(2,128)S(1)} %copy-done.6, f32[8,2,8,384]{3,2,1,0:T(8,128)S(1)} %bitcast.139, f32[1024,768]{1,0:T(8,128)} %get-tuple-element.34.local, f32[1024,384]{1,0:T(8,128)S(1)} %get-tuple-element.35.prods, ...), custom_call_target="tpu_custom_call" | custom-call | tf_op jit(solution)/shard_map/pallas_call | solution.py:340
  213.6 5.3 %fusion.5 = (f32[768]{0:T(1024)S(1)}, f32[1024]{0:T(1024)S(1)}, bf16[1024,768]{1,0:T(8,128)(2,1)S(1)}, f32[1024,768]{1,0:T(8,128)}) fusion(f32[8,64,2,768]{3,0,1,2:T(8,128)S(1)} %copy-done.8, f32[1024]{0:T(1024)S(1)} %copy-done.28, f32[768]{0:T(1024)S(1)} %copy-done.32, bf16[1920,768]{1,0:T(8,128)(2,1)S(1)} %bitcast.149, ...), kind=kOutput, calls=%fused_computation.22 | convolution fusion | flops 3034839296 | bytes 14759936 | tf_op jit(solution)/shard_map/dot_general | solution.py:381
  218.9 4.1 convolution_convert_fusion.3
  225.4 5.2 %convolution_convert_fusion.1 = bf16[1536,768]{1,0:T(8,128)(2,1)S(1)} fusion(bf16[1024,1536]{1,0:T(8,128)(2,1)} %copy-done.44, bf16[1024,768]{1,0:T(8,128)(2,1)} %multiply_convert_fusion.5), kind=kOutput, calls=%fused_computation.9 | convolution fusion | flops 2417098752 | bytes 7077888 | tf_op jit(solution)/shard_map/dot_general | solution.py:385
  240.3 7.3 %add_convert_fusion = bf16[1024,768]{1,0:T(8,128)(2,1)} fusion(f32[1024,768]{1,0:T(8,128)} %get-tuple-element.53, bf16[1024,1536]{1,0:T(8,128)(2,1)} %get-tuple-element.61, bf16[1536,768]{1,0:T(8,128)(2,1)} %all-gather.16.cloned.1.call-done), kind=kOutput, calls=%fused_computation.38 | convolution fusion | flops 2417491968 | bytes 10223616 | tf_op jit(solution)/shard_map/dot_general | solution.py:381
  247.6 28.9 %reduce-scatter.3.cloned.1.call-done = bf16[1,7,48,768]{3,2,1,0:T(8,128)(2,1)} async-done(((bf16[8,7,48,768]{3,2,1,0:T(8,128)(2,1)}), bf16[1,7,48,768]{3,2,1,0:T(8,128)(2,1)}) %reduce-scatter.3.cloned.1.call-update) | async-done | bytes 516112 | tf_op jit(solution)/shard_map/reduce_scatter | solution.py:548
  276.5 69.0 %reduce-scatter.5.cloned.1.call-done = bf16[1,3,192,768]{3,2,1,0:T(8,128)(2,1)} async-done(((bf16[8,3,192,768]{3,2,1,0:T(8,128)(2,1)}), bf16[1,3,192,768]{3,2,1,0:T(8,128)(2,1)}) %reduce-scatter.5.cloned.1.call-update) | async-done | bytes 884752 | tf_op jit(solution)/shard_map/reduce_scatter | solution.py:501
  355.0 41.2 %psum.21 = f32[3072]{0:T(1024)S(1)} all-reduce(f32[3072]{0:T(1024)S(1)} %constant_dynamic-update-slice_fusion), channel_id=1, replica_groups=mesh['dp'=4,'mp'=8] {'dp','mp'}, use_global_device_ids=true, to_apply=%region_13.14 | all-reduce | flops 3072 | bytes 24576 | tf_op jit(solution)/shard_map/psum | solution.py:554
  398.6 13.6 %all-reduce.3.cloned.1.call-done = (bf16[7,48,768]{2,1,0:T(8,128)(2,1)}, bf16[3,192,768]{2,1,0:T(8,128)(2,1)}) async-done(((bf16[7,48,768]{2,1,0:T(8,128)(2,1)}, bf16[3,192,768]{2,1,0:T(8,128)(2,1)}), (bf16[7,48,768]{2,1,0:T(8,128)(2,1)}, bf16[3,192,768]{2,1,0:T(8,128)(2,1)})) %all-reduce.3.cloned.1.call-update) | async-done | bytes 1400848 | tf_op jit(solution)/shard_map/psum | solution.py:549
  (179 shorter events, 78.1 us)
Async XLA Ops:
  7.2 21.4 %copy-start.11 = (bf16[512,2,768]{2,1,0:T(2,128)(2,1)S(1)}, bf16[512,2,768]{2,1,0:T(2,128)(2,1)}, u32[]{:S(2)}) copy-start(bf16[512,2,768]{2,1,0:T(2,128)(2,1)} %param.17) | copy-start | bytes 4718596
  7.2 34.1 %all-gather.20.cloned.1.call-start = ((), (), s32[]{:S(2)}) async-start(), calls=%async_computation.8 | async-start | bytes 1327104 | tf_op jit(solution)/shard_map/all_gather | solution.py:438
  7.9 62.8 %all-gather.18.cloned.1.call-start = ((), (), s32[]{:S(2)}) async-start(), calls=%async_computation.7 | async-start | bytes 3317760 | tf_op jit(solution)/shard_map/all_gather | solution.py:435
  9.8 100.3 %all-gather.14.cloned.1.call-start = ((), (), s32[]{:S(2)}) async-start(), calls=%async_computation.3 | async-start | bytes 2654208 | tf_op jit(solution)/shard_map/all_gather | solution.py:442
  10.5 122.2 %all-gather.12.cloned.1.call-start = ((), (), s32[]{:S(2)}) async-start(), calls=%async_computation.2 | async-start | bytes 2654208 | tf_op jit(solution)/shard_map/all_gather | solution.py:441
  11.1 152.4 %all-gather.16.cloned.1.call-start = ((), (), s32[]{:S(2)}) async-start(), calls=%async_computation.4 | async-start | bytes 2654208 | tf_op jit(solution)/shard_map/all_gather | solution.py:443
  11.7 264.8 %reduce-scatter.3.cloned.1.call-start = ((), (), s32[]{:S(2)}) async-start(), calls=%async_computation.5 | async-start | bytes 4644864 | tf_op jit(solution)/shard_map/reduce_scatter | solution.py:548
  13.1 13.4 %copy-start.34 = (f32[48]{0:T(128)}, f32[48]{0:T(128)S(1)}, u32[]{:S(2)}) copy-start(f32[48]{0:T(128)S(1)} %reduce_max.9) | copy-start | bytes 580
  13.9 12.7 %copy-start.36 = (f32[48]{0:T(128)}, f32[48]{0:T(128)S(1)}, u32[]{:S(2)}) copy-start(f32[48]{0:T(128)S(1)} %fusion.16) | copy-start | bytes 580
  15.4 11.1 %copy-start.38 = (f32[48]{0:T(128)}, f32[48]{0:T(128)S(1)}, u32[]{:S(2)}) copy-start(f32[48]{0:T(128)S(1)} %multiply_reduce_fusion.6) | copy-start | bytes 580
  43.7 30.7 %copy-start.23 = (bf16[2,64,8,768]{3,2,1,0:T(8,128)(2,1)S(1)}, bf16[2,64,8,768]{3,2,1,0:T(8,128)(2,1)}, u32[]{:S(2)}) copy-start(bf16[2,64,8,768]{3,2,1,0:T(8,128)(2,1)} %fusion.9) | copy-start | bytes 4718596
  80.0 15.7 %copy-start.5 = (f32[2,8]{1,0:T(2,128)S(1)}, f32[2,8]{1,0:T(2,128)}, u32[]{:S(2)}) copy-start(f32[2,8]{1,0:T(2,128)} %compare_convert_fusion.1.keep) | copy-start | bytes 196
  85.9 12.3 %copy-start.29 = (f32[768]{0:T(1024)S(1)}, f32[768]{0:T(1024)}, u32[]{:S(2)}) copy-start(f32[768]{0:T(1024)} %mul.383) | copy-start | bytes 9220
  98.1 89.2 %copy-start = (f32[1024,768]{1,0:T(8,128)}, f32[1024,768]{1,0:T(8,128)S(1)}, u32[]{:S(2)}) copy-start(f32[1024,768]{1,0:T(8,128)S(1)} %get-tuple-element.31.states) | copy-start | bytes 9437188
  163.5 10.5 %copy-start.43 = (bf16[1536,768]{1,0:T(8,128)(2,1)S(1)}, bf16[1536,768]{1,0:T(8,128)(2,1)}, u32[]{:S(2)}) copy-start(bf16[1536,768]{1,0:T(8,128)(2,1)} %all-gather.12.cloned.1.call-done) | copy-start | bytes 7077892
  193.7 12.9 %copy-start.4 = (f32[2,2,8,384]{3,2,1,0:T(8,128)S(1)}, f32[2,2,8,384]{3,2,1,0:T(8,128)}, u32[]{:S(2)}) copy-start(f32[2,2,8,384]{3,2,1,0:T(8,128)} %copy-done.3) | copy-start | bytes 147460
  193.8 12.9 %copy-start.6 = (f32[2,8]{1,0:T(2,128)S(1)}, f32[2,8]{1,0:T(2,128)}, u32[]{:S(2)}) copy-start(f32[2,8]{1,0:T(2,128)} %compare_convert_fusion.1.keep) | copy-start | bytes 196
  225.3 120.3 %reduce-scatter.5.cloned.1.call-start = ((), (), s32[]{:S(2)}) async-start(), calls=%async_computation.6 | async-start | bytes 7962624 | tf_op jit(solution)/shard_map/reduce_scatter | solution.py:501
  240.0 172.2 %all-reduce.3.cloned.1.call-start = ((), (), s32[]{:S(2)}) async-start(), calls=%async_computation.9 | async-start | bytes 2801664 | tf_op jit(solution)/shard_map/psum | solution.py:549
  349.3 48.6 %copy-start.27 = (f32[12,48]{1,0:T(8,128)S(1)}, f32[12,48]{1,0:T(8,128)}, u32[]{:S(2)}) copy-start(f32[12,48]{1,0:T(8,128)} %param.26) | copy-start | bytes 6916
  349.3 48.6 %copy-start.35 = (f32[48]{0:T(128)S(1)}, f32[48]{0:T(128)}, u32[]{:S(2)}) copy-start(f32[48]{0:T(128)} %copy-done.34) | copy-start | bytes 580
  349.3 48.6 %copy-start.37 = (f32[48]{0:T(128)S(1)}, f32[48]{0:T(128)}, u32[]{:S(2)}) copy-start(f32[48]{0:T(128)} %copy-done.36) | copy-start | bytes 580
  349.3 48.6 %copy-start.39 = (f32[48]{0:T(128)S(1)}, f32[48]{0:T(128)}, u32[]{:S(2)}) copy-start(f32[48]{0:T(128)} %copy-done.38) | copy-start | bytes 580
  349.3 48.6 %copy-start.41 = (f32[12]{0:T(128)S(1)}, f32[12]{0:T(128)}, u32[]{:S(2)}) copy-start(f32[12]{0:T(128)} %copy-done.40) | copy-start | bytes 148
  (32 other events, 133.1 us)
Sparse Core Ops, SparseCore 0:
  9.9 26.7 all-gather.19
  39.2 31.4 all-gather.17
  72.6 29.2 all-gather.13
  103.6 28.9 all-gather.11
  134.4 29.0 all-gather.15
  225.4 51.0 reduce-scatter.2
  280.0 65.4 reduce-scatter.4
  348.2 63.9 all-reduce.2

commit v2 on v0

v2 whole, which is shorter than its diff:
```python
import functools

import jax
import jax.numpy as jnp
from jax import lax
from jax.experimental import pallas as pl
from jax.experimental.pallas import tpu as pltpu
from jax.sharding import PartitionSpec as P

EPSILON = 1e-06
CHUNKS = 8
TILE = 256
MIB = 1024 * 1024
F32 = jnp.float32
BF16 = jnp.bfloat16


class Near:
    def __init__(self, value):
        self.value = value


def kernel_call(body, grid, in_specs, out_specs, out_shape, scratch=(), vmem=32):
    def space(shape):
        if isinstance(shape, Near):
            return pltpu.VMEM(shape.value.shape, shape.value.dtype)
        return pltpu.HBM(shape.shape, shape.dtype) if shape.size >= 65536 else shape

    def placed(value):
        if isinstance(value, Near):
            return pltpu.with_memory_space_constraint(value.value, pltpu.VMEM)
        if value.size < 65536:
            return value
        return pltpu.with_memory_space_constraint(value, pltpu.HBM)

    single = not isinstance(out_shape, (list, tuple))
    call = pl.pallas_call(
        body,
        grid=grid,
        in_specs=in_specs,
        out_specs=out_specs,
        out_shape=space(out_shape) if single else [space(shape) for shape in out_shape],
        scratch_shapes=scratch,
        cost_estimate=pl.CostEstimate(flops=1, bytes_accessed=1, transcendentals=0),
        compiler_params=pltpu.CompilerParams(vmem_limit_bytes=vmem * MIB),
    )
    return lambda *args: call(*map(placed, args))


def shaped(shape, dtype=F32):
    return jax.ShapeDtypeStruct(shape, dtype)


def whole(shape, start=None):
    start = start or (0,) * len(shape)
    return pl.BlockSpec(shape, lambda *_: start, pipeline_mode=pl.Buffered(1))


def kept(shape):
    zeros = (0,) * len(shape)
    return pl.BlockSpec(shape, lambda *_: zeros)


def per_group(shape):
    zeros = (0,) * (len(shape) - 1)
    return pl.BlockSpec(shape, lambda g, t: (g,) + zeros)


def ahead(tiles, rows, width):
    return pl.BlockSpec((rows, width), lambda g, t: (g * tiles + t, 0))


def behind(tiles, rows, width):
    return pl.BlockSpec((rows, width), lambda g, t: (g * tiles + tiles - 1 - t, 0))


SMEM_SPEC = pl.BlockSpec(memory_space=pltpu.SMEM)
VMEM_SPEC = pl.BlockSpec(memory_space=pltpu.VMEM)


def turn(cos, sin, re, im):
    return cos * re - sin * im, sin * re + cos * im


def back_turn(cos, sin, re, im):
    return cos * re + sin * im, cos * im - sin * re


def sigmoid(values):
    return 0.5 * jnp.tanh(0.5 * values) + 0.5


def nt(left, right):
    return lax.dot_general(left, right, (((1,), (1,)), ((), ())), preferred_element_type=F32)


def nn(left, right):
    return lax.dot_general(left, right, (((1,), (0,)), ((), ())), preferred_element_type=F32)


def tn(left, right):
    return lax.dot_general(left, right, (((0,), (0,)), ((), ())), preferred_element_type=F32)


def rms_rows(values):
    return lax.rsqrt(jnp.mean(values * values, axis=-1, keepdims=True) + EPSILON)


def rms_pull(unit, inv, gain, d_out):
    scaled = d_out * gain
    return inv * (scaled - unit * jnp.mean(scaled * unit, axis=-1, keepdims=True))


def step_rows(j):
    return pl.ds(pl.multiple_of(j * CHUNKS, CHUNKS), CHUNKS)


def chain_chunks(order, turning, angles, prod, end_re, end_im, chain, totals):
    cos_chunk, sin_chunk = angles[2:3, :], angles[3:4, :]
    zero = jnp.zeros_like(prod[0:1])
    run, run_re, run_im = zero + 1.0, zero, zero
    for s in order:
        chain[0, 0, s : s + 1, :] = run
        chain[0, 1, s : s + 1, :] = run_re
        chain[0, 2, s : s + 1, :] = run_im
        turned_re, turned_im = turning(cos_chunk, sin_chunk, run_re, run_im)
        run_re = prod[s : s + 1] * turned_re + end_re[s : s + 1]
        run_im = prod[s : s + 1] * turned_im + end_im[s : s + 1]
        run = run * prod[s : s + 1]
    totals[0] = jnp.zeros_like(prod)
    totals[0, 0:1, :] = run
    totals[0, 1:2, :] = run_re
    totals[0, 2:3, :] = run_im


def project_body(
    steps, chans, tokens, gain, w, bound, angles, normed, pre, pre_out, local, decays, prefix, totals, carry
):
    t = pl.program_id(1)

    @pl.when(t == 0)
    def _():
        carry[0:2] = jnp.zeros((2,) + carry.shape[1:], F32)
        carry[2] = jnp.ones(carry.shape[1:], F32)

    values = tokens[...].astype(F32)
    unit = (values * rms_rows(values) * gain[...]).astype(BF16)
    normed[...] = unit
    low = bound[0:1, :]
    scan = nt(unit, w[4 * chans : 7 * chans, :])
    pre[...] = scan
    decay = low + (1.0 - low) * sigmoid(scan[:, 2 * chans :])
    decays[...] = decay
    in_re, in_im = scan[:, 0:chans], scan[:, chans : 2 * chans]
    local[:, 0:chans] = (1.0 - decay) * (in_re * sigmoid(in_re))
    local[:, chans:] = (1.0 - decay) * (in_im * sigmoid(in_im))
    pre_out[...] = nt(unit, w[2 * chans : 4 * chans, :])
    cos_one, sin_one = angles[0:1, :], angles[1:2, :]

    def step(j, state):
        state_re, state_im, prod = state
        rows = step_rows(j)
        decay = decays[rows, :]
        turned_re, turned_im = turn(cos_one, sin_one, state_re, state_im)
        state_re = decay * turned_re + local[rows, 0:chans]
        state_im = decay * turned_im + local[rows, chans:]
        local[rows, 0:chans] = state_re
        local[rows, chans:] = state_im
        return state_re, state_im, prod * decay

    end_re, end_im, prod = lax.fori_loop(
        0, steps, step, (carry[0], carry[1], carry[2]), unroll=8
    )
    carry[0], carry[1], carry[2] = end_re, end_im, prod

    @pl.when(t == pl.num_programs(1) - 1)
    def _():
        chain_chunks(range(CHUNKS), turn, angles, prod, end_re, end_im, prefix, totals)


def project(tokens, gain, w, bound, angles, groups, chans):
    rows, width = tokens.shape
    per = rows // groups
    tile = min(TILE, per)
    tiles = per // tile
    rowed = functools.partial(ahead, tiles, tile)
    return kernel_call(
        functools.partial(project_body, tile // CHUNKS, chans),
        (groups, tiles),
        [rowed(width), whole((1, width)), whole(w.shape), whole((1, chans)), whole(angles.shape)],
        [
            rowed(width),
            rowed(3 * chans),
            rowed(2 * chans),
            rowed(2 * chans),
            rowed(chans),
            per_group((1, 3, CHUNKS, chans)),
            per_group((1, CHUNKS, chans)),
        ],
        [
            shaped((rows, width), BF16),
            shaped((rows, 3 * chans)),
            shaped((rows, 2 * chans)),
            Near(shaped((rows, 2 * chans))),
            shaped((rows, chans)),
            shaped((groups, 3, CHUNKS, chans)),
            shaped((groups, CHUNKS, chans)),
        ],
        [pltpu.VMEM((3, CHUNKS, chans), F32)],
    )(tokens, gain, w, bound, angles)


def mix_body(
    steps,
    chans,
    blocks,
    me,
    keep,
    gathered,
    local,
    decays,
    prefix,
    angles,
    table,
    pre_out,
    tokens,
    w_out,
    out_gain,
    ffn_gain,
    states,
    entering,
    gated,
    mix_out,
    mid,
    ffn_normed,
    carry,
):
    g, t = pl.program_id(0), pl.program_id(1)

    @pl.when(t == 0)
    def _():
        cos_dev, sin_dev = angles[4:5, :], angles[5:6, :]
        state_re = jnp.zeros((1, chans), F32)
        state_im = jnp.zeros((1, chans), F32)
        for d in range(blocks):
            kept_one = keep[g, d]
            turned_re, turned_im = turn(cos_dev, sin_dev, kept_one * state_re, kept_one * state_im)
            decay = gathered[d, 0, 0:1, :]
            earlier = d < me[0]
            state_re = jnp.where(earlier, decay * turned_re + gathered[d, 0, 1:2, :], state_re)
            state_im = jnp.where(earlier, decay * turned_im + gathered[d, 0, 2:3, :], state_im)
        kept_one = keep[g, me[0]]
        state_re, state_im = kept_one * state_re, kept_one * state_im
        cos_chunk, sin_chunk = angles[2:3, :], angles[3:4, :]
        for s in range(CHUNKS):
            run = prefix[0, 0, s : s + 1, :]
            entering[0, 0, s : s + 1, :] = run * state_re + prefix[0, 1, s : s + 1, :]
            entering[0, 1, s : s + 1, :] = run * state_im + prefix[0, 2, s : s + 1, :]
            state_re, state_im = turn(cos_chunk, sin_chunk, state_re, state_im)
        carry[...] = jnp.ones_like(carry)

    enter_re, enter_im = entering[0, 0], entering[0, 1]

    def step(j, prod):
        rows = step_rows(j)
        prod = prod * decays[rows, :]
        lag = pl.ds(t * steps + j, 1)
        turned_re, turned_im = turn(table[lag, 0:chans], table[lag, chans:], enter_re, enter_im)
        states[rows, 0:chans] = local[rows, 0:chans] + prod * turned_re
        states[rows, chans:] = local[rows, chans:] + prod * turned_im
        return prod

    carry[...] = lax.fori_loop(0, steps, step, carry[...], unroll=8)
    state = states[...]
    inv_rms = rms_rows(state)
    gate = pre_out[...]
    gate_in = (state * out_gain[...] * (gate * sigmoid(gate))).astype(BF16)
    gated[...] = gate_in
    mixed = nn(gate_in, w_out[...])
    mix_out[...] = mixed
    stream = tokens[...].astype(F32) + inv_rms * mixed
    mid[...] = stream
    ffn_normed[...] = (stream * rms_rows(stream) * ffn_gain[...]).astype(BF16)


def mix(
    me, keep, gathered, local, decays, prefix, angles, table, pre_out, tokens, w, out_gain, ffn_gain, groups, chans
):
    rows, width = tokens.shape
    per = rows // groups
    tile = min(TILE, per)
    tiles = per // tile
    blocks = gathered.shape[0]
    rowed = functools.partial(ahead, tiles, tile)
    return kernel_call(
        functools.partial(mix_body, tile // CHUNKS, chans, blocks),
        (groups, tiles),
        [
            SMEM_SPEC,
            SMEM_SPEC,
            pl.BlockSpec((blocks, 1, CHUNKS, chans), lambda g, t: (0, g, 0, 0)),
            rowed(2 * chans),
            rowed(chans),
            per_group((1, 3, CHUNKS, chans)),
            whole(angles.shape),
            whole(table.shape),
            rowed(2 * chans),
            rowed(width),
            whole((2 * chans, width)),
            whole((1, 2 * chans)),
            whole((1, width)),
        ],
        [
            rowed(2 * chans),
            per_group((1, 2, CHUNKS, chans)),
            rowed(2 * chans),
            rowed(width),
            rowed(width),
            rowed(width),
        ],
        [
            shaped((rows, 2 * chans)),
            shaped((groups, 2, CHUNKS, chans)),
            shaped((rows, 2 * chans), BF16),
            shaped((rows, width)),
            shaped((rows, width)),
            Near(shaped((rows, width), BF16)),
        ],
        [pltpu.VMEM((CHUNKS, chans), F32)],
    )(me, keep, gathered, Near(local), decays, prefix, angles, table, pre_out, tokens, w, out_gain, ffn_gain)


def split_by_core(first, grads, span, unit, same, other):
    for chip in range(span // (2 * unit)):
        for k, part in enumerate(grads):
            even = part[2 * chip * unit : (2 * chip + 1) * unit]
            odd = part[(2 * chip + 1) * unit : (2 * chip + 2) * unit]
            rows = slice(k * unit, (k + 1) * unit)
            same[chip, rows, :] = jnp.where(first, even, odd)
            other[chip, rows, :] = jnp.where(first, odd, even)


def swiglu_body(unit, tile, x, up, w, act, d_pre, grads):
    devices = w.shape[0]

    def every(part):
        return jnp.concatenate([w[dev, part] for dev in range(devices)], axis=0)

    span = devices * unit
    w_pre = jnp.concatenate([every(0), every(1)], axis=0)
    w_down = every(2)
    for start in range(0, x.shape[0], tile):
        rows = slice(start, start + tile)
        pre = nt(x[rows, :], w_pre)
        d_hidden = nt(up[rows, :], w_down)
        gate, lift = pre[:, :span], pre[:, span:]
        sigma = sigmoid(gate)
        silu = gate * sigma
        act[rows, :] = (silu * lift).astype(BF16)
        d_pre[rows, :span] = (d_hidden * lift * (sigma + silu * (1.0 - sigma))).astype(BF16)
        d_pre[rows, span:] = (d_hidden * silu).astype(BF16)
    g_pre = tn(d_pre[...], x[...]).astype(BF16)
    g_down = tn(act[...], up[...]).astype(BF16)
    for dev in range(devices):
        own = slice(dev * unit, (dev + 1) * unit)
        grads[dev, 0:unit, :] = g_pre[own]
        grads[dev, unit : 2 * unit, :] = g_pre[span + dev * unit : span + (dev + 1) * unit]
        grads[dev, 2 * unit : 3 * unit, :] = g_down[own]


def units_at_once(blocks, unit):
    devices = 2
    while devices < blocks and (devices * unit % 128 or devices * unit < 384):
        devices *= 2
    return devices


def swiglu(x, up, w):
    rows, width = x.shape
    blocks, _, unit, _ = w.shape
    devices = units_at_once(blocks, unit)
    span = devices * unit
    return kernel_call(
        functools.partial(swiglu_body, unit, min(rows, 512)),
        (blocks // devices,),
        [
            whole((rows, width)),
            whole((rows, width)),
            pl.BlockSpec((devices, 3, unit, width), lambda q: (q, 0, 0, 0)),
        ],
        [
            pl.BlockSpec((rows, span), lambda q: (0, q)),
            pl.BlockSpec((rows, 2 * span), lambda q: (0, q)),
            pl.BlockSpec((devices, 3 * unit, width), lambda q: (q, 0, 0)),
        ],
        [
            shaped((rows, blocks * unit), BF16),
            Near(shaped((rows, 2 * blocks * unit), BF16)),
            shaped((blocks, 3 * unit, width), BF16),
        ],
    )(Near(x), up, w)


def finish_grads(core, acc, kinds, chans, unit, same, other):
    if unit % 16:
        same[...] = acc[...].astype(BF16)
        other[...] = jnp.zeros_like(other)
        return
    grads = [acc[k * chans : (k + 1) * chans, :].astype(BF16) for k in range(kinds)]
    split_by_core(core[0] == 0, grads, chans, unit, same, other)


def grads_shapes(kinds, chans, unit, width):
    if unit % 16:
        return [(kinds * chans, width), (16, width)]
    return [(chans // (2 * unit), kinds * unit, width)] * 2


def first_step():
    return jnp.logical_and(pl.program_id(0) == 0, pl.program_id(1) == 0)


def last_step():
    return jnp.logical_and(
        pl.program_id(0) == pl.num_programs(0) - 1, pl.program_id(1) == pl.num_programs(1) - 1
    )


def mix_back_body(steps, chans, unit_chans, parts, core, *refs):
    d_pres, refs = refs[:parts], refs[parts:]
    (
        w_ffn,
        mid,
        upstream,
        mix_out,
        states,
        pre_out,
        gated,
        normed,
        decays,
        w_out,
        out_gain,
        ffn_gain,
        angles,
        d_mid,
        d_outgate,
        local,
        suffix,
        totals,
        same,
        other,
        sums,
        acc,
        w_pre,
        carry,
    ) = refs
    blocks, _, units, _ = w_ffn.shape
    unit = units // parts
    devices = units_at_once(blocks, unit)

    @pl.when(first_step())
    def _():
        acc[...] = jnp.zeros_like(acc)
        sums[...] = jnp.zeros_like(sums)
        at = 0
        for part in range(parts):
            for q in range(0, blocks, devices):
                for kind in (0, 1):
                    for dev in range(q, q + devices):
                        w_pre[at : at + unit, :] = w_ffn[dev, kind, part * unit : (part + 1) * unit, :]
                        at += unit

    @pl.when(pl.program_id(1) == 0)
    def _():
        carry[0:2] = jnp.zeros((2,) + carry.shape[1:], F32)
        carry[2] = jnp.ones(carry.shape[1:], F32)

    span = 2 * units * blocks // parts
    d_norm = nn(d_pres[0][...], w_pre[0:span, :])
    for part in range(1, parts):
        d_norm += nn(d_pres[part][...], w_pre[part * span : (part + 1) * span, :])
    stream = mid[...]
    inv_mid = rms_rows(stream)
    unit_mid = stream * inv_mid
    sums[0:1, :] += jnp.sum(d_norm * unit_mid, axis=0, keepdims=True)
    d_stream = upstream[...].astype(F32) + rms_pull(unit_mid, inv_mid, ffn_gain[...], d_norm)
    d_mid[...] = d_stream
    state = states[...]
    inv_rms = rms_rows(state)
    d_mix = (inv_rms * d_stream).astype(BF16)
    d_rms = jnp.sum(d_stream * mix_out[...], axis=-1, keepdims=True)
    d_square = (-0.5 / chans) * inv_rms * inv_rms * inv_rms * d_rms
    d_gated = nt(d_mix, w_out[...])
    gate = pre_out[...]
    sigma = sigmoid(gate)
    silu = gate * sigma
    gain = out_gain[...]
    local[...] = d_gated * gain * silu + d_square * state
    d_state_gate = d_gated * state
    sums[1:2, :] += jnp.sum(d_state_gate * silu, axis=0, keepdims=True)
    d_gate = (d_state_gate * gain * (sigma + silu * (1.0 - sigma))).astype(BF16)
    d_outgate[...] = d_gate
    acc[0 : 2 * chans, :] += tn(gated[...], d_mix)
    acc[2 * chans : 4 * chans, :] += tn(d_gate, normed[...])
    cos_one, sin_one = angles[0:1, :], angles[1:2, :]

    def step(i, flow):
        flow_re, flow_im, prod = flow
        rows = step_rows(steps - 1 - i)
        grad_re = local[rows, 0:chans] + flow_re
        grad_im = local[rows, chans:] + flow_im
        local[rows, 0:chans] = grad_re
        local[rows, chans:] = grad_im
        decay = decays[rows, :]
        turned_re, turned_im = back_turn(cos_one, sin_one, grad_re, grad_im)
        return decay * turned_re, decay * turned_im, prod * decay

    end_re, end_im, prod = lax.fori_loop(
        0, steps, step, (carry[0], carry[1], carry[2]), unroll=8
    )
    carry[0], carry[1], carry[2] = end_re, end_im, prod

    @pl.when(pl.program_id(1) == pl.num_programs(1) - 1)
    def _():
        chain_chunks(reversed(range(CHUNKS)), back_turn, angles, prod, end_re, end_im, suffix, totals)

    @pl.when(last_step())
    def _():
        finish_grads(core, acc, 4, chans, unit_chans, same, other)


def mix_back(
    core,
    unit_chans,
    d_pres,
    w_ffn,
    mid,
    upstream,
    mix_out,
    states,
    pre_out,
    gated,
    normed,
    decays,
    w,
    out_gain,
    ffn_gain,
    angles,
    groups,
    chans,
):
    rows, width = mid.shape
    per = rows // groups
    tile = min(TILE, per)
    tiles = per // tile
    blocks, _, units, _ = w_ffn.shape
    parts = len(d_pres)
    rowed = functools.partial(behind, tiles, tile)
    return kernel_call(
        functools.partial(mix_back_body, tile // CHUNKS, chans, unit_chans, parts),
        (groups, tiles),
        [SMEM_SPEC]
        + [rowed(part.shape[1]) for part in d_pres]
        + [
            whole((blocks, 2, units, width)),
            rowed(width),
            rowed(width),
            rowed(width),
            rowed(2 * chans),
            rowed(2 * chans),
            rowed(2 * chans),
            rowed(width),
            rowed(chans),
            whole((2 * chans, width)),
            whole((1, 2 * chans)),
            whole((1, width)),
            whole(angles.shape),
        ],
        [
            rowed(width),
            rowed(2 * chans),
            rowed(2 * chans),
            per_group((1, 3, CHUNKS, chans)),
            per_group((1, CHUNKS, chans)),
            *map(kept, grads_shapes(4, chans, unit_chans, width)),
            kept((8, width)),
        ],
        [
            shaped((rows, width)),
            shaped((rows, 2 * chans), BF16),
            Near(shaped((rows, 2 * chans))),
            shaped((groups, 3, CHUNKS, chans)),
            shaped((groups, CHUNKS, chans)),
            *(shaped(shape, BF16) for shape in grads_shapes(4, chans, unit_chans, width)),
            shaped((8, width)),
        ],
        [
            pltpu.VMEM((4 * chans, width), F32),
            pltpu.VMEM((2 * blocks * units, width), BF16),
            pltpu.VMEM((3, CHUNKS, chans), F32),
        ],
        vmem=46,
    )(
        core,
        *map(Near, d_pres),
        w_ffn,
        mid,
        upstream,
        mix_out,
        states,
        pre_out,
        gated,
        normed,
        decays,
        w,
        out_gain,
        ffn_gain,
        angles,
    )


def silu_slope(values, sigma):
    return sigma * (1.0 + values * (1.0 - sigma))


def adjoint_finish_body(
    steps,
    chans,
    blocks,
    unit_chans,
    me,
    core,
    keep,
    gathered,
    local,
    decays,
    suffix,
    pre,
    states,
    before,
    entering,
    bound,
    angles,
    table,
    normed,
    d_pre,
    sums,
    same,
    other,
    leaving,
    full,
    acc,
    carry,
):
    g, t = pl.program_id(0), pl.program_id(1)
    tiles = pl.num_programs(1)

    @pl.when(first_step())
    def _():
        acc[...] = jnp.zeros_like(acc)

    @pl.when(t == 0)
    def _():
        cos_chunk, sin_chunk = angles[2:3, :], angles[3:4, :]
        cos_dev, sin_dev = angles[4:5, :], angles[5:6, :]
        flow_re = jnp.zeros((1, chans), F32)
        flow_im = jnp.zeros((1, chans), F32)
        for d in reversed(range(blocks)):
            kept_one = keep[g, d]
            turned_re, turned_im = back_turn(cos_dev, sin_dev, flow_re, flow_im)
            decay = gathered[d, 0, 0:1, :]
            later = d > me[0]
            flow_re = jnp.where(
                later, kept_one * (decay * turned_re + gathered[d, 0, 1:2, :]), flow_re
            )
            flow_im = jnp.where(
                later, kept_one * (decay * turned_im + gathered[d, 0, 2:3, :]), flow_im
            )
        for s in reversed(range(CHUNKS)):
            run = suffix[0, 0, s : s + 1, :]
            leaving[0, s : s + 1, :] = run * flow_re + suffix[0, 1, s : s + 1, :]
            leaving[1, s : s + 1, :] = run * flow_im + suffix[0, 2, s : s + 1, :]
            flow_re, flow_im = back_turn(cos_chunk, sin_chunk, flow_re, flow_im)
        carry[...] = jnp.ones_like(carry)
        sums[...] = jnp.zeros_like(sums)

    low = bound[0:1, :]
    cos_one, sin_one = angles[0:1, :], angles[1:2, :]
    leave_re, leave_im = leaving[0], leaving[1]

    def step(i, prod):
        rows = step_rows(steps - 1 - i)
        lag = pl.ds(t * steps + i, 1)
        turned_re, turned_im = back_turn(table[lag, 0:chans], table[lag, chans:], leave_re, leave_im)
        full[rows, 0:chans] = local[rows, 0:chans] + prod * turned_re
        full[rows, chans:] = local[rows, chans:] + prod * turned_im
        return prod * decays[rows, :]

    carry[...] = lax.fori_loop(0, steps, step, carry[...], unroll=8)
    first_tile = t == tiles - 1
    last_re = jnp.where(first_tile, entering[0, 0], before[:, 0:chans])
    last_im = jnp.where(first_tile, entering[0, 1], before[:, chans:])
    if steps > 1:
        rows = slice(0, (steps - 1) * CHUNKS)
        last_re = jnp.concatenate([last_re, states[rows, 0:chans]], axis=0)
        last_im = jnp.concatenate([last_im, states[rows, chans:]], axis=0)
    grad_re, grad_im = full[:, 0:chans], full[:, chans:]
    in_re, in_im = pre[:, 0:chans], pre[:, chans : 2 * chans]
    sigma_re, sigma_im = sigmoid(in_re), sigmoid(in_im)
    sigma = sigmoid(pre[:, 2 * chans :])
    decay = decays[...]
    cross_re = grad_re * last_re + grad_im * last_im
    cross_im = grad_im * last_re - grad_re * last_im
    along, across = back_turn(cos_one, sin_one, cross_re, cross_im)
    d_decay = along - (grad_re * in_re * sigma_re + grad_im * in_im * sigma_im)
    rest = 1.0 - decay
    d_low = d_decay * (1.0 - sigma)
    d_re = (grad_re * rest * silu_slope(in_re, sigma_re)).astype(BF16)
    d_im = (grad_im * rest * silu_slope(in_im, sigma_im)).astype(BF16)
    d_forget = (d_low * (1.0 - low) * sigma).astype(BF16)
    d_pre[:, 0:chans] = d_re
    d_pre[:, chans : 2 * chans] = d_im
    d_pre[:, 2 * chans :] = d_forget
    sums[0, 0] += jnp.sum((decay * across).reshape(steps, CHUNKS, chans), axis=0)
    sums[0, 1] += jnp.sum(d_low.reshape(steps, CHUNKS, chans), axis=0)
    acc[...] += tn(d_pre[...], normed[...])

    @pl.when(last_step())
    def _():
        finish_grads(core, acc, 3, chans, unit_chans, same, other)


def adjoint_finish(
    unit_chans,
    me,
    core,
    keep,
    gathered,
    local,
    decays,
    suffix,
    pre,
    states,
    entering,
    bound,
    angles,
    table,
    normed,
    groups,
    chans,
):
    rows, width = normed.shape
    per = rows // groups
    tile = min(TILE, per)
    tiles = per // tile
    steps = tile // CHUNKS
    blocks = gathered.shape[0]
    rowed = functools.partial(behind, tiles, tile)

    def one_before(g, t):
        return (jnp.maximum((g * tiles + tiles - 1 - t) * steps - 1, 0), 0)

    return kernel_call(
        functools.partial(adjoint_finish_body, steps, chans, blocks, unit_chans),
        (groups, tiles),
        [
            SMEM_SPEC,
            SMEM_SPEC,
            SMEM_SPEC,
            pl.BlockSpec((blocks, 1, CHUNKS, chans), lambda g, t: (0, g, 0, 0)),
            rowed(2 * chans),
            rowed(chans),
            per_group((1, 3, CHUNKS, chans)),
            rowed(3 * chans),
            rowed(2 * chans),
            pl.BlockSpec((CHUNKS, 2 * chans), one_before),
            per_group((1, 2, CHUNKS, chans)),
            whole((1, chans)),
            whole(angles.shape),
            whole(table.shape),
            rowed(width),
        ],
        [
            rowed(3 * chans),
            per_group((1, 2, CHUNKS, chans)),
            *map(kept, grads_shapes(3, chans, unit_chans, width)),
        ],
        [
            Near(shaped((rows, 3 * chans), BF16)),
            shaped((groups, 2, CHUNKS, chans)),
            *(shaped(shape, BF16) for shape in grads_shapes(3, chans, unit_chans, width)),
        ],
        [
            pltpu.VMEM((2, CHUNKS, chans), F32),
            pltpu.VMEM((tile, 2 * chans), F32),
            pltpu.VMEM((3 * chans, width), F32),
            pltpu.VMEM((CHUNKS, chans), F32),
        ],
    )(
        me,
        core,
        keep,
        gathered,
        Near(local),
        decays,
        suffix,
        pre,
        states,
        states,
        entering,
        bound,
        angles,
        table,
        normed,
    )


def tokens_back_body(chans, d_scan, d_outgate, w, tokens, d_mid, gain, early, scan, grad_tokens, sums):
    @pl.when(first_step())
    def _():
        sums[...] = jnp.zeros_like(sums)
        sums[1:3, :] = early[0:2, :]
        sums[3:4, 0:chans] = jnp.sum(scan[:, 0], axis=(0, 1))[None]
        sums[3:4, chans : 2 * chans] = jnp.sum(scan[:, 1], axis=(0, 1))[None]

    d_normed = nn(d_scan[...], w[4 * chans : 7 * chans, :])
    d_normed += nn(d_outgate[...], w[2 * chans : 4 * chans, :])
    values = tokens[...].astype(F32)
    inv = rms_rows(values)
    unit = values * inv
    sums[0:1, :] += jnp.sum(d_normed * unit, axis=0, keepdims=True)
    grad_tokens[...] = (d_mid[...] + rms_pull(unit, inv, gain[...], d_normed)).astype(BF16)


def tokens_back(d_scan, d_outgate, w, tokens, d_mid, gain, early, scan, groups, chans):
    rows, width = tokens.shape
    per = rows // groups
    tile = min(TILE, per)
    tiles = per // tile
    rowed = functools.partial(ahead, tiles, tile)
    return kernel_call(
        functools.partial(tokens_back_body, chans),
        (groups, tiles),
        [
            rowed(3 * chans),
            rowed(2 * chans),
            whole(w.shape),
            rowed(width),
            rowed(width),
            whole((1, width)),
            whole(early.shape),
            whole(scan.shape),
        ],
        [rowed(width), kept((8, width))],
        [Near(shaped((rows, width), BF16)), shaped((8, width))],
        vmem=20,
    )(Near(d_scan), d_outgate, w, tokens, d_mid, gain, early, scan)


def result_body(parts, *refs):
    acts, (w_down, mid, result) = refs[:parts], refs[parts:]
    blocks, _, units, _ = w_down.shape
    unit = units // parts
    total = mid[...]
    for part, act in enumerate(acts):
        rows = slice(part * unit, (part + 1) * unit)
        total += nn(
            act[...], jnp.concatenate([w_down[dev, 0, rows, :] for dev in range(blocks)], axis=0)
        )
    result[...] = total.astype(BF16)


def block_result(acts, w_ffn, mid):
    rows, width = mid.shape
    blocks, _, units, _ = w_ffn.shape
    tile = min(TILE, rows)

    def rowed(wide):
        return pl.BlockSpec((tile, wide), lambda i: (i, 0))

    return kernel_call(
        functools.partial(result_body, len(acts)),
        (rows // tile,),
        [rowed(act.shape[1]) for act in acts]
        + [whole((blocks, 1, units, width), (0, 2, 0, 0)), rowed(width)],
        rowed(width),
        Near(shaped((rows, width), BF16)),
        vmem=20,
    )(*acts, w_ffn, mid)


def swap(values, axis, bit, size):
    return lax.ppermute(values, axis, [(i, i ^ bit) for i in range(size)])


def joined(*parts):
    return sum(part.astype(F32) for part in parts)


def pick(values, index, axis):
    return lax.dynamic_index_in_dim(values, index, axis, keepdims=False)


def gather_pieces(shard, size):
    half = shard.shape[0] // 2
    near_x = swap(shard, "mp", 2, size)
    near_y = swap(shard, "mp", 4, size)
    core = swap(shard, "mp", 1, size)
    far_one = swap(near_x[:half], "mp", 4, size)
    far_two = swap(near_y[half:], "mp", 2, size)
    core_x = swap(near_x, "mp", 1, size)
    core_y = swap(near_y, "mp", 1, size)
    far = jnp.concatenate([far_one, far_two], axis=0)
    core_far = swap(far, "mp", 1, size)
    return shard, core, near_x, core_x, near_y, core_y, far, core_far


def reduce_mp(grads):
    return lax.psum_scatter(grads, "mp", scatter_dimension=0, tiled=False)


def sends_body(chip, same, got, out_x, out_y, out_far):
    for b, out in ((1, out_x), (2, out_y), (3, out_far)):
        at = chip[0] ^ b
        out[...] = (same[at].astype(F32) + got[at].astype(F32)).astype(BF16)


def sends(chip, same, got):
    return pl.pallas_call(
        sends_body,
        in_specs=[SMEM_SPEC, VMEM_SPEC, VMEM_SPEC],
        out_specs=[VMEM_SPEC] * 3,
        out_shape=[jax.ShapeDtypeStruct(same.shape[1:], BF16)] * 3,
        cost_estimate=pl.CostEstimate(flops=1, bytes_accessed=1, transcendentals=0),
        compiler_params=pltpu.CompilerParams(vmem_limit_bytes=16 * MIB),
    )(chip, same, got)


class Reduction:
    def __init__(self, same, other, chip, size, layers):
        self.same, self.chip, self.size, self.layers = same, chip, size, layers
        self.flying = [swap(other, "mp", 1, size)]

    def arrived(self, *others):
        count = len(self.flying)
        both = tied(*self.flying, *others)
        self.flying = both[:count]
        return both[count:] if len(others) > 1 else both[-1]

    def to_chips(self, other):
        self.got = self.flying[0]
        *parts, other = tied(*sends(self.chip, self.same, self.got), other)
        self.flying = [swap(part, "mp", 2 * b, self.size) for b, part in zip((1, 2, 3), parts)]
        return other

    def share_here(self):
        at = self.chip[0]
        mine = pick(self.same, at, 0), pick(self.got, at, 0)
        return joined(*mine, *self.flying).astype(BF16)

    def to_layer(self, number, other):
        if number == 1:
            self.share = self.share_here()
        else:
            self.share = joined(self.share, *self.flying).astype(BF16)
        self.share, other = tied(self.share, other)
        self.flying = [swap(self.share, "dp", number, self.layers)]
        return other

    def total(self):
        return joined(self.share, *self.flying).astype(BF16).astype(F32)


def assemble_body(kinds, size, me, *refs):
    out, extra = refs[-2:]
    for b, ref in enumerate(refs[:-2]):
        d = me[0] ^ b
        for k in range(kinds):
            out[k, d] = ref[k * size : (k + 1) * size, :]
        extra[d] = ref[kinds * size :, :]


def assemble(me, pieces, kinds, size):
    rows, width = pieces[0].shape
    vmem = VMEM_SPEC
    return pl.pallas_call(
        functools.partial(assemble_body, kinds, size),
        in_specs=[SMEM_SPEC] + [vmem] * len(pieces),
        out_specs=[vmem, vmem],
        out_shape=[
            jax.ShapeDtypeStruct((kinds, len(pieces), size, width), BF16),
            jax.ShapeDtypeStruct((len(pieces), rows - kinds * size, width), BF16),
        ],
        cost_estimate=pl.CostEstimate(flops=1, bytes_accessed=1, transcendentals=0),
        compiler_params=pltpu.CompilerParams(vmem_limit_bytes=16 * MIB),
    )(me, *pieces)


def split_three(values):
    one = lax.reduce_precision(values, 8, 7)
    two = lax.reduce_precision(values - one, 8, 7)
    three = values - one - two
    return jnp.stack([one, two, three], axis=0).astype(BF16)


def tied(*values):
    return lax.optimization_barrier(values)


def shards(
    tokens,
    upstream,
    pieces,
    layer_index,
    mix_gain,
    w_input,
    w_forget,
    w_outgate,
    phase_angle,
    lower_logits,
    out_gain,
    w_output,
    ffn_gain,
    w_gate,
    w_up,
    w_down,
):
    rows_dev, groups, width = tokens.shape
    blocks = lax.axis_size("mp")
    me = lax.axis_index("mp")
    layers_z = lax.axis_size("dp")
    seq_len = rows_dev * blocks
    chans_dev = w_input.shape[2]
    chans = chans_dev * blocks
    units_dev = w_gate.shape[1]
    units = units_dev * blocks
    steps = rows_dev // CHUNKS
    rows = rows_dev * groups

    def to_rows(values):
        return jnp.transpose(
            values.reshape(CHUNKS, steps, groups, width), (2, 1, 0, 3)
        ).reshape(rows, width)

    def from_rows(values):
        return jnp.transpose(
            values.reshape(groups, steps, CHUNKS, width), (2, 1, 0, 3)
        ).reshape(rows_dev, groups, width)

    me_one = me[None].astype(jnp.int32)
    layer_mask = (jnp.arange(lower_logits.shape[0], dtype=jnp.int32) < layer_index[0]).astype(F32)
    soft = jax.nn.softmax(lower_logits, axis=0)
    bound_own = jnp.sum(soft * layer_mask[:, None], axis=0)
    small = jnp.concatenate([bound_own[None], phase_angle[None], out_gain], axis=0)
    mix_shard = jnp.concatenate(
        [
            w_output,
            jnp.transpose(w_outgate, (1, 2, 0)),
            jnp.transpose(w_input, (1, 2, 0)),
            jnp.transpose(w_forget)[None],
        ],
        axis=0,
    ).reshape(7 * chans_dev, width)
    if blocks == 8 and 4 * chans_dev <= width:
        terms = split_three(small.reshape(1, -1)).reshape(3, 4 * chans_dev)
        terms = jnp.pad(terms, ((0, 13), (0, width - 4 * chans_dev)))
        pieces_w = gather_pieces(jnp.concatenate([mix_shard, terms], axis=0), blocks)
        w_mix, extra = assemble(me_one, pieces_w, 7, chans_dev)
        small = jnp.sum(extra[:, 0:3, 0 : 4 * chans_dev].astype(F32), axis=1)
        small = small.reshape(blocks, 4, chans_dev)
    else:
        w_mix = lax.all_gather(mix_shard.reshape(7, chans_dev, width), "mp", axis=0)
        w_mix = jnp.transpose(w_mix, (1, 0, 2, 3))
        small = lax.all_gather(small, "mp", axis=0)
    w_mix = w_mix.reshape(7 * chans, width)
    ffn_shard = jnp.concatenate([jnp.transpose(w_gate), jnp.transpose(w_up), w_down], axis=0)
    w_ffn = lax.all_gather(ffn_shard, "mp", axis=0)

    small = jnp.transpose(small, (1, 0, 2)).reshape(4, chans)
    bound = small[0:1]
    phase = small[1:2]
    gain_row = small[2:4].reshape(1, 2 * chans)
    spans = phase * jnp.array([[1.0], [steps], [rows_dev]], F32)
    angles = jnp.stack([jnp.cos(spans), jnp.sin(spans)], axis=1).reshape(6, chans)
    lags = phase * jnp.arange(steps + 1, dtype=F32)[:, None]
    table = jnp.concatenate([jnp.cos(lags), jnp.sin(lags)], axis=1)
    starts = jnp.arange(blocks, dtype=jnp.int32) * rows_dev
    keep = (starts[None, :] % (seq_len // pieces)[:, None] != 0).astype(F32)

    tok = to_rows(tokens)
    up_rows = to_rows(upstream)
    mix_row, ffn_row = mix_gain[None], ffn_gain[None]
    normed, pre, pre_out, local, decays, prefix, totals = project(
        tok, mix_row, w_mix, bound, angles, groups, chans
    )
    ends = lax.all_gather(totals, "mp", axis=0)
    states, entering, gated, mix_out, mid, ffn_normed = mix(
        me_one,
        keep,
        ends,
        local,
        decays,
        prefix,
        angles,
        table[1:],
        pre_out,
        tok,
        w_mix,
        gain_row,
        ffn_row,
        groups,
        chans,
    )
    by_hand = blocks == 8 and layers_z == 4
    core = (me & 1) if by_hand else jnp.zeros_like(me)
    core_one = core[None].astype(jnp.int32)
    chip_one = (me >> 1)[None].astype(jnp.int32)
    w_ffn = w_ffn.reshape(blocks, 3, units_dev, width)

    def reduction(same, other):
        return Reduction(same, other, chip_one, blocks, layers_z)

    act, d_pre, grad_ffn = swiglu(ffn_normed, up_rows, w_ffn)
    grad_ffn = lax.psum(reduce_mp(grad_ffn), "dp")
    acts, d_pres = [act], [d_pre]
    d_mid, d_outgate, back_local, suffix, back_totals, same, other, early_sums = mix_back(
        core_one,
        chans_dev,
        d_pres,
        w_ffn,
        mid,
        up_rows,
        mix_out,
        states,
        pre_out,
        gated,
        normed,
        decays,
        w_mix,
        gain_row,
        ffn_row,
        angles,
        groups,
        chans,
    )
    if by_hand:
        early = reduction(same, other)
    else:
        early = jnp.moveaxis(same.reshape(4, blocks, chans_dev, width), 1, 0)
    back_ends = lax.all_gather(back_totals, "mp", axis=0)
    if by_hand:
        back_ends = early.to_chips(early.arrived(back_ends))
    d_scan, sums, same, other = adjoint_finish(
        chans_dev,
        me_one,
        core_one,
        keep,
        back_ends,
        back_local,
        decays,
        suffix,
        pre,
        states,
        entering,
        bound,
        angles,
        table[:-1],
        normed,
        groups,
        chans,
    )
    if by_hand:
        other, d_scan = early.arrived(other, d_scan)
        late = reduction(same, other)
        d_scan = early.to_layer(1, d_scan)
        mid, d_scan = tied(mid, d_scan)
        result = block_result(acts, w_ffn, mid)
        d_scan = late.to_chips(late.arrived(d_scan, result)[0])
    else:
        late = jnp.moveaxis(same.reshape(3, blocks, chans_dev, width), 1, 0)
    grad_tokens, flat = tokens_back(
        d_scan, d_outgate, w_mix, tok, d_mid, mix_row, early_sums, sums, groups, chans
    )
    if by_hand:
        flat = early.to_layer(2, early.arrived(flat))
    else:
        early = lax.psum(reduce_mp(early.reshape(blocks, -1, width)), "dp").astype(F32)
        late = lax.psum(reduce_mp(late.reshape(blocks, -1, width)), "dp").astype(F32)
    if by_hand:
        flat = flat + swap(flat, "mp", 1, blocks)
        out_tokens, out_result = from_rows(grad_tokens), from_rows(result)
        flat, out_tokens, out_result = late.arrived(flat, out_tokens, out_result)
        flat = late.to_layer(1, flat)
        flat = flat + swap(flat, "mp", 2, blocks)
        flat = flat + swap(flat, "mp", 4, blocks)
        flat = late.to_layer(2, late.arrived(flat))
        flat = flat + swap(flat, "dp", 1, layers_z)
        flat = flat + swap(flat, "dp", 2, layers_z)
        early, late = early.total(), late.total()
    else:
        flat = lax.psum(flat, ("dp", "mp"))
        out_tokens, out_result = from_rows(grad_tokens), from_rows(block_result(acts, w_ffn, mid))
    grad_ffn = grad_ffn.astype(F32).reshape(3, units_dev, width)
    early = early.reshape(4, chans_dev, width)
    late = late.reshape(3, chans_dev, width)
    own = me * chans_dev

    def own_part(row, offset):
        return lax.dynamic_slice(flat, (row, offset * chans + own), (1, chans_dev))[0]

    grad_gain = jnp.stack([own_part(2, 0), own_part(2, 1)], axis=0)
    d_bound = own_part(3, 1)
    grad_lower = soft * (layer_mask[:, None] - bound_own[None]) * d_bound[None]
    return (
        out_result,
        out_tokens,
        flat[0],
        jnp.transpose(late[0:2], (2, 0, 1)),
        jnp.transpose(late[2]),
        jnp.transpose(early[2:4], (2, 0, 1)),
        own_part(3, 0),
        grad_lower,
        grad_gain,
        early[0:2],
        flat[1],
        jnp.transpose(grad_ffn[0]),
        jnp.transpose(grad_ffn[1]),
        grad_ffn[2],
    )


def solution(mesh):
    in_specs = (
        P("mp", "dp", None),
        P("mp", "dp", None),
        P("dp"),
        P(),
        P(),
        P(None, None, "mp"),
        P(None, "mp"),
        P(None, None, "mp"),
        P("mp"),
        P(None, "mp"),
        P(None, "mp"),
        P(None, "mp", None),
        P(),
        P(None, "mp"),
        P(None, "mp"),
        P("mp", None),
    )
    out_specs = (
        P("mp", "dp", None),
        P("mp", "dp", None),
        P(),
        P(None, None, "mp"),
        P(None, "mp"),
        P(None, None, "mp"),
        P("mp"),
        P(None, "mp"),
        P(None, "mp"),
        P(None, "mp", None),
        P(),
        P(None, "mp"),
        P(None, "mp"),
        P("mp", None),
    )
    return jax.shard_map(shards, mesh=mesh, in_specs=in_specs, out_specs=out_specs, check_vma=False)
```

time: 1650 us -> 276 us (0.17)
  waiting for transfers between devices: 829 us -> 86.9 us
  local copies, waits for them, and re-layouts: 327 us -> 31.9 us
  other arithmetic: 277 us -> 8.03 us
  matrix products: 120 us -> 0 us
  Pallas kernels: 0 us -> 88.9 us
  blocking collectives: 61.7 us -> 21 us
  starting transfers between devices: 1.38 us -> 23.8 us
    reduce_scatter x4 -> x1, waiting for transfers between devices: 486 us -> 0.01 us  [reduce_mp(): return lax.psum_scatter(grads, 'mp', scatter_dimension=0, tiled=False)]
    all_gather x4 -> x1, waiting for transfers between devices: 242 us -> 0.01 us  [shards(): w_ffn = lax.all_gather(ffn_shard, 'mp', axis=0)]
    slice x126 -> x10, local copies, waits for them, and re-layouts: 142 us -> 3.2 us  [the longest x1 0.85 us: shards(): grad_ffn[2]]
    dot_general x12 -> x0, matrix products: 120 us -> none  [the longest x1 15.8 us: shards(): jnp.einsum('tsd,fd->tsf', part_up, w_down, preferred_element_type=jnp.flo...]
    dynamic_update_slice x64 -> x0, other arithmetic: 109 us -> none  [blocked_scan(): totals, inner = lax.scan(advance, start, blocked)]
    pallas_call x0 -> x10, Pallas kernels: none -> 88.9 us  [the longest x7 86.9 us: kernel_call(): return lambda *args: call(*map(placed, args))]
    psum x2 -> x0, blocking collectives: 53.2 us -> none  [the longest x1 39.4 us: shards(): lax.psum((grad_mix_gain, grad_ffn_gain), ('dp', 'mp'))]
    ppermute x0 -> x25, waiting for transfers between devices: none -> 47.4 us  [swap(): return lax.ppermute(values, axis, [(i, i ^ bit) for i in range(size)])]
  transfers between devices with their start and end apart: 10 -> 28, of which waited for: 10 -> 15; matrix products, arithmetic and copies ran while one was open for 6% -> 7% of each run, Pallas kernels for 0% -> 25%
where the time goes in v2:
time: 276 us
  Pallas kernels  88.9 us (32%)
  waiting for transfers between devices  86.9 us (31%)
  local copies, waits for them, and re-layouts  31.9 us (12%)
  starting transfers between devices  23.8 us (9%)
  blocking collectives  21 us (8%)
  between operations  15 us (5%)
  other arithmetic  8.03 us (3%)
    pallas_call x7, Pallas kernels, kernel_call(): return lambda *args: call(*map(placed, args))  86.9 us
    ppermute x25, waiting for transfers between devices, swap(): return lax.ppermute(values, axis, [(i, i ^ bit) for i in range(size)])  47.4 us
    psum x1, waiting for transfers between devices, shards(): grad_ffn = lax.psum(reduce_mp(grad_ffn), 'dp')  39.4 us
    ppermute x25, starting transfers between devices, swap(): return lax.ppermute(values, axis, [(i, i ^ bit) for i in range(size)])  23.5 us
    unnamed x69, local copies, waits for them, and re-layouts  14.9 us
    all_gather x1, blocking collectives, shards(): ends = lax.all_gather(totals, 'mp', axis=0)  11 us
    all_gather x1, blocking collectives, shards(): back_ends = lax.all_gather(back_totals, 'mp', axis=0)  10 us
    reshape x2, local copies, waits for them, and re-layouts, to_rows(): values.reshape(CHUNKS, steps, groups, width)  5.56 us
  transfers between devices with their start and end apart: 28, of which 15 were waited for; matrix products, arithmetic and copies ran while one was open for 7% of the time, Pallas kernels for 25%

profile of v2, /device:TPU:0, one launch (start us, length us, event | category | flops | bytes accessed | tf_op | source)
XLA Modules:
  0.0 275.5 jit_solution(6885253016706723118)
XLA Ops:
  11.2 3.0 %collective-permute-start.1 = (bf16[352,768]{1,0:T(8,128)(2,1)S(1)}, bf16[352,768]{1,0:T(8,128)(2,1)S(1)}, u32[]{:S(2)}, u32[]{:S(2)}) collective-permute-start(bf16[352,768]{1,0:T(8,128)(2,1)S(1)} %pad_maximum_fusion.1.refs_0_), channel_id=1, source_target_pairs={{0,2},{1,3},{2,0},{3,1},{4,6},{5,7},{6,4},{7,5},{8,10},{9,11},{10,... | collective-permute-start | bytes 1622024 | tf_op jit(solution)/shard_map/ppermute | solution.py:893
  15.7 15.9 %collective-permute-done.1.refs_2_ = bf16[352,768]{1,0:T(8,128)(2,1)S(1)} collective-permute-done((bf16[352,768]{1,0:T(8,128)(2,1)S(1)}, bf16[352,768]{1,0:T(8,128)(2,1)S(1)}, u32[]{:S(2)}, u32[]{:S(2)}) %collective-permute-start.1) | collective-permute-done | bytes 540704 | tf_op jit(solution)/shard_map/ppermute | solution.py:893
  35.6 3.5 %copy.40 = bf16[8,64,2,768]{3,0,1,2:T(8,128)(2,1)} copy(bf16[8,64,2,768]{3,2,1,0:T(2,128)(2,1)} %bitcast.87) | data formatting | bytes 3145728 | tf_op jit(solution)/shard_map/reshape | solution.py:1042
  48.2 9.4 %shard_map.276 = (bf16[1024,768]{1,0:T(8,128)(2,1)}, f32[1024,1152]{1,0:T(8,128)}, f32[1024,768]{1,0:T(8,128)}, f32[1024,768]{1,0:T(8,128)S(1)}, f32[1024,384]{1...) custom-call(bf16[1024,768]{1,0:T(8,128)(2,1)} %bitcast.81, f32[1,768]{1,0:T(1,128)S(1)} %broadcast_in_dim.35.gain, ...), custom_call_target="tpu_custom_call" | custom-call | flops 1 | bytes 1 | tf_op jit(solution)/shard_map/pallas_call | solution.py:47
  57.7 11.0 %all-gather = f32[16,8,384]{2,1,0:T(8,128)S(1)} all-gather(f32[2,8,384]{2,1,0:T(8,128)S(1)} %get-tuple-element.91), channel_id=2, replica_groups=mesh['dp'=4,'mp'=8] {'mp'}, dimensions={0}, use_global_device_ids=true | all-gather | bytes 221184 | tf_op jit(solution)/shard_map/all_gather | solution.py:1096
  69.2 9.1 %shard_map.277 = (f32[1024,768]{1,0:T(8,128)}, f32[2,2,8,384]{3,2,1,0:T(8,128)S(1)}, bf16[1024,768]{1,0:T(8,128)(2,1)}, f32[1024,768]{1,0:T(8,128)}, f32[1024,768]{1,0:T(8,128)}, /*index=5*/bf16[1024,768]{1,0:T(8,128)(2,1)S(1)}) custom-call(s32[1]{0:T(128)} %bitcast.1.me, f32[2,8]{1,0:T(2,128)S(1)} %compare_convert_fusion.1.keep, ...), custom_call_target="tpu_custom_call" | custom-call | flops 1 | bytes 1 | tf_op jit(solution)/shard_map/pallas_call | solution.py:47
  80.8 20.4 %shard_map.278 = (bf16[1024,1536]{1,0:T(8,128)(2,1)}, bf16[1024,3072]{1,0:T(8,128)(2,1)S(1)}, bf16[8,576,768]{2,1,0:T(8,128)(2,1)}) custom-call(bf16[1024,768]{1,0:T(8,128)(2,1)S(1)} %copy-done.7, bf16[1024,768]{1,0:T(8,128)(2,1)} %bitcast.84, bf16[8,3,192,768]{3,2,1,0:T(8,128)(2,1)} %bitcast.78), custom_call_target="tpu_custom_call" | custom-call | flops 1 | bytes 1 | tf_op jit(solution)/shard_map/pallas_call | solution.py:47
  101.3 2.6 copy-done.1
  104.1 2.8 %copy-done.2 = bf16[1024,3072]{1,0:T(8,128)(2,1)S(1)} copy-done((bf16[1024,3072]{1,0:T(8,128)(2,1)S(1)}, bf16[1024,3072]{1,0:T(8,128)(2,1)}, u32[]{:S(2)}) %copy-start.2) | copy-done | bytes 6291480
  106.9 23.2 %shard_map.279 = (f32[1024,768]{1,0:T(8,128)}, bf16[1024,768]{1,0:T(8,128)(2,1)}, f32[1024,768]{1,0:T(8,128)S(1)}, f32[2,3,8,384]{3,2,1,0:T(8,128)}, f32[2,8,384...) custom-call(s32[1]{0:T(128)} %bitcast.2.core, ...), custom_call_target="tpu_custom_call" | custom-call | flops 1 | bytes 1 | tf_op jit(solution)/shard_map/pallas_call | solution.py:47
  130.5 10.0 %all-gather.2 = f32[16,8,384]{2,1,0:T(8,128)S(1)} all-gather(f32[2,8,384]{2,1,0:T(8,128)} %get-tuple-element.105), channel_id=4, replica_groups=mesh['dp'=4,'mp'=8] {'mp'}, dimensions={0}, use_global_device_ids=true | all-gather | bytes 221184 | tf_op jit(solution)/shard_map/all_gather | solution.py:1150
  146.8 10.1 %shard_map.281 = (bf16[1024,1152]{1,0:T(8,128)(2,1)S(1)}, f32[2,2,8,384]{3,2,1,0:T(8,128)S(1)}, bf16[4,144,768]{2,1,0:T(8,128)(2,1)}, bf16[4,144,768]{2,1,0:T(8,128)(2,1)}) custom-call(s32[1]{0:T(128)} %bitcast.1.me, s32[1]{0:T(128)} %bitcast.2.core, f32[2,8]{1,0:T(2,128)S(1)} %compare_convert_fusion.1.keep, f32[8,2,8,384]{3,2,1,0:T(8,128)S(1)} %bitcast.76, ...), custom_call_target="tpu_custom_call" | custom-call | flops 1 | bytes 1 | tf_op jit(solution)/shard_map/pallas_call | solution.py:47
  158.3 4.8 %collective-permute-done.10 = bf16[192,768]{1,0:T(8,128)(2,1)} collective-permute-done((bf16[192,768]{1,0:T(8,128)(2,1)S(1)}, bf16[192,768]{1,0:T(8,128)(2,1)}, u32[]{:S(2)}, u32[]{:S(2)}) %collective-permute-start.10) | collective-permute-done | bytes 294944 | tf_op jit(solution)/shard_map/ppermute | solution.py:893
  167.0 6.8 %shard_map.282 = bf16[1024,768]{1,0:T(8,128)(2,1)S(1)} custom-call(bf16[1024,1536]{1,0:T(8,128)(2,1)} %get-tuple-element.129.refs_0_, bf16[8,3,192,768]{3,2,1,0:T(8,128)(2,1)} %bitcast.80, f32[1024,768]{1,0:T(8,128)} %get-tuple-element.130.refs_2_), custom_call_target="tpu_custom_call" | custom-call | flops 1 | bytes 1 | tf_op jit(solution)/shard_map/pallas_call | solution.py:47
  174.5 7.9 %shard_map.284 = (bf16[1024,768]{1,0:T(8,128)(2,1)S(1)}, f32[8,768]{1,0:T(8,128)S(1)}) custom-call(bf16[1024,1152]{1,0:T(8,128)(2,1)S(1)} %copy-done.4, bf16[1024,768]{1,0:T(8,128)(2,1)} %get-tuple-element.141.d_outgate, bf16[2688,768]{1,0:T(8,128)(2,1)} %bitcast.73, bf16[1024,768]{1,0:T(8,128)(2,1)} %bitcast.83, f32[1024,768]{1,0:T(8,128)} %get-tuple-element.142.d_mid, ...), custom_call_target="tpu_custom_call" | custom-call | flops 1 | bytes 1 | tf_op jit(solution)/shard_map/pallas_call | solution.py:47
  186.1 2.8 %copy.44 = bf16[8,64,2,768]{3,2,1,0:T(2,128)(2,1)} copy(bf16[8,64,2,768]{3,0,1,2:T(8,128)(2,1)S(1)} %bitcast.74) | data formatting | bytes 3145728 | tf_op jit(solution)/shard_map/transpose | solution.py:1046
  188.9 2.8 %copy.43 = bf16[8,64,2,768]{3,2,1,0:T(2,128)(2,1)} copy(bf16[8,64,2,768]{3,0,1,2:T(8,128)(2,1)S(1)} %bitcast.75) | data formatting | bytes 3145728 | tf_op jit(solution)/shard_map/transpose | solution.py:1046
  191.7 4.1 %collective-permute-done.14 = bf16[144,768]{1,0:T(8,128)(2,1)S(1)} collective-permute-done((bf16[144,768]{1,0:T(8,128)(2,1)S(1)}, bf16[144,768]{1,0:T(8,128)(2,1)S(1)}, u32[]{:S(2)}, u32[]{:S(2)}) %collective-permute-start.14) | collective-permute-done | bytes 221216 | tf_op jit(solution)/shard_map/ppermute | solution.py:893
  199.2 3.2 %collective-permute-done.19 = f32[8,768]{1,0:T(8,128)S(1)} collective-permute-done((f32[8,768]{1,0:T(8,128)S(1)}, f32[8,768]{1,0:T(8,128)S(1)}, u32[]{:S(2)}, u32[]{:S(2)}) %collective-permute-start.19) | collective-permute-done | bytes 24608 | tf_op jit(solution)/shard_map/ppermute | solution.py:893
  203.3 3.0 %collective-permute-done.20 = f32[8,768]{1,0:T(8,128)S(1)} collective-permute-done((f32[8,768]{1,0:T(8,128)S(1)}, f32[8,768]{1,0:T(8,128)S(1)}, u32[]{:S(2)}, u32[]{:S(2)}) %collective-permute-start.20) | collective-permute-done | bytes 24608 | tf_op jit(solution)/shard_map/ppermute | solution.py:893
  208.3 2.8 %collective-permute-done.24 = bf16[192,768]{1,0:T(8,128)(2,1)S(1)} collective-permute-done((bf16[192,768]{1,0:T(8,128)(2,1)S(1)}, bf16[192,768]{1,0:T(8,128)(2,1)S(1)}, u32[]{:S(2)}, u32[]{:S(2)}) %collective-permute-start.24) | collective-permute-done | bytes 294944 | tf_op jit(solution)/shard_map/ppermute | solution.py:893
  212.6 2.9 %collective-permute-start.23 = (bf16[144,768]{1,0:T(8,128)(2,1)S(1)}, bf16[144,768]{1,0:T(8,128)(2,1)S(1)}, u32[]{:S(2)}, u32[]{:S(2)}) collective-permute-start(bf16[144,768]{1,0:T(8,128)(2,1)S(1)} %add_convert_fusion.3), channel_id=1, source_target_pairs={{0,16},{8,24},{16,0},{24,8},{1,17},{9,25},{17,1},{25,9},{2,18},{10... | collective-permute-start | bytes 663560 | tf_op jit(solution)/shard_map/ppermute | solution.py:893
  219.5 4.9 %collective-permute-done.23 = bf16[144,768]{1,0:T(8,128)(2,1)S(1)} collective-permute-done((bf16[144,768]{1,0:T(8,128)(2,1)S(1)}, bf16[144,768]{1,0:T(8,128)(2,1)S(1)}, u32[]{:S(2)}, u32[]{:S(2)}) %collective-permute-start.23) | collective-permute-done | bytes 221216 | tf_op jit(solution)/shard_map/ppermute | solution.py:893
  225.8 39.4 %all-reduce.3.cloned.1.call-done = bf16[576,768]{1,0:T(8,128)(2,1)} async-done(((bf16[576,768]{1,0:T(8,128)(2,1)}), bf16[576,768]{1,0:T(8,128)(2,1)}) %all-reduce.3.cloned.1.call-update) | async-done | bytes 884752 | tf_op jit(solution)/shard_map/psum | solution.py:1124
  (173 shorter events, 54.1 us)
Async XLA Ops:
  7.3 72.2 %all-gather.5.cloned.1.call-start = ((), (), s32[]{:S(2)}) async-start(), calls=%async_computation.3 | async-start | bytes 7962624 | tf_op jit(solution)/shard_map/all_gather | solution.py:1077
  9.6 208.0 %reduce-scatter.2.cloned.1.call-start = ((), (), s32[]{:S(2)}) async-start(), calls=%async_computation.1 | async-start | bytes 7962624 | tf_op jit(solution)/shard_map/reduce_scatter | solution.py:919
  11.2 20.4 %collective-permute-start.1 = (bf16[352,768]{1,0:T(8,128)(2,1)S(1)}, bf16[352,768]{1,0:T(8,128)(2,1)S(1)}, u32[]{:S(2)}, u32[]{:S(2)}) collective-permute-start(bf16[352,768]{1,0:T(8,128)(2,1)S(1)} %pad_maximum_fusion.1.refs_0_), channel_id=1, source_target_pairs={{0,2},{1,3},{2,0},{3,1},{4,6},{5,7},{6,4},{7,5},{8,10},{9,11},{10,... | collective-permute-start | bytes 1622024 | tf_op jit(solution)/shard_map/ppermute | solution.py:893
  14.2 21.0 %collective-permute-start.3 = (bf16[352,768]{1,0:T(8,128)(2,1)S(1)}, bf16[352,768]{1,0:T(8,128)(2,1)S(1)}, u32[]{:S(2)}, u32[]{:S(2)}) collective-permute-start(bf16[352,768]{1,0:T(8,128)(2,1)S(1)} %pad_maximum_fusion.1.refs_0_), channel_id=1, source_target_pairs={{0,4},{1,5},{2,6},{3,7},{4,0},{5,1},{6,2},{7,3},{8,12},{9,13},{10,... | collective-permute-start | bytes 1622024 | tf_op jit(solution)/shard_map/ppermute | solution.py:893
  31.6 11.6 %collective-permute-start.5 = (bf16[176,768]{1,0:T(8,128)(2,1)S(1)}, bf16[176,768]{1,0:T(8,128)(2,1)S(1)}, u32[]{:S(2)}, u32[]{:S(2)}) collective-permute-start(bf16[176,768]{1,0:T(8,128)(2,1)S(1)} %slice.90), channel_id=1, source_target_pairs={{0,4},{1,5},{2,6},{3,7},{4,0},{5,1},{6,2},{7,3},{8,12},{9,13},{10,... | collective-permute-start | bytes 811016 | tf_op jit(solution)/shard_map/ppermute | solution.py:893
  35.2 8.0 %collective-permute-start.6 = (bf16[176,768]{1,0:T(8,128)(2,1)S(1)}, bf16[176,768]{1,0:T(8,128)(2,1)S(1)}, u32[]{:S(2)}, u32[]{:S(2)}) collective-permute-start(bf16[176,768]{1,0:T(8,128)(2,1)S(1)} %slice.91), channel_id=1, source_target_pairs={{0,2},{1,3},{2,0},{3,1},{4,6},{5,7},{6,4},{7,5},{8,10},{9,11},{10,... | collective-permute-start | bytes 811016 | tf_op jit(solution)/shard_map/ppermute | solution.py:893
  35.6 8.1 %collective-permute-start = (bf16[352,768]{1,0:T(8,128)(2,1)S(1)}, bf16[352,768]{1,0:T(8,128)(2,1)S(1)}, u32[]{:S(2)}, u32[]{:S(2)}) collective-permute-start(bf16[352,768]{1,0:T(8,128)(2,1)S(1)} %pad_maximum_fusion.1.refs_0_), channel_id=1, source_target_pairs={{0,1},{1,0},{2,3},{3,2},{4,5},{5,4},{6,7},{7,6},{8,9},{9,8},{10,11... | collective-permute-start | bytes 1622024 | tf_op jit(solution)/shard_map/ppermute | solution.py:893
  103.9 161.4 %all-reduce.3.cloned.1.call-start = ((), (), s32[]{:S(2)}) async-start(), calls=%async_computation.2 | async-start | bytes 1769472 | tf_op jit(solution)/shard_map/psum | solution.py:1124
  130.1 10.4 %collective-permute-start.8 = (bf16[4,192,768]{2,1,0:T(8,128)(2,1)}, bf16[4,192,768]{2,1,0:T(8,128)(2,1)}, u32[]{:S(2)}, u32[]{:S(2)}) collective-permute-start(bf16[4,192,768]{2,1,0:T(8,128)(2,1)} %get-tuple-element.104), channel_id=1, source_target_pairs={{0,1},{1,0},{2,3},{3,2},{4,5},{5,4},{6,7},{7,6},{8,9},{9,8},{10,11... | collective-permute-start | bytes 3538952 | tf_op jit(solution)/shard_map/ppermute | solution.py:893
  143.3 19.9 %collective-permute-start.10 = (bf16[192,768]{1,0:T(8,128)(2,1)S(1)}, bf16[192,768]{1,0:T(8,128)(2,1)}, u32[]{:S(2)}, u32[]{:S(2)}) collective-permute-start(bf16[192,768]{1,0:T(8,128)(2,1)S(1)} %get-tuple-element.118), channel_id=1, source_target_pairs={{0,4},{1,5},{2,6},{3,7},{4,0},{5,1},{6,2},{7,3},{8,12},{9,13},{10,... | collective-permute-start | bytes 884744 | tf_op jit(solution)/shard_map/ppermute | solution.py:893
  144.0 19.1 %collective-permute-start.11 = (bf16[192,768]{1,0:T(8,128)(2,1)S(1)}, bf16[192,768]{1,0:T(8,128)(2,1)S(1)}, u32[]{:S(2)}, u32[]{:S(2)}) collective-permute-start(bf16[192,768]{1,0:T(8,128)(2,1)S(1)} %get-tuple-element.119), channel_id=1, source_target_pairs={{0,6},{1,7},{2,4},{3,5},{4,2},{5,3},{6,0},{7,1},{8,14},{9,15},{10,... | collective-permute-start | bytes 884744 | tf_op jit(solution)/shard_map/ppermute | solution.py:893
  145.5 17.6 %collective-permute-start.9 = (bf16[192,768]{1,0:T(8,128)(2,1)S(1)}, bf16[192,768]{1,0:T(8,128)(2,1)S(1)}, u32[]{:S(2)}, u32[]{:S(2)}) collective-permute-start(bf16[192,768]{1,0:T(8,128)(2,1)S(1)} %get-tuple-element.117), channel_id=1, source_target_pairs={{0,2},{1,3},{2,0},{3,1},{4,6},{5,7},{6,4},{7,5},{8,10},{9,11},{10,... | collective-permute-start | bytes 884744 | tf_op jit(solution)/shard_map/ppermute | solution.py:893
  163.9 9.8 %collective-permute-start.12 = (bf16[4,144,768]{2,1,0:T(8,128)(2,1)}, bf16[4,144,768]{2,1,0:T(8,128)(2,1)S(1)}, u32[]{:S(2)}, u32[]{:S(2)}) collective-permute-start(bf16[4,144,768]{2,1,0:T(8,128)(2,1)} %get-tuple-element.122), channel_id=1, source_target_pairs={{0,1},{1,0},{2,3},{3,2},{4,5},{5,4},{6,7},{7,6},{8,9},{9,8},{10,11... | collective-permute-start | bytes 2654216 | tf_op jit(solution)/shard_map/ppermute | solution.py:893
  165.4 17.0 %collective-permute-start.16 = (bf16[192,768]{1,0:T(8,128)(2,1)S(1)}, bf16[192,768]{1,0:T(8,128)(2,1)S(1)}, u32[]{:S(2)}, u32[]{:S(2)}) collective-permute-start(bf16[192,768]{1,0:T(8,128)(2,1)S(1)} %fusion.2), channel_id=1, source_target_pairs={{0,8},{8,0},{16,24},{24,16},{1,9},{9,1},{17,25},{25,17},{2,10},{10... | collective-permute-start | bytes 884744 | tf_op jit(solution)/shard_map/ppermute | solution.py:893
  182.4 9.2 %collective-permute-start.13 = (bf16[144,768]{1,0:T(8,128)(2,1)S(1)}, bf16[144,768]{1,0:T(8,128)(2,1)S(1)}, u32[]{:S(2)}, u32[]{:S(2)}) collective-permute-start(bf16[144,768]{1,0:T(8,128)(2,1)S(1)} %get-tuple-element.136), channel_id=1, source_target_pairs={{0,2},{1,3},{2,0},{3,1},{4,6},{5,7},{6,4},{7,5},{8,10},{9,11},{10,... | collective-permute-start | bytes 663560 | tf_op jit(solution)/shard_map/ppermute | solution.py:893
  183.7 12.1 %collective-permute-start.14 = (bf16[144,768]{1,0:T(8,128)(2,1)S(1)}, bf16[144,768]{1,0:T(8,128)(2,1)S(1)}, u32[]{:S(2)}, u32[]{:S(2)}) collective-permute-start(bf16[144,768]{1,0:T(8,128)(2,1)S(1)} %get-tuple-element.137), channel_id=1, source_target_pairs={{0,4},{1,5},{2,6},{3,7},{4,0},{5,1},{6,2},{7,3},{8,12},{9,13},{10,... | collective-permute-start | bytes 663560 | tf_op jit(solution)/shard_map/ppermute | solution.py:893
  183.9 11.9 %collective-permute-start.15 = (bf16[144,768]{1,0:T(8,128)(2,1)S(1)}, bf16[144,768]{1,0:T(8,128)(2,1)S(1)}, u32[]{:S(2)}, u32[]{:S(2)}) collective-permute-start(bf16[144,768]{1,0:T(8,128)(2,1)S(1)} %get-tuple-element.138), channel_id=1, source_target_pairs={{0,6},{1,7},{2,4},{3,5},{4,2},{5,3},{6,0},{7,1},{8,14},{9,15},{10,... | collective-permute-start | bytes 663560 | tf_op jit(solution)/shard_map/ppermute | solution.py:893
  186.1 5.6 %collective-permute-start.17 = (f32[8,768]{1,0:T(8,128)S(1)}, f32[8,768]{1,0:T(8,128)S(1)}, u32[]{:S(2)}, u32[]{:S(2)}) collective-permute-start(f32[8,768]{1,0:T(8,128)S(1)} %get-tuple-element.148), channel_id=1, source_target_pairs={{0,1},{1,0},{2,3},{3,2},{4,5},{5,4},{6,7},{7,6},{8,9},{9,8},{10,11... | collective-permute-start | bytes 73736 | tf_op jit(solution)/shard_map/ppermute | solution.py:893
  196.0 11.8 %collective-permute-start.18 = (bf16[144,768]{1,0:T(8,128)(2,1)S(1)}, bf16[144,768]{1,0:T(8,128)(2,1)S(1)}, u32[]{:S(2)}, u32[]{:S(2)}) collective-permute-start(bf16[144,768]{1,0:T(8,128)(2,1)S(1)} %fusion.5), channel_id=1, source_target_pairs={{0,8},{8,0},{16,24},{24,16},{1,9},{9,1},{17,25},{25,17},{2,10},{10... | collective-permute-start | bytes 663560 | tf_op jit(solution)/shard_map/ppermute | solution.py:893
  196.2 14.9 %collective-permute-start.24 = (bf16[192,768]{1,0:T(8,128)(2,1)S(1)}, bf16[192,768]{1,0:T(8,128)(2,1)S(1)}, u32[]{:S(2)}, u32[]{:S(2)}) collective-permute-start(bf16[192,768]{1,0:T(8,128)(2,1)S(1)} %add_convert_fusion.1), channel_id=1, source_target_pairs={{0,16},{8,24},{16,0},{24,8},{1,17},{9,25},{17,1},{25,9},{2,18},{10... | collective-permute-start | bytes 884744 | tf_op jit(solution)/shard_map/ppermute | solution.py:893
  198.6 3.8 %collective-permute-start.19 = (f32[8,768]{1,0:T(8,128)S(1)}, f32[8,768]{1,0:T(8,128)S(1)}, u32[]{:S(2)}, u32[]{:S(2)}) collective-permute-start(f32[8,768]{1,0:T(8,128)S(1)} %add.104), channel_id=1, source_target_pairs={{0,2},{1,3},{2,0},{3,1},{4,6},{5,7},{6,4},{7,5},{8,10},{9,11},{10,... | collective-permute-start | bytes 73736 | tf_op jit(solution)/shard_map/ppermute | solution.py:893
  207.8 3.9 %collective-permute-start.21 = (f32[8,768]{1,0:T(8,128)S(1)}, f32[8,768]{1,0:T(8,128)S(1)}, u32[]{:S(2)}, u32[]{:S(2)}) collective-permute-start(f32[8,768]{1,0:T(8,128)S(1)} %add.111), channel_id=1, source_target_pairs={{0,8},{8,0},{16,24},{24,16},{1,9},{9,1},{17,25},{25,17},{2,10},{10... | collective-permute-start | bytes 73736 | tf_op jit(solution)/shard_map/ppermute | solution.py:893
  211.7 5.3 %collective-permute-start.22 = (f32[8,768]{1,0:T(8,128)S(1)}, f32[8,768]{1,0:T(8,128)S(1)}, u32[]{:S(2)}, u32[]{:S(2)}) collective-permute-start(f32[8,768]{1,0:T(8,128)S(1)} %add.113), channel_id=1, source_target_pairs={{0,16},{8,24},{16,0},{24,8},{1,17},{9,25},{17,1},{25,9},{2,18},{10... | collective-permute-start | bytes 73736 | tf_op jit(solution)/shard_map/ppermute | solution.py:893
  212.6 11.8 %collective-permute-start.23 = (bf16[144,768]{1,0:T(8,128)(2,1)S(1)}, bf16[144,768]{1,0:T(8,128)(2,1)S(1)}, u32[]{:S(2)}, u32[]{:S(2)}) collective-permute-start(bf16[144,768]{1,0:T(8,128)(2,1)S(1)} %add_convert_fusion.3), channel_id=1, source_target_pairs={{0,16},{8,24},{16,0},{24,8},{1,17},{9,25},{17,1},{25,9},{2,18},{10... | collective-permute-start | bytes 663560 | tf_op jit(solution)/shard_map/ppermute | solution.py:893
  (38 other events, 220.3 us)
Sparse Core Ops, SparseCore 0:
  10.0 60.7 all-gather.4
  104.0 77.4 reduce-scatter.1
  217.8 47.4 all-reduce.2

commit v3 on v2

--- a/solution.py
+++ b/solution.py
@@ -20,7 +20,7 @@
         self.value = value
 
 
-def kernel_call(body, grid, in_specs, out_specs, out_shape, scratch=(), vmem=32):
+def kernel_call(body, grid, in_specs, out_specs, out_shape, scratch=(), vmem=32, free=()):
     def space(shape):
         if isinstance(shape, Near):
             return pltpu.VMEM(shape.value.shape, shape.value.dtype)
@@ -44,7 +44,9 @@
         cost_estimate=pl.CostEstimate(flops=1, bytes_accessed=1, transcendentals=0),
         compiler_params=pltpu.CompilerParams(vmem_limit_bytes=vmem * MIB),
     )
-    return lambda *args: call(*map(placed, args))
+    return lambda *args: call(
+        *(arg if at in free else placed(arg) for at, arg in enumerate(args))
+    )
 
 
 def shaped(shape, dtype=F32):
@@ -116,7 +118,7 @@
 
 
 def chain_chunks(order, turning, angles, prod, end_re, end_im, chain, totals):
-    cos_chunk, sin_chunk = angles[2:3, :], angles[3:4, :]
+    cos_chunk, sin_chunk = angles[CHUNK : CHUNK + 1, :], angles[CHUNK + 1 : CHUNK + 2, :]
     zero = jnp.zeros_like(prod[0:1])
     run, run_re, run_im = zero + 1.0, zero, zero
     for s in order:
@@ -133,9 +135,60 @@
     totals[0, 2:3, :] = run_im
 
 
-def project_body(
-    steps, chans, tokens, gain, w, bound, angles, normed, pre, pre_out, local, decays, prefix, totals, carry
-):
+BOUND, PHASE, ONE, CHUNK, DEVICE, GAIN = 0, 1, 2, 4, 6, 8
+
+
+def channel_rows(logits, phase, out_gain):
+    return jnp.concatenate([logits, phase[None], out_gain], axis=0)
+
+
+def make_tables(rows, layer, steps, rows_dev, tables, lags):
+    layers = rows.shape[0] - 3
+    logits = rows[:layers]
+    phase = rows[layers : layers + 1]
+    grown = jnp.exp(logits - jnp.max(logits, axis=0, keepdims=True))
+    below = lax.broadcasted_iota(jnp.int32, grown.shape, 0) < layer
+    bound = jnp.sum(jnp.where(below, grown, 0.0), axis=0, keepdims=True)
+    tables[BOUND : BOUND + 1, :] = bound / jnp.sum(grown, axis=0, keepdims=True)
+    tables[PHASE : PHASE + 1, :] = phase
+    for at, span in ((ONE, 1), (CHUNK, steps), (DEVICE, rows_dev)):
+        tables[at : at + 1, :] = jnp.cos(phase * span)
+        tables[at + 1 : at + 2, :] = jnp.sin(phase * span)
+    tables[GAIN : GAIN + 2, :] = rows[layers + 1 :]
+    count, chans = lags.shape[0], phase.shape[1]
+    turns = phase * lax.broadcasted_iota(jnp.int32, (count, chans), 0).astype(F32)
+    lags[:, 0:chans] = jnp.cos(turns)
+    lags[:, chans:] = jnp.sin(turns)
+
+
+def gathered_weights(chans, kinds, me, pieces, proj, w_out):
+    size = chans // len(pieces)
+    spare = pieces[0].shape[0] - 7 * size
+    total = jnp.zeros((spare, chans), F32)
+    column = lax.broadcasted_iota(jnp.int32, (128, chans), 1)
+    row = lax.broadcasted_iota(jnp.int32, (128, chans), 0)
+    for b, piece in enumerate(pieces):
+        d = me[0] ^ b
+        for k in range(5):
+            proj[k, d] = piece[k * size : (k + 1) * size, :]
+        for k in range(2):
+            w_out[k, d] = piece[(5 + k) * size : (6 + k) * size, :]
+        here = jnp.logical_and(column == d * size + row, row < size)
+        total += nn(piece[7 * size :, 0:128], here.astype(F32).astype(BF16))
+    return total[0:kinds] + total[kinds : 2 * kinds] + total[2 * kinds : 3 * kinds]
+
+
+def project_body(steps, chans, count, kinds, per_dev, me, layer, tokens, gain, *refs):
+    given, refs = refs[: max(count, 2)], refs[max(count, 2) :]
+    normed, pre, pre_out, local, decays, prefix, totals, tables, lags, *made, carry = refs
+    chunk = per_dev // CHUNKS
+
+    @pl.when(first_step())
+    def _():
+        rows = gathered_weights(chans, kinds, me, given, *made) if count else given[1][...]
+        make_tables(rows, layer[0], chunk, per_dev, tables, lags)
+
+    w = made[0][...].reshape(5 * chans, made[0].shape[-1]) if count else given[0][...]
     t = pl.program_id(1)
 
     @pl.when(t == 0)
@@ -146,16 +199,16 @@
     values = tokens[...].astype(F32)
     unit = (values * rms_rows(values) * gain[...]).astype(BF16)
     normed[...] = unit
-    low = bound[0:1, :]
-    scan = nt(unit, w[4 * chans : 7 * chans, :])
-    pre[...] = scan
+    low = tables[BOUND : BOUND + 1, :]
+    scan = nt(unit, w[2 * chans : 5 * chans])
+    pre[...] = scan.astype(BF16)
     decay = low + (1.0 - low) * sigmoid(scan[:, 2 * chans :])
     decays[...] = decay
     in_re, in_im = scan[:, 0:chans], scan[:, chans : 2 * chans]
     local[:, 0:chans] = (1.0 - decay) * (in_re * sigmoid(in_re))
     local[:, chans:] = (1.0 - decay) * (in_im * sigmoid(in_im))
-    pre_out[...] = nt(unit, w[2 * chans : 4 * chans, :])
-    cos_one, sin_one = angles[0:1, :], angles[1:2, :]
+    pre_out[...] = nt(unit, w[0 : 2 * chans]).astype(BF16)
+    cos_one, sin_one = tables[ONE : ONE + 1, :], tables[ONE + 1 : ONE + 2, :]
 
     def step(j, state):
         state_re, state_im, prod = state
@@ -175,19 +228,28 @@
 
     @pl.when(t == pl.num_programs(1) - 1)
     def _():
-        chain_chunks(range(CHUNKS), turn, angles, prod, end_re, end_im, prefix, totals)
-
-
-def project(tokens, gain, w, bound, angles, groups, chans):
+        chain_chunks(range(CHUNKS), turn, tables, prod, end_re, end_im, prefix, totals)
+
+
+def project(me, layer, tokens, gain, pieces, kinds, w_proj, rows_all, groups, chans):
     rows, width = tokens.shape
     per = rows // groups
     tile = min(TILE, per)
     tiles = per // tile
     rowed = functools.partial(ahead, tiles, tile)
+    made = [(5, 8, chans // 8, width), (2, 8, chans // 8, width)] if pieces else []
+    given = pieces if pieces else [w_proj, rows_all]
+    lags = (per // CHUNKS + 8, 2 * chans)
     return kernel_call(
-        functools.partial(project_body, tile // CHUNKS, chans),
+        functools.partial(project_body, tile // CHUNKS, chans, len(pieces), kinds, per),
         (groups, tiles),
-        [rowed(width), whole((1, width)), whole(w.shape), whole((1, chans)), whole(angles.shape)],
+        [
+            SMEM_SPEC,
+            SMEM_SPEC,
+            rowed(width),
+            whole((1, width)),
+            *(whole(value.shape) for value in given),
+        ],
         [
             rowed(width),
             rowed(3 * chans),
@@ -196,18 +258,26 @@
             rowed(chans),
             per_group((1, 3, CHUNKS, chans)),
             per_group((1, CHUNKS, chans)),
+            kept((16, chans)),
+            kept(lags),
+            *map(kept, made),
         ],
         [
             shaped((rows, width), BF16),
-            shaped((rows, 3 * chans)),
-            shaped((rows, 2 * chans)),
+            shaped((rows, 3 * chans), BF16),
+            shaped((rows, 2 * chans), BF16),
             Near(shaped((rows, 2 * chans))),
             shaped((rows, chans)),
             shaped((groups, 3, CHUNKS, chans)),
             shaped((groups, CHUNKS, chans)),
+            shaped((16, chans)),
+            shaped(lags),
+            *(shaped(shape, BF16) for shape in made),
         ],
         [pltpu.VMEM((3, CHUNKS, chans), F32)],
-    )(tokens, gain, w, bound, angles)
+        vmem=36,
+        free=range(4, 4 + len(pieces)),
+    )(me, layer, tokens, gain, *given)
 
 
 def mix_body(
@@ -230,16 +300,16 @@
     states,
     entering,
     gated,
-    mix_out,
     mid,
     ffn_normed,
+    full,
     carry,
 ):
     g, t = pl.program_id(0), pl.program_id(1)
 
     @pl.when(t == 0)
     def _():
-        cos_dev, sin_dev = angles[4:5, :], angles[5:6, :]
+        cos_dev, sin_dev = angles[DEVICE : DEVICE + 1, :], angles[DEVICE + 1 : DEVICE + 2, :]
         state_re = jnp.zeros((1, chans), F32)
         state_im = jnp.zeros((1, chans), F32)
         for d in range(blocks):
@@ -251,7 +321,7 @@
             state_im = jnp.where(earlier, decay * turned_im + gathered[d, 0, 2:3, :], state_im)
         kept_one = keep[g, me[0]]
         state_re, state_im = kept_one * state_re, kept_one * state_im
-        cos_chunk, sin_chunk = angles[2:3, :], angles[3:4, :]
+        cos_chunk, sin_chunk = angles[CHUNK : CHUNK + 1, :], angles[CHUNK + 1 : CHUNK + 2, :]
         for s in range(CHUNKS):
             run = prefix[0, 0, s : s + 1, :]
             entering[0, 0, s : s + 1, :] = run * state_re + prefix[0, 1, s : s + 1, :]
@@ -264,21 +334,20 @@
     def step(j, prod):
         rows = step_rows(j)
         prod = prod * decays[rows, :]
-        lag = pl.ds(t * steps + j, 1)
+        lag = pl.ds(t * steps + j + 1, 1)
         turned_re, turned_im = turn(table[lag, 0:chans], table[lag, chans:], enter_re, enter_im)
-        states[rows, 0:chans] = local[rows, 0:chans] + prod * turned_re
-        states[rows, chans:] = local[rows, chans:] + prod * turned_im
+        full[rows, 0:chans] = local[rows, 0:chans] + prod * turned_re
+        full[rows, chans:] = local[rows, chans:] + prod * turned_im
         return prod
 
     carry[...] = lax.fori_loop(0, steps, step, carry[...], unroll=8)
-    state = states[...]
+    state = full[...]
+    states[...] = state.astype(BF16)
     inv_rms = rms_rows(state)
-    gate = pre_out[...]
+    gate = pre_out[...].astype(F32)
     gate_in = (state * out_gain[...] * (gate * sigmoid(gate))).astype(BF16)
     gated[...] = gate_in
-    mixed = nn(gate_in, w_out[...])
-    mix_out[...] = mixed
-    stream = tokens[...].astype(F32) + inv_rms * mixed
+    stream = tokens[...].astype(F32) + inv_rms * nn(gate_in, w_out[...])
     mid[...] = stream
     ffn_normed[...] = (stream * rms_rows(stream) * ffn_gain[...]).astype(BF16)
 
@@ -316,17 +385,15 @@
             rowed(2 * chans),
             rowed(width),
             rowed(width),
-            rowed(width),
-        ],
-        [
-            shaped((rows, 2 * chans)),
+        ],
+        [
+            shaped((rows, 2 * chans), BF16),
             shaped((groups, 2, CHUNKS, chans)),
             shaped((rows, 2 * chans), BF16),
             shaped((rows, width)),
-            shaped((rows, width)),
-            Near(shaped((rows, width), BF16)),
-        ],
-        [pltpu.VMEM((CHUNKS, chans), F32)],
+            shaped((rows, width), BF16),
+        ],
+        [pltpu.VMEM((tile, 2 * chans), F32), pltpu.VMEM((CHUNKS, chans), F32)],
     )(me, keep, gathered, Near(local), decays, prefix, angles, table, pre_out, tokens, w, out_gain, ffn_gain)
 
 
@@ -340,7 +407,7 @@
             other[chip, rows, :] = jnp.where(first, odd, even)
 
 
-def swiglu_body(unit, tile, x, up, w, act, d_pre, grads):
+def swiglu_body(unit, tile, x, up, w, act, d_pre, grads, w_out):
     devices = w.shape[0]
 
     def every(part):
@@ -349,6 +416,7 @@
     span = devices * unit
     w_pre = jnp.concatenate([every(0), every(1)], axis=0)
     w_down = every(2)
+    w_out[...] = w_pre
     for start in range(0, x.shape[0], tile):
         rows = slice(start, start + tile)
         pre = nt(x[rows, :], w_pre)
@@ -392,22 +460,25 @@
             pl.BlockSpec((rows, span), lambda q: (0, q)),
             pl.BlockSpec((rows, 2 * span), lambda q: (0, q)),
             pl.BlockSpec((devices, 3 * unit, width), lambda q: (q, 0, 0)),
+            pl.BlockSpec((2 * span, width), lambda q: (q, 0)),
         ],
         [
             shaped((rows, blocks * unit), BF16),
-            Near(shaped((rows, 2 * blocks * unit), BF16)),
+            shaped((rows, 2 * blocks * unit), BF16),
             shaped((blocks, 3 * unit, width), BF16),
-        ],
-    )(Near(x), up, w)
-
-
-def finish_grads(core, acc, kinds, chans, unit, same, other):
+            shaped((2 * blocks * unit, width), BF16),
+        ],
+    )(x, up, w)
+
+
+def finish_grads(core, grads, kinds, chans, unit, same, other):
+    grads = [grad.astype(BF16) for grad in grads]
     if unit % 16:
-        same[...] = acc[...].astype(BF16)
+        same[...] = jnp.concatenate(grads, axis=0)
         other[...] = jnp.zeros_like(other)
         return
-    grads = [acc[k * chans : (k + 1) * chans, :].astype(BF16) for k in range(kinds)]
-    split_by_core(core[0] == 0, grads, chans, unit, same, other)
+    each = [grad[at : at + chans] for grad in grads for at in range(0, grad.shape[0], chans)]
+    split_by_core(core[0] == 0, each, chans, unit, same, other)
 
 
 def grads_shapes(kinds, chans, unit, width):
@@ -426,72 +497,74 @@
     )
 
 
-def mix_back_body(steps, chans, unit_chans, parts, core, *refs):
-    d_pres, refs = refs[:parts], refs[parts:]
-    (
-        w_ffn,
-        mid,
-        upstream,
-        mix_out,
-        states,
-        pre_out,
-        gated,
-        normed,
-        decays,
-        w_out,
-        out_gain,
-        ffn_gain,
-        angles,
-        d_mid,
-        d_outgate,
-        local,
-        suffix,
-        totals,
-        same,
-        other,
-        sums,
-        acc,
-        w_pre,
-        carry,
-    ) = refs
-    blocks, _, units, _ = w_ffn.shape
-    unit = units // parts
-    devices = units_at_once(blocks, unit)
+def mix_back_body(
+    steps,
+    chans,
+    unit_chans,
+    core,
+    d_pre,
+    w_pre,
+    mid,
+    upstream,
+    tokens,
+    states,
+    pre_out,
+    gated,
+    normed,
+    decays,
+    w_out,
+    out_gain,
+    ffn_gain,
+    angles,
+    d_mid,
+    d_outgate,
+    local,
+    suffix,
+    totals,
+    same,
+    other,
+    sums,
+    d_mixes,
+    d_gates,
+    carry,
+    gated_here,
+    normed_here,
+    arrivals,
+):
+    rows_here = steps * CHUNKS
+    at = pl.program_id(0) * pl.num_programs(1) + pl.num_programs(1) - 1 - pl.program_id(1)
+    here = pl.ds(pl.multiple_of(at * rows_here, rows_here), rows_here)
+
+    fetches = [
+        pltpu.make_async_copy(gated, gated_here, arrivals.at[0]),
+        pltpu.make_async_copy(normed, normed_here, arrivals.at[1]),
+    ]
 
     @pl.when(first_step())
     def _():
-        acc[...] = jnp.zeros_like(acc)
         sums[...] = jnp.zeros_like(sums)
-        at = 0
-        for part in range(parts):
-            for q in range(0, blocks, devices):
-                for kind in (0, 1):
-                    for dev in range(q, q + devices):
-                        w_pre[at : at + unit, :] = w_ffn[dev, kind, part * unit : (part + 1) * unit, :]
-                        at += unit
+        for fetch in fetches:
+            fetch.start()
 
     @pl.when(pl.program_id(1) == 0)
     def _():
         carry[0:2] = jnp.zeros((2,) + carry.shape[1:], F32)
         carry[2] = jnp.ones(carry.shape[1:], F32)
 
-    span = 2 * units * blocks // parts
-    d_norm = nn(d_pres[0][...], w_pre[0:span, :])
-    for part in range(1, parts):
-        d_norm += nn(d_pres[part][...], w_pre[part * span : (part + 1) * span, :])
+    d_norm = nn(d_pre[...], w_pre[...])
     stream = mid[...]
     inv_mid = rms_rows(stream)
     unit_mid = stream * inv_mid
     sums[0:1, :] += jnp.sum(d_norm * unit_mid, axis=0, keepdims=True)
     d_stream = upstream[...].astype(F32) + rms_pull(unit_mid, inv_mid, ffn_gain[...], d_norm)
-    d_mid[...] = d_stream
-    state = states[...]
+    d_mid[...] = d_stream.astype(BF16)
+    state = states[...].astype(F32)
     inv_rms = rms_rows(state)
     d_mix = (inv_rms * d_stream).astype(BF16)
-    d_rms = jnp.sum(d_stream * mix_out[...], axis=-1, keepdims=True)
-    d_square = (-0.5 / chans) * inv_rms * inv_rms * inv_rms * d_rms
+    mixed = stream - tokens[...].astype(F32)
+    d_square = (-0.5 / chans) * inv_rms * inv_rms * jnp.sum(d_stream * mixed, axis=-1, keepdims=True)
     d_gated = nt(d_mix, w_out[...])
-    gate = pre_out[...]
+    gate = pre_out[...].astype(F32)
     sigma = sigmoid(gate)
     silu = gate * sigma
     gain = out_gain[...]
@@ -500,9 +573,9 @@
     sums[1:2, :] += jnp.sum(d_state_gate * silu, axis=0, keepdims=True)
     d_gate = (d_state_gate * gain * (sigma + silu * (1.0 - sigma))).astype(BF16)
     d_outgate[...] = d_gate
-    acc[0 : 2 * chans, :] += tn(gated[...], d_mix)
-    acc[2 * chans : 4 * chans, :] += tn(d_gate, normed[...])
-    cos_one, sin_one = angles[0:1, :], angles[1:2, :]
+    d_mixes[here, :] = d_mix
+    d_gates[here, :] = d_gate
+    cos_one, sin_one = angles[ONE : ONE + 1, :], angles[ONE + 1 : ONE + 2, :]
 
     def step(i, flow):
         flow_re, flow_im, prod = flow
@@ -526,17 +599,20 @@
 
     @pl.when(last_step())
     def _():
-        finish_grads(core, acc, 4, chans, unit_chans, same, other)
+        for fetch in fetches:
+            fetch.wait()
+        grads = [tn(gated_here[...], d_mixes[...]), tn(d_gates[...], normed_here[...])]
+        finish_grads(core, grads, 4, chans, unit_chans, same, other)
 
 
 def mix_back(
     core,
     unit_chans,
-    d_pres,
-    w_ffn,
+    d_pre,
+    w_pre,
     mid,
     upstream,
-    mix_out,
+    tokens,
     states,
     pre_out,
     gated,
@@ -553,23 +629,21 @@
     per = rows // groups
     tile = min(TILE, per)
     tiles = per // tile
-    blocks, _, units, _ = w_ffn.shape
-    parts = len(d_pres)
     rowed = functools.partial(behind, tiles, tile)
     return kernel_call(
-        functools.partial(mix_back_body, tile // CHUNKS, chans, unit_chans, parts),
+        functools.partial(mix_back_body, tile // CHUNKS, chans, unit_chans),
         (groups, tiles),
-        [SMEM_SPEC]
-        + [rowed(part.shape[1]) for part in d_pres]
-        + [
-            whole((blocks, 2, units, width)),
+        [
+            SMEM_SPEC,
+            rowed(d_pre.shape[1]),
+            whole(w_pre.shape),
             rowed(width),
             rowed(width),
             rowed(width),
             rowed(2 * chans),
             rowed(2 * chans),
-            rowed(2 * chans),
-            rowed(width),
+            pl.BlockSpec(memory_space=pl.ANY),
+            pl.BlockSpec(memory_space=pl.ANY),
             rowed(chans),
             whole((2 * chans, width)),
             whole((1, 2 * chans)),
@@ -586,7 +660,7 @@
             kept((8, width)),
         ],
         [
-            shaped((rows, width)),
+            shaped((rows, width), BF16),
             shaped((rows, 2 * chans), BF16),
             Near(shaped((rows, 2 * chans))),
             shaped((groups, 3, CHUNKS, chans)),
@@ -595,18 +669,21 @@
             shaped((8, width)),
         ],
         [
-            pltpu.VMEM((4 * chans, width), F32),
-            pltpu.VMEM((2 * blocks * units, width), BF16),
+            pltpu.VMEM((rows, width), BF16),
+            pltpu.VMEM((rows, 2 * chans), BF16),
             pltpu.VMEM((3, CHUNKS, chans), F32),
-        ],
-        vmem=46,
+            pltpu.VMEM((rows, 2 * chans), BF16),
+            pltpu.VMEM((rows, width), BF16),
+            pltpu.SemaphoreType.DMA((2,)),
+        ],
+        vmem=40,
     )(
         core,
-        *map(Near, d_pres),
-        w_ffn,
+        d_pre,
+        w_pre,
         mid,
         upstream,
-        mix_out,
+        tokens,
         states,
         pre_out,
         gated,
@@ -639,7 +716,6 @@
     states,
     before,
     entering,
-    bound,
     angles,
     table,
     normed,
@@ -649,20 +725,18 @@
     other,
     leaving,
     full,
-    acc,
+    d_pres,
     carry,
 ):
     g, t = pl.program_id(0), pl.program_id(1)
     tiles = pl.num_programs(1)
-
-    @pl.when(first_step())
-    def _():
-        acc[...] = jnp.zeros_like(acc)
+    rows_here = steps * CHUNKS
+    here = pl.ds(pl.multiple_of((g * tiles + tiles - 1 - t) * rows_here, rows_here), rows_here)
 
     @pl.when(t == 0)
     def _():
-        cos_chunk, sin_chunk = angles[2:3, :], angles[3:4, :]
-        cos_dev, sin_dev = angles[4:5, :], angles[5:6, :]
+        cos_chunk, sin_chunk = angles[CHUNK : CHUNK + 1, :], angles[CHUNK + 1 : CHUNK + 2, :]
+        cos_dev, sin_dev = angles[DEVICE : DEVICE + 1, :], angles[DEVICE + 1 : DEVICE + 2, :]
         flow_re = jnp.zeros((1, chans), F32)
         flow_im = jnp.zeros((1, chans), F32)
         for d in reversed(range(blocks)):
@@ -684,8 +758,8 @@
         carry[...] = jnp.ones_like(carry)
         sums[...] = jnp.zeros_like(sums)
 
-    low = bound[0:1, :]
-    cos_one, sin_one = angles[0:1, :], angles[1:2, :]
+    low = angles[BOUND : BOUND + 1, :]
+    cos_one, sin_one = angles[ONE : ONE + 1, :], angles[ONE + 1 : ONE + 2, :]
     leave_re, leave_im = leaving[0], leaving[1]
 
     def step(i, prod):
@@ -698,16 +772,17 @@
 
     carry[...] = lax.fori_loop(0, steps, step, carry[...], unroll=8)
     first_tile = t == tiles - 1
-    last_re = jnp.where(first_tile, entering[0, 0], before[:, 0:chans])
-    last_im = jnp.where(first_tile, entering[0, 1], before[:, chans:])
-    if steps > 1:
-        rows = slice(0, (steps - 1) * CHUNKS)
-        last_re = jnp.concatenate([last_re, states[rows, 0:chans]], axis=0)
-        last_im = jnp.concatenate([last_im, states[rows, chans:]], axis=0)
+    last = before[...].astype(F32)[CHUNKS:]
+    last_re = jnp.where(first_tile, entering[0, 0], last[:, 0:chans])
+    last_im = jnp.where(first_tile, entering[0, 1], last[:, chans:])
+    state = states[...].astype(F32)[: (steps - 1) * CHUNKS]
+    last_re = jnp.concatenate([last_re, state[:, 0:chans]], axis=0)
+    last_im = jnp.concatenate([last_im, state[:, chans:]], axis=0)
     grad_re, grad_im = full[:, 0:chans], full[:, chans:]
-    in_re, in_im = pre[:, 0:chans], pre[:, chans : 2 * chans]
+    scan = pre[...].astype(F32)
+    in_re, in_im = scan[:, 0:chans], scan[:, chans : 2 * chans]
     sigma_re, sigma_im = sigmoid(in_re), sigmoid(in_im)
-    sigma = sigmoid(pre[:, 2 * chans :])
+    sigma = sigmoid(scan[:, 2 * chans :])
     decay = decays[...]
     cross_re = grad_re * last_re + grad_im * last_im
     cross_im = grad_im * last_re - grad_re * last_im
@@ -718,16 +793,15 @@
     d_re = (grad_re * rest * silu_slope(in_re, sigma_re)).astype(BF16)
     d_im = (grad_im * rest * silu_slope(in_im, sigma_im)).astype(BF16)
     d_forget = (d_low * (1.0 - low) * sigma).astype(BF16)
-    d_pre[:, 0:chans] = d_re
-    d_pre[:, chans : 2 * chans] = d_im
-    d_pre[:, 2 * chans :] = d_forget
+    d_all = jnp.concatenate([d_re, d_im, d_forget], axis=1)
+    d_pre[...] = d_all
+    d_pres[here, :] = d_all
     sums[0, 0] += jnp.sum((decay * across).reshape(steps, CHUNKS, chans), axis=0)
     sums[0, 1] += jnp.sum(d_low.reshape(steps, CHUNKS, chans), axis=0)
-    acc[...] += tn(d_pre[...], normed[...])
 
     @pl.when(last_step())
     def _():
-        finish_grads(core, acc, 3, chans, unit_chans, same, other)
+        finish_grads(core, [tn(d_pres[...], normed[...])], 3, chans, unit_chans, same, other)
 
 
 def adjoint_finish(
@@ -742,7 +816,6 @@
     pre,
     states,
     entering,
-    bound,
     angles,
     table,
     normed,
@@ -758,7 +831,7 @@
     rowed = functools.partial(behind, tiles, tile)
 
     def one_before(g, t):
-        return (jnp.maximum((g * tiles + tiles - 1 - t) * steps - 1, 0), 0)
+        return (jnp.maximum((g * tiles + tiles - 1 - t) * (steps // 2) - 1, 0), 0)
 
     return kernel_call(
         functools.partial(adjoint_finish_body, steps, chans, blocks, unit_chans),
@@ -773,12 +846,11 @@
             per_group((1, 3, CHUNKS, chans)),
             rowed(3 * chans),
             rowed(2 * chans),
-            pl.BlockSpec((CHUNKS, 2 * chans), one_before),
+            pl.BlockSpec((2 * CHUNKS, 2 * chans), one_before),
             per_group((1, 2, CHUNKS, chans)),
-            whole((1, chans)),
             whole(angles.shape),
             whole(table.shape),
-            rowed(width),
+            whole((rows, width)),
         ],
         [
             rowed(3 * chans),
@@ -786,14 +858,14 @@
             *map(kept, grads_shapes(3, chans, unit_chans, width)),
         ],
         [
-            Near(shaped((rows, 3 * chans), BF16)),
+            shaped((rows, 3 * chans), BF16),
             shaped((groups, 2, CHUNKS, chans)),
             *(shaped(shape, BF16) for shape in grads_shapes(3, chans, unit_chans, width)),
         ],
         [
             pltpu.VMEM((2, CHUNKS, chans), F32),
             pltpu.VMEM((tile, 2 * chans), F32),
-            pltpu.VMEM((3 * chans, width), F32),
+            pltpu.VMEM((rows, 3 * chans), BF16),
             pltpu.VMEM((CHUNKS, chans), F32),
         ],
     )(
@@ -808,7 +880,6 @@
         states,
         states,
         entering,
-        bound,
         angles,
         table,
         normed,
@@ -823,13 +894,13 @@
         sums[3:4, 0:chans] = jnp.sum(scan[:, 0], axis=(0, 1))[None]
         sums[3:4, chans : 2 * chans] = jnp.sum(scan[:, 1], axis=(0, 1))[None]
 
-    d_normed = nn(d_scan[...], w[4 * chans : 7 * chans, :])
-    d_normed += nn(d_outgate[...], w[2 * chans : 4 * chans, :])
+    d_normed = nn(d_scan[...], w[2 * chans : 5 * chans, :])
+    d_normed += nn(d_outgate[...], w[0 : 2 * chans, :])
     values = tokens[...].astype(F32)
     inv = rms_rows(values)
     unit = values * inv
     sums[0:1, :] += jnp.sum(d_normed * unit, axis=0, keepdims=True)
-    grad_tokens[...] = (d_mid[...] + rms_pull(unit, inv, gain[...], d_normed)).astype(BF16)
+    grad_tokens[...] = (d_mid[...].astype(F32) + rms_pull(unit, inv, gain[...], d_normed)).astype(BF16)
 
 
 def tokens_back(d_scan, d_outgate, w, tokens, d_mid, gain, early, scan, groups, chans):
@@ -854,23 +925,16 @@
         [rowed(width), kept((8, width))],
         [Near(shaped((rows, width), BF16)), shaped((8, width))],
         vmem=20,
-    )(Near(d_scan), d_outgate, w, tokens, d_mid, gain, early, scan)
-
-
-def result_body(parts, *refs):
-    acts, (w_down, mid, result) = refs[:parts], refs[parts:]
-    blocks, _, units, _ = w_down.shape
-    unit = units // parts
-    total = mid[...]
-    for part, act in enumerate(acts):
-        rows = slice(part * unit, (part + 1) * unit)
-        total += nn(
-            act[...], jnp.concatenate([w_down[dev, 0, rows, :] for dev in range(blocks)], axis=0)
-        )
-    result[...] = total.astype(BF16)
-
-
-def block_result(acts, w_ffn, mid):
+    )(d_scan, d_outgate, w, tokens, d_mid, gain, early, scan)
+
+
+def result_body(act, w_down, mid, result):
+    blocks = w_down.shape[0]
+    down = jnp.concatenate([w_down[dev, 0] for dev in range(blocks)], axis=0)
+    result[...] = (mid[...] + nn(act[...], down)).astype(BF16)
+
+
+def block_result(act, w_ffn, mid):
     rows, width = mid.shape
     blocks, _, units, _ = w_ffn.shape
     tile = min(TILE, rows)
@@ -879,14 +943,13 @@
         return pl.BlockSpec((tile, wide), lambda i: (i, 0))
 
     return kernel_call(
-        functools.partial(result_body, len(acts)),
+        result_body,
         (rows // tile,),
-        [rowed(act.shape[1]) for act in acts]
-        + [whole((blocks, 1, units, width), (0, 2, 0, 0)), rowed(width)],
+        [rowed(act.shape[1]), whole((blocks, 1, units, width), (0, 2, 0, 0)), rowed(width)],
         rowed(width),
         Near(shaped((rows, width), BF16)),
         vmem=20,
-    )(*acts, w_ffn, mid)
+    )(act, w_ffn, mid)
 
 
 def swap(values, axis, bit, size):
@@ -901,18 +964,19 @@
     return lax.dynamic_index_in_dim(values, index, axis, keepdims=False)
 
 
-def gather_pieces(shard, size):
-    half = shard.shape[0] // 2
+def gather_pieces(shard, size, *others):
+    half = shard.shape[0] // 32 * 16
     near_x = swap(shard, "mp", 2, size)
     near_y = swap(shard, "mp", 4, size)
     core = swap(shard, "mp", 1, size)
+    near_x, near_y, *others = tied(near_x, near_y, *others)
     far_one = swap(near_x[:half], "mp", 4, size)
     far_two = swap(near_y[half:], "mp", 2, size)
     core_x = swap(near_x, "mp", 1, size)
     core_y = swap(near_y, "mp", 1, size)
     far = jnp.concatenate([far_one, far_two], axis=0)
     core_far = swap(far, "mp", 1, size)
-    return shard, core, near_x, core_x, near_y, core_y, far, core_far
+    return [shard, core, near_x, core_x, near_y, core_y, far, core_far], *others
 
 
 def reduce_mp(grads):
@@ -936,10 +1000,30 @@
     )(chip, same, got)
 
 
+def last_sums(finish, order, size, layers, flat, chip, same, got, early, early_got):
+    last = Reduction(same, None, chip, size, layers)
+    last.flying = [got]
+    flat = flat + swap(flat, "mp", 2 * order[0], size)
+    flat = last.to_chips(flat)
+    early, flat = tied(both(early, early_got), flat)
+    early_got = along_layers(2, early)
+    flat = flat + swap(flat, "mp", 2 * order[1], size)
+    late, early, early_got, flat = tied(last.share_here(), early, early_got, flat)
+    late_got = along_layers(1, late)
+    early = both(early, early_got)
+    early_got = along_layers(3, early)
+    one, two, three = (swap(flat, "dp", bit, layers) for bit in (1, 2, 3))
+    flat = (flat + one) + (two + three)
+    for number in (2, 3):
+        late = both(late, late_got)
+        late_got = along_layers(number, late)
+    return finish(flat, settled(late, late_got), settled(early, early_got))
+
+
 class Reduction:
     def __init__(self, same, other, chip, size, layers):
         self.same, self.chip, self.size, self.layers = same, chip, size, layers
-        self.flying = [swap(other, "mp", 1, size)]
+        self.flying = [] if other is None else [swap(other, "mp", 1, size)]
 
     def arrived(self, *others):
         count = len(self.flying)
@@ -958,42 +1042,20 @@
         mine = pick(self.same, at, 0), pick(self.got, at, 0)
         return joined(*mine, *self.flying).astype(BF16)
 
-    def to_layer(self, number, other):
-        if number == 1:
-            self.share = self.share_here()
-        else:
-            self.share = joined(self.share, *self.flying).astype(BF16)
-        self.share, other = tied(self.share, other)
-        self.flying = [swap(self.share, "dp", number, self.layers)]
-        return other
-
-    def total(self):
-        return joined(self.share, *self.flying).astype(BF16).astype(F32)
-
-
-def assemble_body(kinds, size, me, *refs):
-    out, extra = refs[-2:]
-    for b, ref in enumerate(refs[:-2]):
-        d = me[0] ^ b
-        for k in range(kinds):
-            out[k, d] = ref[k * size : (k + 1) * size, :]
-        extra[d] = ref[kinds * size :, :]
-
-
-def assemble(me, pieces, kinds, size):
-    rows, width = pieces[0].shape
-    vmem = VMEM_SPEC
-    return pl.pallas_call(
-        functools.partial(assemble_body, kinds, size),
-        in_specs=[SMEM_SPEC] + [vmem] * len(pieces),
-        out_specs=[vmem, vmem],
-        out_shape=[
-            jax.ShapeDtypeStruct((kinds, len(pieces), size, width), BF16),
-            jax.ShapeDtypeStruct((len(pieces), rows - kinds * size, width), BF16),
-        ],
-        cost_estimate=pl.CostEstimate(flops=1, bytes_accessed=1, transcendentals=0),
-        compiler_params=pltpu.CompilerParams(vmem_limit_bytes=16 * MIB),
-    )(me, *pieces)
+
+def along_layers(number, share):
+    pairs = {1: [(0, 1), (3, 2)], 2: [(1, 2), (2, 1)], 3: [(1, 0), (2, 3)]}[number]
+    return lax.ppermute(share, "dp", pairs)
+
+
+def both(share, got):
+    return joined(share, got).astype(BF16)
+
+
+def settled(share, got):
+    z = lax.axis_index("dp")
+    inner = jnp.logical_or(z == 1, z == 2)
+    return jnp.where(inner, share, got).astype(F32)
 
 
 def split_three(values):
@@ -1048,53 +1110,47 @@
         ).reshape(rows_dev, groups, width)
 
     me_one = me[None].astype(jnp.int32)
-    layer_mask = (jnp.arange(lower_logits.shape[0], dtype=jnp.int32) < layer_index[0]).astype(F32)
-    soft = jax.nn.softmax(lower_logits, axis=0)
-    bound_own = jnp.sum(soft * layer_mask[:, None], axis=0)
-    small = jnp.concatenate([bound_own[None], phase_angle[None], out_gain], axis=0)
+    rows_own = channel_rows(lower_logits, phase_angle, out_gain)
+    kinds = rows_own.shape[0]
+    by_hand = blocks == 8 and layers_z == 4 and chans_dev % 16 == 0
     mix_shard = jnp.concatenate(
         [
-            w_output,
             jnp.transpose(w_outgate, (1, 2, 0)),
             jnp.transpose(w_input, (1, 2, 0)),
             jnp.transpose(w_forget)[None],
+            w_output,
         ],
         axis=0,
-    ).reshape(7 * chans_dev, width)
-    if blocks == 8 and 4 * chans_dev <= width:
-        terms = split_three(small.reshape(1, -1)).reshape(3, 4 * chans_dev)
-        terms = jnp.pad(terms, ((0, 13), (0, width - 4 * chans_dev)))
-        pieces_w = gather_pieces(jnp.concatenate([mix_shard, terms], axis=0), blocks)
-        w_mix, extra = assemble(me_one, pieces_w, 7, chans_dev)
-        small = jnp.sum(extra[:, 0:3, 0 : 4 * chans_dev].astype(F32), axis=1)
-        small = small.reshape(blocks, 4, chans_dev)
+    )
+    ffn_parts = jnp.transpose(w_gate), jnp.transpose(w_up), w_down
+    tok, up_rows = to_rows(tokens), to_rows(upstream)
+    pieces_w, w_proj, rows_all = [], None, None
+    if by_hand:
+        terms = split_three(rows_own).reshape(3 * kinds, chans_dev)
+        spare = (3 * kinds + 15) // 16 * 16
+        terms = jnp.pad(terms, ((0, spare - 3 * kinds), (0, width - chans_dev)))
+        own = jnp.concatenate([mix_shard.reshape(7 * chans_dev, width), terms], axis=0)
+        own, *ffn_parts = tied(own, *ffn_parts)
+        pieces_w, tok, up_rows = gather_pieces(own, blocks, tok, up_rows)
     else:
-        w_mix = lax.all_gather(mix_shard.reshape(7, chans_dev, width), "mp", axis=0)
-        w_mix = jnp.transpose(w_mix, (1, 0, 2, 3))
-        small = lax.all_gather(small, "mp", axis=0)
-    w_mix = w_mix.reshape(7 * chans, width)
-    ffn_shard = jnp.concatenate([jnp.transpose(w_gate), jnp.transpose(w_up), w_down], axis=0)
-    w_ffn = lax.all_gather(ffn_shard, "mp", axis=0)
-
-    small = jnp.transpose(small, (1, 0, 2)).reshape(4, chans)
-    bound = small[0:1]
-    phase = small[1:2]
-    gain_row = small[2:4].reshape(1, 2 * chans)
-    spans = phase * jnp.array([[1.0], [steps], [rows_dev]], F32)
-    angles = jnp.stack([jnp.cos(spans), jnp.sin(spans)], axis=1).reshape(6, chans)
-    lags = phase * jnp.arange(steps + 1, dtype=F32)[:, None]
-    table = jnp.concatenate([jnp.cos(lags), jnp.sin(lags)], axis=1)
+        w_mix = lax.all_gather(mix_shard, "mp", axis=0)
+        w_mix = jnp.transpose(w_mix, (1, 0, 2, 3)).reshape(7 * chans, width)
+        w_proj, w_out = w_mix[: 5 * chans], w_mix[5 * chans :]
+        rows_all = lax.all_gather(rows_own, "mp", axis=0)
+        rows_all = jnp.transpose(rows_all, (1, 0, 2)).reshape(kinds, chans)
+    w_ffn = lax.all_gather(jnp.concatenate(ffn_parts, axis=0), "mp", axis=0)
     starts = jnp.arange(blocks, dtype=jnp.int32) * rows_dev
     keep = (starts[None, :] % (seq_len // pieces)[:, None] != 0).astype(F32)
 
-    tok = to_rows(tokens)
-    up_rows = to_rows(upstream)
     mix_row, ffn_row = mix_gain[None], ffn_gain[None]
-    normed, pre, pre_out, local, decays, prefix, totals = project(
-        tok, mix_row, w_mix, bound, angles, groups, chans
-    )
+    normed, pre, pre_out, local, decays, prefix, totals, angles, lags, *made = project(
+        me_one, layer_index, tok, mix_row, pieces_w, kinds, w_proj, rows_all, groups, chans
+    )
+    if by_hand:
+        w_proj, w_out = made[0].reshape(5 * chans, width), made[1].reshape(2 * chans, width)
+    gain_row = angles[GAIN : GAIN + 2].reshape(1, 2 * chans)
     ends = lax.all_gather(totals, "mp", axis=0)
-    states, entering, gated, mix_out, mid, ffn_normed = mix(
+    states, entering, gated, mid, ffn_normed = mix(
         me_one,
         keep,
         ends,
@@ -1102,16 +1158,15 @@
         decays,
         prefix,
         angles,
-        table[1:],
+        lags,
         pre_out,
         tok,
-        w_mix,
+        w_out,
         gain_row,
         ffn_row,
         groups,
         chans,
     )
-    by_hand = blocks == 8 and layers_z == 4
     core = (me & 1) if by_hand else jnp.zeros_like(me)
     core_one = core[None].astype(jnp.int32)
     chip_one = (me >> 1)[None].astype(jnp.int32)
@@ -1120,23 +1175,22 @@
     def reduction(same, other):
         return Reduction(same, other, chip_one, blocks, layers_z)
 
-    act, d_pre, grad_ffn = swiglu(ffn_normed, up_rows, w_ffn)
-    grad_ffn = lax.psum(reduce_mp(grad_ffn), "dp")
-    acts, d_pres = [act], [d_pre]
+    act, d_pre, grad_ffn, w_pre = swiglu(ffn_normed, up_rows, w_ffn)
+    grad_ffn = reduce_mp(grad_ffn)
     d_mid, d_outgate, back_local, suffix, back_totals, same, other, early_sums = mix_back(
         core_one,
         chans_dev,
-        d_pres,
-        w_ffn,
+        d_pre,
+        w_pre,
         mid,
         up_rows,
-        mix_out,
+        tok,
         states,
         pre_out,
         gated,
         normed,
         decays,
-        w_mix,
+        w_out,
         gain_row,
         ffn_row,
         angles,
@@ -1150,6 +1204,10 @@
     back_ends = lax.all_gather(back_totals, "mp", axis=0)
     if by_hand:
         back_ends = early.to_chips(early.arrived(back_ends))
+        mid, back_ends = tied(mid, back_ends)
+    out_result = from_rows(block_result(act, w_ffn, mid))
+    if by_hand:
+        back_ends, out_result = tied(back_ends, out_result)
     d_scan, sums, same, other = adjoint_finish(
         chans_dev,
         me_one,
@@ -1162,9 +1220,8 @@
         pre,
         states,
         entering,
-        bound,
         angles,
-        table[:-1],
+        lags,
         normed,
         groups,
         chans,
@@ -1172,57 +1229,72 @@
     if by_hand:
         other, d_scan = early.arrived(other, d_scan)
         late = reduction(same, other)
-        d_scan = early.to_layer(1, d_scan)
-        mid, d_scan = tied(mid, d_scan)
-        result = block_result(acts, w_ffn, mid)
-        d_scan = late.to_chips(late.arrived(d_scan, result)[0])
+        early_share, d_scan = tied(early.share_here(), d_scan)
+        early_got = along_layers(1, early_share)
     else:
         late = jnp.moveaxis(same.reshape(3, blocks, chans_dev, width), 1, 0)
+    def finish(flat, late, early):
+        early = early.reshape(4, chans_dev, width)
+        late = late.reshape(3, chans_dev, width)
+        own = me * chans_dev
+
+        def own_part(row, offset):
+            return lax.dynamic_slice(flat, (row, offset * chans + own), (1, chans_dev))[0]
+
+        grad_gain = jnp.stack([own_part(2, 0), own_part(2, 1)], axis=0)
+        below = jnp.arange(lower_logits.shape[0], dtype=jnp.int32) < layer_index[0]
+        below = below.astype(F32)[:, None]
+        soft = jax.nn.softmax(lower_logits, axis=0)
+        bound_own = jnp.sum(soft * below, axis=0, keepdims=True)
+        return (
+            flat[0],
+            jnp.transpose(late[0:2], (2, 0, 1)),
+            jnp.transpose(late[2]),
+            jnp.transpose(early[2:4], (2, 0, 1)),
+            own_part(3, 0),
+            soft * (below - bound_own) * own_part(3, 1)[None],
+            grad_gain,
+            early[0:2],
+            flat[1],
+        )
+
     grad_tokens, flat = tokens_back(
-        d_scan, d_outgate, w_mix, tok, d_mid, mix_row, early_sums, sums, groups, chans
+        d_scan, d_outgate, w_proj, tok, d_mid, mix_row, early_sums, sums, groups, chans
     )
     if by_hand:
-        flat = early.to_layer(2, early.arrived(flat))
+        flat = flat + swap(flat, "mp", 1, blocks)
+        out_tokens = from_rows(grad_tokens)
+        early_got, flat = tied(early_got, flat)
+        flat, out_tokens, grad_ffn = late.arrived(flat, out_tokens, grad_ffn)
+        same, got = late.same, late.flying[0]
     else:
         early = lax.psum(reduce_mp(early.reshape(blocks, -1, width)), "dp").astype(F32)
         late = lax.psum(reduce_mp(late.reshape(blocks, -1, width)), "dp").astype(F32)
     if by_hand:
-        flat = flat + swap(flat, "mp", 1, blocks)
-        out_tokens, out_result = from_rows(grad_tokens), from_rows(result)
-        flat, out_tokens, out_result = late.arrived(flat, out_tokens, out_result)
-        flat = late.to_layer(1, flat)
-        flat = flat + swap(flat, "mp", 2, blocks)
-        flat = flat + swap(flat, "mp", 4, blocks)
-        flat = late.to_layer(2, late.arrived(flat))
-        flat = flat + swap(flat, "dp", 1, layers_z)
-        flat = flat + swap(flat, "dp", 2, layers_z)
-        early, late = early.total(), late.total()
+        finished = lax.cond(
+            layer_index[0] > 0,
+            functools.partial(last_sums, finish, (1, 2), blocks, layers_z),
+            functools.partial(last_sums, finish, (2, 1), blocks, layers_z),
+            flat,
+            chip_one,
+            same,
+            got,
+            early_share,
+            early_got,
+        )
     else:
         flat = lax.psum(flat, ("dp", "mp"))
-        out_tokens, out_result = from_rows(grad_tokens), from_rows(block_result(acts, w_ffn, mid))
+        out_tokens = from_rows(grad_tokens)
+    grad_ffn = lax.psum(grad_ffn, "dp")
+    if by_hand:
+        *finished, grad_ffn = tied(*finished, grad_ffn)
+    else:
+        finished = finish(flat, late, early)
     grad_ffn = grad_ffn.astype(F32).reshape(3, units_dev, width)
-    early = early.reshape(4, chans_dev, width)
-    late = late.reshape(3, chans_dev, width)
-    own = me * chans_dev
-
-    def own_part(row, offset):
-        return lax.dynamic_slice(flat, (row, offset * chans + own), (1, chans_dev))[0]
-
-    grad_gain = jnp.stack([own_part(2, 0), own_part(2, 1)], axis=0)
-    d_bound = own_part(3, 1)
-    grad_lower = soft * (layer_mask[:, None] - bound_own[None]) * d_bound[None]
     return (
         out_result,
         out_tokens,
-        flat[0],
-        jnp.transpose(late[0:2], (2, 0, 1)),
-        jnp.transpose(late[2]),
-        jnp.transpose(early[2:4], (2, 0, 1)),
-        own_part(3, 0),
-        grad_lower,
-        grad_gain,
-        early[0:2],
-        flat[1],
+        *finished,
         jnp.transpose(grad_ffn[0]),
         jnp.transpose(grad_ffn[1]),
         grad_ffn[2],

time: 276 us -> 257 us (0.931)
  waiting for transfers between devices: 86.9 us -> 57.7 us
  starting transfers between devices: 23.8 us -> 47.8 us
  local copies, waits for them, and re-layouts: 31.9 us -> 19.8 us
    psum x1, waiting for transfers between devices: 39.4 us -> 0.01 us  [shards(): grad_ffn = lax.psum(grad_ffn, 'dp')]
    ppermute x0 -> x6, waiting for transfers between devices: none -> 26.1 us  [along_layers(): return lax.ppermute(share, 'dp', pairs)]
    ppermute x25 -> x22, waiting for transfers between devices: 47.4 us -> 31.2 us  [swap(): return lax.ppermute(values, axis, [(i, i ^ bit) for i in range(size)])]
    ppermute x0 -> x6, starting transfers between devices: none -> 12.2 us  [along_layers(): return lax.ppermute(share, 'dp', pairs)]
    ppermute x25 -> x22, starting transfers between devices: 23.5 us -> 35.3 us  [swap(): return lax.ppermute(values, axis, [(i, i ^ bit) for i in range(size)])]
    unnamed x69 -> x45, local copies, waits for them, and re-layouts: 14.9 us -> 5.29 us
    pallas_call x8 -> x7, Pallas kernels: 87.2 us -> 85.3 us  [kernel_call(): call(*(arg if at in free else placed(arg) for at, arg in enumerate(args)))]
  transfers between devices with their start and end apart: 28 -> 31, of which waited for: 15 -> 11; matrix products, arithmetic and copies ran while one was open for 7% -> 7% of each run, Pallas kernels for 25% -> 26%
where the time goes in v3:
time: 257 us; the launch traced here: 256 us
  Pallas kernels  87 us (34%)
  waiting for transfers between devices  57.7 us (22%)
  starting transfers between devices  47.8 us (19%)
  local copies, waits for them, and re-layouts  19.8 us (8%)
  blocking collectives  19.2 us (7%)
  between operations  14.8 us (6%)
  other arithmetic  9.58 us (4%)
    pallas_call x7, Pallas kernels, kernel_call(): call(*(arg if at in free else placed(arg) for at, arg in enumerate(args)))  85.3 us
    ppermute x22, starting transfers between devices, swap(): return lax.ppermute(values, axis, [(i, i ^ bit) for i in range(size)])  35.3 us
    ppermute x22, waiting for transfers between devices, swap(): return lax.ppermute(values, axis, [(i, i ^ bit) for i in range(size)])  31.2 us
    ppermute x6, waiting for transfers between devices, along_layers(): return lax.ppermute(share, 'dp', pairs)  26.1 us
    ppermute x6, starting transfers between devices, along_layers(): return lax.ppermute(share, 'dp', pairs)  12.2 us
    all_gather x1, blocking collectives, shards(): ends = lax.all_gather(totals, 'mp', axis=0)  9.82 us
    all_gather x1, blocking collectives, shards(): back_ends = lax.all_gather(back_totals, 'mp', axis=0)  9.35 us
    transpose x2, local copies, waits for them, and re-layouts, from_rows(): jnp.transpose(values.reshape(groups, steps, CHUNKS, width), (2, 1, 0, 3))  5.52 us
  transfers between devices with their start and end apart: 31, of which 11 were waited for; matrix products, arithmetic and copies ran while one was open for 7% of the time, Pallas kernels for 26%

profile of v3, /device:TPU:0, one launch (start us, length us, event | category | flops | bytes accessed | tf_op | source)
XLA Modules:
  0.0 256.1 jit_solution(17524744833903900436)
XLA Ops:
  10.4 3.0 %collective-permute-start.26 = (bf16[384,768]{1,0:T(8,128)(2,1)S(1)}, bf16[384,768]{1,0:T(8,128)(2,1)S(1)}, u32[]{:S(2)}, u32[]{:S(2)}) collective-permute-start(bf16[384,768]{1,0:T(8,128)(2,1)S(1)} %fusion.15.refs_0_), channel_id=1, source_target_pairs={{0,2},{1,3},{2,0},{3,1},{4,6},{5,7},{6,4},{7,5},{8,10},{9,11},{10,... | collective-permute-start | bytes 1769480 | tf_op jit(solution)/shard_map/ppermute | solution.py:956
  19.0 12.6 %collective-permute-done.26.refs_2_ = bf16[384,768]{1,0:T(8,128)(2,1)S(1)} collective-permute-done((bf16[384,768]{1,0:T(8,128)(2,1)S(1)}, bf16[384,768]{1,0:T(8,128)(2,1)S(1)}, u32[]{:S(2)}, u32[]{:S(2)}) %collective-permute-start.26) | collective-permute-done | bytes 589856 | tf_op jit(solution)/shard_map/ppermute | solution.py:956
  31.6 2.8 %collective-permute-done.27.refs_4_ = bf16[384,768]{1,0:T(8,128)(2,1)S(1)} collective-permute-done((bf16[384,768]{1,0:T(8,128)(2,1)S(1)}, bf16[384,768]{1,0:T(8,128)(2,1)S(1)}, u32[]{:S(2)}, u32[]{:S(2)}) %collective-permute-start.27) | collective-permute-done | bytes 589856 | tf_op jit(solution)/shard_map/ppermute | solution.py:956
  34.5 2.5 collective-permute-start.31
  37.8 6.2 %collective-permute-done.31 = bf16[192,768]{1,0:T(8,128)(2,1)S(1)} collective-permute-done((bf16[192,768]{1,0:T(8,128)(2,1)S(1)}, bf16[192,768]{1,0:T(8,128)(2,1)S(1)}, u32[]{:S(2)}, u32[]{:S(2)}) %collective-permute-start.31) | collective-permute-done | bytes 294944 | tf_op jit(solution)/shard_map/ppermute | solution.py:956
  47.5 11.6 %shard_map.263 = (bf16[1024,768]{1,0:T(8,128)(2,1)}, bf16[1024,1152]{1,0:T(8,128)(2,1)}, bf16[1024,768]{1,0:T(8,128)(2,1)}, f32[1024,768]{1,0:T(8,128)S(1)}, f32...) custom-call(s32[1]{0:T(128)} %bitcast.24.me, ...), custom_call_target="tpu_custom_call" | custom-call | flops 1 | bytes 1 | tf_op jit(solution)/shard_map/pallas_call | solution.py:47
  59.1 9.8 %all-gather = f32[16,8,384]{2,1,0:T(8,128)S(1)} all-gather(f32[2,8,384]{2,1,0:T(8,128)S(1)} %get-tuple-element.191), channel_id=2, replica_groups=mesh['dp'=4,'mp'=8] {'mp'}, dimensions={0}, use_global_device_ids=true | all-gather | bytes 221184 | tf_op jit(solution)/shard_map/all_gather | solution.py:1152
  68.9 7.8 %shard_map.264 = (bf16[1024,768]{1,0:T(8,128)(2,1)}, f32[2,2,8,384]{3,2,1,0:T(8,128)S(1)}, bf16[1024,768]{1,0:T(8,128)(2,1)}, f32[1024,768]{1,0:T(8,128)}, bf16[1024,768]{1,0:T(8,128)(2,1)}) custom-call(s32[1]{0:T(128)} %bitcast.24.me, f32[2,8]{1,0:T(2,128)S(1)} %compare_convert_fusion.2.keep, f32[8,2,8,384]{3,2,1,0:T(8,128)S(1)} %bitcast.100, ...), custom_call_target="tpu_custom_call" | custom-call | flops 1 | bytes 1 | tf_op jit(solution)/shard_map/pallas_call | solution.py:47
  76.7 20.7 %shard_map.265 = (bf16[1024,1536]{1,0:T(8,128)(2,1)}, bf16[1024,3072]{1,0:T(8,128)(2,1)}, bf16[8,576,768]{2,1,0:T(8,128)(2,1)}, bf16[3072,768]{1,0:T(8,128)(2,1)}) custom-call(bf16[1024,768]{1,0:T(8,128)(2,1)} %get-tuple-element.200.x, bf16[1024,768]{1,0:T(8,128)(2,1)} %bitcast.109, bf16[8,3,192,768]{3,2,1,0:T(8,128)(2,1)} %bitcast.107), custom_call_target="tpu_custom_call" | custom-call | flops 1 | bytes 1 | tf_op jit(solution)/shard_map/pallas_call | solution.py:47
  97.7 21.1 %shard_map.266 = (bf16[1024,768]{1,0:T(8,128)(2,1)}, bf16[1024,768]{1,0:T(8,128)(2,1)}, f32[1024,768]{1,0:T(8,128)S(1)}, f32[2,3,8,384]{3,2,1,0:T(8,128)S(1)}, f...) custom-call(s32[1]{0:T(128)} %bitcast.44.core, ...), custom_call_target="tpu_custom_call" | custom-call | flops 1 | bytes 1 | tf_op jit(solution)/shard_map/pallas_call | solution.py:47
  120.4 9.4 %all-gather.2 = f32[16,8,384]{2,1,0:T(8,128)S(1)} all-gather(f32[2,8,384]{2,1,0:T(8,128)} %copy-done.7), channel_id=4, replica_groups=mesh['dp'=4,'mp'=8] {'mp'}, dimensions={0}, use_global_device_ids=true | all-gather | bytes 221184 | tf_op jit(solution)/shard_map/all_gather | solution.py:1204
  136.1 6.1 %shard_map.268 = bf16[1024,768]{1,0:T(8,128)(2,1)S(1)} custom-call(bf16[1024,1536]{1,0:T(8,128)(2,1)} %get-tuple-element.220.act, bf16[8,3,192,768]{3,2,1,0:T(8,128)(2,1)} %bitcast.108, f32[1024,768]{1,0:T(8,128)} %get-tuple-element.221.mid), custom_call_target="tpu_custom_call" | custom-call | flops 1 | bytes 1 | tf_op jit(solution)/shard_map/pallas_call | solution.py:47
  142.2 2.8 %copy.36 = bf16[8,64,2,768]{3,2,1,0:T(2,128)(2,1)} copy(bf16[8,64,2,768]{3,0,1,2:T(8,128)(2,1)S(1)} %bitcast.97) | data formatting | bytes 3145728 | tf_op jit(solution)/shard_map/transpose | solution.py:1108
  144.9 10.2 %shard_map.269 = (bf16[1024,1152]{1,0:T(8,128)(2,1)}, f32[2,2,8,384]{3,2,1,0:T(8,128)S(1)}, bf16[4,144,768]{2,1,0:T(8,128)(2,1)}, bf16[4,144,768]{2,1,0:T(8,128)(2,1)}) custom-call(s32[1]{0:T(128)} %bitcast.24.me, s32[1]{0:T(128)} %bitcast.44.core, f32[2,8]{1,0:T(2,128)S(1)} %compare_convert_fusion.2.keep, f32[8,2,8,384]{3,2,1,0:T(8,128)S(1)} %bitcast.99, ...), custom_call_target="tpu_custom_call" | custom-call | flops 1 | bytes 1 | tf_op jit(solution)/shard_map/pallas_call | solution.py:47
  158.9 3.7 %collective-permute-start.39 = (bf16[192,768]{1,0:T(8,128)(2,1)S(1)}, bf16[192,768]{1,0:T(8,128)(2,1)S(1)}, u32[]{:S(2)}, u32[]{:S(2)}) collective-permute-start(bf16[192,768]{1,0:T(8,128)(2,1)S(1)} %fusion.18), channel_id=1, source_target_pairs={{0,8},{24,16},{1,9},{25,17},{2,10},{26,18},{3,11},{27,19},{4,12},{... | collective-permute-start | bytes 884744 | tf_op jit(solution)/shard_map/ppermute | solution.py:1048
  162.7 7.8 %shard_map.270 = (bf16[1024,768]{1,0:T(8,128)(2,1)S(1)}, f32[8,768]{1,0:T(8,128)S(1)}) custom-call(bf16[1024,1152]{1,0:T(8,128)(2,1)} %get-tuple-element.239.d_scan, bf16[1024,768]{1,0:T(8,128)(2,1)} %get-tuple-element.240.d_outgate, bf16[1920,768]{1,0:T(8,128)(2,1)} %bitcast.113, bf16[1024,768]{1,0:T(8,128)(2,1)} %bitcast.106, ...), custom_call_target="tpu_custom_call" | custom-call | flops 1 | bytes 1 | tf_op jit(solution)/shard_map/pallas_call | solution.py:47
  170.8 2.8 %copy.37 = bf16[8,64,2,768]{3,2,1,0:T(2,128)(2,1)} copy(bf16[8,64,2,768]{3,0,1,2:T(8,128)(2,1)S(1)} %bitcast.98) | data formatting | bytes 3145728 | tf_op jit(solution)/shard_map/transpose | solution.py:1108
  174.0 72.2 %conditional.1 = (f32[768]{0:T(1024)}, f32[768,2,48]{0,2,1:T(8,128)}, f32[768,48]{0,1:T(8,128)}, f32[768,2,48]{0,2,1:T(8,128)}, f32[48]{0:T(128)S(1)}, /*index=5...) conditional(s32[]{:T(128)} %bitcast.56, (s32[]{:T(128)}, ...), branch_computations={%region_1.5_spmd, %region_5.9_spmd} | conditional | flops 3724026 | bytes 17012220 | solution.py:1274
  184.8 5.5 %collective-permute-done.18 = f32[8,768]{1,0:T(8,128)S(1)} collective-permute-done((f32[8,768]{1,0:T(8,128)S(1)}, f32[8,768]{1,0:T(8,128)S(1)}, u32[]{:S(2)}, u32[]{:S(2)}) %collective-permute-start.18) | collective-permute-done | bytes 24608 | tf_op jit(solution)/shard_map/cond/branch_1_fun/ppermute | solution.py:956
  191.4 14.4 %collective-permute-start.19 = (f32[8,768]{1,0:T(8,128)S(1)}, f32[8,768]{1,0:T(8,128)S(1)}, u32[]{:S(2)}, u32[]{:S(2)}) collective-permute-start(f32[8,768]{1,0:T(8,128)S(1)} %add.141), channel_id=1, source_target_pairs={{0,8},{8,0},{16,24},{24,16},{1,9},{9,1},{17,25},{25,17},{2,10},{10... | collective-permute-start | bytes 73736 | tf_op jit(solution)/shard_map/cond/branch_1_fun/ppermute | solution.py:956
  209.6 4.6 %collective-permute-start.22 = (bf16[144,768]{1,0:T(8,128)(2,1)S(1)}, bf16[144,768]{1,0:T(8,128)(2,1)S(1)}, u32[]{:S(2)}, u32[]{:S(2)}) collective-permute-start(bf16[144,768]{1,0:T(8,128)(2,1)S(1)} %fusion.9), channel_id=1, source_target_pairs={{0,8},{24,16},{1,9},{25,17},{2,10},{26,18},{3,11},{27,19},{4,12},{... | collective-permute-start | bytes 663560 | tf_op jit(solution)/shard_map/cond/branch_1_fun/ppermute | solution.py:1048
  215.6 8.3 %collective-permute-done.22 = bf16[144,768]{1,0:T(8,128)(2,1)S(1)} collective-permute-done((bf16[144,768]{1,0:T(8,128)(2,1)S(1)}, bf16[144,768]{1,0:T(8,128)(2,1)S(1)}, u32[]{:S(2)}, u32[]{:S(2)}) %collective-permute-start.22) | collective-permute-done | bytes 221216 | tf_op jit(solution)/shard_map/cond/branch_1_fun/ppermute | solution.py:1048
  224.6 4.8 %collective-permute-done.25 = bf16[192,768]{1,0:T(8,128)(2,1)S(1)} collective-permute-done((bf16[192,768]{1,0:T(8,128)(2,1)S(1)}, bf16[192,768]{1,0:T(8,128)(2,1)S(1)}, u32[]{:S(2)}, u32[]{:S(2)}) %collective-permute-start.25) | collective-permute-done | bytes 294944 | tf_op jit(solution)/shard_map/cond/branch_1_fun/ppermute | solution.py:1048
  231.7 13.0 %collective-permute-done.24 = bf16[144,768]{1,0:T(8,128)(2,1)S(1)} collective-permute-done((bf16[144,768]{1,0:T(8,128)(2,1)S(1)}, bf16[144,768]{1,0:T(8,128)(2,1)S(1)}, u32[]{:S(2)}, u32[]{:S(2)}) %collective-permute-start.24) | collective-permute-done | bytes 221216 | tf_op jit(solution)/shard_map/cond/branch_1_fun/ppermute | solution.py:1048
  (148 shorter events, 49.5 us)
Async XLA Ops:
  7.2 69.5 %all-gather.5.cloned.1.call-start = ((), (), s32[]{:S(2)}) async-start(), calls=%async_computation.3 | async-start | bytes 7962624 | tf_op jit(solution)/shard_map/all_gather | solution.py:1141
  10.3 163.6 %reduce-scatter.2.cloned.1.call-start = ((), (), s32[]{:S(2)}) async-start(), calls=%async_computation.1 | async-start | bytes 7962624 | tf_op jit(solution)/shard_map/reduce_scatter | solution.py:983
  10.4 21.2 %collective-permute-start.26 = (bf16[384,768]{1,0:T(8,128)(2,1)S(1)}, bf16[384,768]{1,0:T(8,128)(2,1)S(1)}, u32[]{:S(2)}, u32[]{:S(2)}) collective-permute-start(bf16[384,768]{1,0:T(8,128)(2,1)S(1)} %fusion.15.refs_0_), channel_id=1, source_target_pairs={{0,2},{1,3},{2,0},{3,1},{4,6},{5,7},{6,4},{7,5},{8,10},{9,11},{10,... | collective-permute-start | bytes 1769480 | tf_op jit(solution)/shard_map/ppermute | solution.py:956
  13.4 21.0 %collective-permute-start.27 = (bf16[384,768]{1,0:T(8,128)(2,1)S(1)}, bf16[384,768]{1,0:T(8,128)(2,1)S(1)}, u32[]{:S(2)}, u32[]{:S(2)}) collective-permute-start(bf16[384,768]{1,0:T(8,128)(2,1)S(1)} %fusion.15.refs_0_), channel_id=1, source_target_pairs={{0,4},{1,5},{2,6},{3,7},{4,0},{5,1},{6,2},{7,3},{8,12},{9,13},{10,... | collective-permute-start | bytes 1769480 | tf_op jit(solution)/shard_map/ppermute | solution.py:956
  34.5 9.5 %collective-permute-start.31 = (bf16[192,768]{1,0:T(8,128)(2,1)S(1)}, bf16[192,768]{1,0:T(8,128)(2,1)S(1)}, u32[]{:S(2)}, u32[]{:S(2)}) collective-permute-start(bf16[192,768]{1,0:T(8,128)(2,1)S(1)} %slice.77), channel_id=1, source_target_pairs={{0,4},{1,5},{2,6},{3,7},{4,0},{5,1},{6,2},{7,3},{8,12},{9,13},{10,... | collective-permute-start | bytes 884744 | tf_op jit(solution)/shard_map/ppermute | solution.py:956
  37.1 8.1 %collective-permute-start.28 = (bf16[384,768]{1,0:T(8,128)(2,1)S(1)}, bf16[384,768]{1,0:T(8,128)(2,1)S(1)}, u32[]{:S(2)}, u32[]{:S(2)}) collective-permute-start(bf16[384,768]{1,0:T(8,128)(2,1)S(1)} %fusion.15.refs_0_), channel_id=1, source_target_pairs={{0,1},{1,0},{2,3},{3,2},{4,5},{5,4},{6,7},{7,6},{8,9},{9,8},{10,11... | collective-permute-start | bytes 1769480 | tf_op jit(solution)/shard_map/ppermute | solution.py:956
  37.7 8.3 %collective-permute-start.30 = (bf16[384,768]{1,0:T(8,128)(2,1)S(1)}, bf16[384,768]{1,0:T(8,128)(2,1)}, u32[]{:S(2)}, u32[]{:S(2)}) collective-permute-start(bf16[384,768]{1,0:T(8,128)(2,1)S(1)} %collective-permute-done.27.refs_4_), channel_id=1, source_target_pairs={{0,1},{1,0},{2,3},{3,2},{4,5},{5,4},{6,7},{7,6},{8,9},{9,8},{10,11... | collective-permute-start | bytes 1769480 | tf_op jit(solution)/shard_map/ppermute | solution.py:956
  97.4 148.7 %all-reduce.3.cloned.1.call-start = ((), (), s32[]{:S(2)}) async-start(), calls=%async_computation.2 | async-start | bytes 1769472 | tf_op jit(solution)/shard_map/psum | solution.py:1288
  120.0 9.7 %collective-permute-start.34 = (bf16[4,192,768]{2,1,0:T(8,128)(2,1)}, bf16[4,192,768]{2,1,0:T(8,128)(2,1)}, u32[]{:S(2)}, u32[]{:S(2)}) collective-permute-start(bf16[4,192,768]{2,1,0:T(8,128)(2,1)} %get-tuple-element.211), channel_id=1, source_target_pairs={{0,1},{1,0},{2,3},{3,2},{4,5},{5,4},{6,7},{7,6},{8,9},{9,8},{10,11... | collective-permute-start | bytes 3538952 | tf_op jit(solution)/shard_map/ppermute | solution.py:956
  132.6 23.3 %collective-permute-start.35 = (bf16[192,768]{1,0:T(8,128)(2,1)S(1)}, bf16[192,768]{1,0:T(8,128)(2,1)}, u32[]{:S(2)}, u32[]{:S(2)}) collective-permute-start(bf16[192,768]{1,0:T(8,128)(2,1)S(1)} %get-tuple-element.223), channel_id=1, source_target_pairs={{0,2},{1,3},{2,0},{3,1},{4,6},{5,7},{6,4},{7,5},{8,10},{9,11},{10,... | collective-permute-start | bytes 884744 | tf_op jit(solution)/shard_map/ppermute | solution.py:956
  133.5 22.4 %collective-permute-start.36 = (bf16[192,768]{1,0:T(8,128)(2,1)S(1)}, bf16[192,768]{1,0:T(8,128)(2,1)}, u32[]{:S(2)}, u32[]{:S(2)}) collective-permute-start(bf16[192,768]{1,0:T(8,128)(2,1)S(1)} %get-tuple-element.224), channel_id=1, source_target_pairs={{0,4},{1,5},{2,6},{3,7},{4,0},{5,1},{6,2},{7,3},{8,12},{9,13},{10,... | collective-permute-start | bytes 884744 | tf_op jit(solution)/shard_map/ppermute | solution.py:956
  134.6 22.8 %collective-permute-start.37 = (bf16[192,768]{1,0:T(8,128)(2,1)S(1)}, bf16[192,768]{1,0:T(8,128)(2,1)}, u32[]{:S(2)}, u32[]{:S(2)}) collective-permute-start(bf16[192,768]{1,0:T(8,128)(2,1)S(1)} %get-tuple-element.225), channel_id=1, source_target_pairs={{0,6},{1,7},{2,4},{3,5},{4,2},{5,3},{6,0},{7,1},{8,14},{9,15},{10,... | collective-permute-start | bytes 884744 | tf_op jit(solution)/shard_map/ppermute | solution.py:956
  157.4 16.2 %collective-permute-start.38 = (bf16[4,144,768]{2,1,0:T(8,128)(2,1)}, bf16[4,144,768]{2,1,0:T(8,128)(2,1)S(1)}, u32[]{:S(2)}, u32[]{:S(2)}) collective-permute-start(bf16[4,144,768]{2,1,0:T(8,128)(2,1)} %get-tuple-element.233), channel_id=1, source_target_pairs={{0,1},{1,0},{2,3},{3,2},{4,5},{5,4},{6,7},{7,6},{8,9},{9,8},{10,11... | collective-permute-start | bytes 2654216 | tf_op jit(solution)/shard_map/ppermute | solution.py:956
  158.9 14.7 %collective-permute-start.39 = (bf16[192,768]{1,0:T(8,128)(2,1)S(1)}, bf16[192,768]{1,0:T(8,128)(2,1)S(1)}, u32[]{:S(2)}, u32[]{:S(2)}) collective-permute-start(bf16[192,768]{1,0:T(8,128)(2,1)S(1)} %fusion.18), channel_id=1, source_target_pairs={{0,8},{24,16},{1,9},{25,17},{2,10},{26,18},{3,11},{27,19},{4,12},{... | collective-permute-start | bytes 884744 | tf_op jit(solution)/shard_map/ppermute | solution.py:1048
  177.9 12.4 %collective-permute-start.14 = (bf16[144,768]{1,0:T(8,128)(2,1)S(1)}, bf16[144,768]{1,0:T(8,128)(2,1)S(1)}, u32[]{:S(2)}, u32[]{:S(2)}) collective-permute-start(bf16[144,768]{1,0:T(8,128)(2,1)S(1)} %get-tuple-element.71), channel_id=1, source_target_pairs={{0,2},{1,3},{2,0},{3,1},{4,6},{5,7},{6,4},{7,5},{8,10},{9,11},{10,... | collective-permute-start | bytes 663560 | tf_op jit(solution)/shard_map/cond/branch_1_fun/ppermute | solution.py:956
  179.2 11.0 %collective-permute-start.15 = (bf16[144,768]{1,0:T(8,128)(2,1)S(1)}, bf16[144,768]{1,0:T(8,128)(2,1)S(1)}, u32[]{:S(2)}, u32[]{:S(2)}) collective-permute-start(bf16[144,768]{1,0:T(8,128)(2,1)S(1)} %get-tuple-element.72), channel_id=1, source_target_pairs={{0,4},{1,5},{2,6},{3,7},{4,0},{5,1},{6,2},{7,3},{8,12},{9,13},{10,... | collective-permute-start | bytes 663560 | tf_op jit(solution)/shard_map/cond/branch_1_fun/ppermute | solution.py:956
  179.9 10.4 %collective-permute-start.16 = (bf16[144,768]{1,0:T(8,128)(2,1)S(1)}, bf16[144,768]{1,0:T(8,128)(2,1)}, u32[]{:S(2)}, u32[]{:S(2)}) collective-permute-start(bf16[144,768]{1,0:T(8,128)(2,1)S(1)} %get-tuple-element.73), channel_id=1, source_target_pairs={{0,6},{1,7},{2,4},{3,5},{4,2},{5,3},{6,0},{7,1},{8,14},{9,15},{10,... | collective-permute-start | bytes 663560 | tf_op jit(solution)/shard_map/cond/branch_1_fun/ppermute | solution.py:956
  182.0 8.2 %collective-permute-start.18 = (f32[8,768]{1,0:T(8,128)S(1)}, f32[8,768]{1,0:T(8,128)S(1)}, u32[]{:S(2)}, u32[]{:S(2)}) collective-permute-start(f32[8,768]{1,0:T(8,128)S(1)} %add.136), channel_id=1, source_target_pairs={{0,4},{1,5},{2,6},{3,7},{4,0},{5,1},{6,2},{7,3},{8,12},{9,13},{10,... | collective-permute-start | bytes 73736 | tf_op jit(solution)/shard_map/cond/branch_1_fun/ppermute | solution.py:956
  191.4 22.8 %collective-permute-start.19 = (f32[8,768]{1,0:T(8,128)S(1)}, f32[8,768]{1,0:T(8,128)S(1)}, u32[]{:S(2)}, u32[]{:S(2)}) collective-permute-start(f32[8,768]{1,0:T(8,128)S(1)} %add.141), channel_id=1, source_target_pairs={{0,8},{8,0},{16,24},{24,16},{1,9},{9,1},{17,25},{25,17},{2,10},{10... | collective-permute-start | bytes 73736 | tf_op jit(solution)/shard_map/cond/branch_1_fun/ppermute | solution.py:956
  205.9 8.3 %collective-permute-start.20 = (f32[8,768]{1,0:T(8,128)S(1)}, f32[8,768]{1,0:T(8,128)S(1)}, u32[]{:S(2)}, u32[]{:S(2)}) collective-permute-start(f32[8,768]{1,0:T(8,128)S(1)} %add.141), channel_id=1, source_target_pairs={{0,16},{8,24},{16,0},{24,8},{1,17},{9,25},{17,1},{25,9},{2,18},{10... | collective-permute-start | bytes 73736 | tf_op jit(solution)/shard_map/cond/branch_1_fun/ppermute | solution.py:956
  205.9 8.3 %collective-permute-start.21 = (f32[8,768]{1,0:T(8,128)S(1)}, f32[8,768]{1,0:T(8,128)S(1)}, u32[]{:S(2)}, u32[]{:S(2)}) collective-permute-start(f32[8,768]{1,0:T(8,128)S(1)} %add.141), channel_id=1, source_target_pairs={{0,24},{8,16},{16,8},{24,0},{1,25},{9,17},{17,9},{25,1},{2,26},{10... | collective-permute-start | bytes 73736 | tf_op jit(solution)/shard_map/cond/branch_1_fun/ppermute | solution.py:956
  208.3 21.1 %collective-permute-start.25 = (bf16[192,768]{1,0:T(8,128)(2,1)S(1)}, bf16[192,768]{1,0:T(8,128)(2,1)S(1)}, u32[]{:S(2)}, u32[]{:S(2)}) collective-permute-start(bf16[192,768]{1,0:T(8,128)(2,1)S(1)} %add_convert_fusion.4), channel_id=1, source_target_pairs={{8,0},{16,24},{9,1},{17,25},{10,2},{18,26},{11,3},{19,27},{12,4},{... | collective-permute-start | bytes 884744 | tf_op jit(solution)/shard_map/cond/branch_1_fun/ppermute | solution.py:1048
  209.6 14.3 %collective-permute-start.22 = (bf16[144,768]{1,0:T(8,128)(2,1)S(1)}, bf16[144,768]{1,0:T(8,128)(2,1)S(1)}, u32[]{:S(2)}, u32[]{:S(2)}) collective-permute-start(bf16[144,768]{1,0:T(8,128)(2,1)S(1)} %fusion.9), channel_id=1, source_target_pairs={{0,8},{24,16},{1,9},{25,17},{2,10},{26,18},{3,11},{27,19},{4,12},{... | collective-permute-start | bytes 663560 | tf_op jit(solution)/shard_map/cond/branch_1_fun/ppermute | solution.py:1048
  229.5 15.2 %collective-permute-start.24 = (bf16[144,768]{1,0:T(8,128)(2,1)S(1)}, bf16[144,768]{1,0:T(8,128)(2,1)S(1)}, u32[]{:S(2)}, u32[]{:S(2)}) collective-permute-start(bf16[144,768]{1,0:T(8,128)(2,1)S(1)} %add_convert_fusion.6), channel_id=1, source_target_pairs={{8,0},{16,24},{9,1},{17,25},{10,2},{18,26},{11,3},{19,27},{12,4},{... | collective-permute-start | bytes 663560 | tf_op jit(solution)/shard_map/cond/branch_1_fun/ppermute | solution.py:1048
  (31 other events, 216.1 us)
Sparse Core Ops, SparseCore 0:
  10.5 59.6 all-gather.4
  97.5 76.3 reduce-scatter.1
  176.4 58.6 all-reduce.2

commit v4 on v3

--- a/solution.py
+++ b/solution.py
@@ -952,6 +952,24 @@
     )(act, w_ffn, mid)
 
 
+def unpack_body(ffn, gate, up, down):
+    rows = gate.shape[0]
+    for k, out in enumerate((gate, up, down)):
+        out[...] = ffn[k * rows : (k + 1) * rows, :].astype(F32)
+
+
+def unpack(ffn):
+    rows, width = ffn.shape[0] // 3, ffn.shape[1]
+    return kernel_call(
+        unpack_body,
+        (1,),
+        [whole(ffn.shape)],
+        [whole((rows, width))] * 3,
+        [shaped((rows, width))] * 3,
+        vmem=16,
+    )(ffn)
+
+
 def swap(values, axis, bit, size):
     return lax.ppermute(values, axis, [(i, i ^ bit) for i in range(size)])
 
@@ -1000,24 +1018,23 @@
     )(chip, same, got)
 
 
-def last_sums(finish, order, size, layers, flat, chip, same, got, early, early_got):
+def last_sums(finish, from_rows, order, size, layers, flat, chip, same, got, early, early_got, tokens):
     last = Reduction(same, None, chip, size, layers)
     last.flying = [got]
+    early = both(early, early_got)
+    early_got = along_layers(2, early)
     flat = flat + swap(flat, "mp", 2 * order[0], size)
-    flat = last.to_chips(flat)
-    early, flat = tied(both(early, early_got), flat)
-    early_got = along_layers(2, early)
+    flat, tokens = tied(last.to_chips(flat), tokens)
     flat = flat + swap(flat, "mp", 2 * order[1], size)
-    late, early, early_got, flat = tied(last.share_here(), early, early_got, flat)
-    late_got = along_layers(1, late)
+    moved = from_rows(tokens)
+    late, flat, moved, early_got = tied(last.share_here(), flat, moved, early_got)
+    one, two, three = (swap(late, "dp", bit, layers) for bit in (1, 2, 3))
     early = both(early, early_got)
     early_got = along_layers(3, early)
-    one, two, three = (swap(flat, "dp", bit, layers) for bit in (1, 2, 3))
-    flat = (flat + one) + (two + three)
-    for number in (2, 3):
-        late = both(late, late_got)
-        late_got = along_layers(number, late)
-    return finish(flat, settled(late, late_got), settled(early, early_got))
+    flat = flat + swap(flat, "mp", 1, size)
+    late = joined(joined(late, one), joined(two, three))
+    early = settled(early, early_got).reshape(2, 2, -1, early.shape[-1])
+    return (*finish(flat, late), moved, early[0], early[1])
 
 
 class Reduction:
@@ -1233,8 +1250,7 @@
         early_got = along_layers(1, early_share)
     else:
         late = jnp.moveaxis(same.reshape(3, blocks, chans_dev, width), 1, 0)
-    def finish(flat, late, early):
-        early = early.reshape(4, chans_dev, width)
+    def finish(flat, late):
         late = late.reshape(3, chans_dev, width)
         own = me * chans_dev
 
@@ -1250,11 +1266,9 @@
             flat[0],
             jnp.transpose(late[0:2], (2, 0, 1)),
             jnp.transpose(late[2]),
-            jnp.transpose(early[2:4], (2, 0, 1)),
             own_part(3, 0),
             soft * (below - bound_own) * own_part(3, 1)[None],
             grad_gain,
-            early[0:2],
             flat[1],
         )
 
@@ -1262,42 +1276,52 @@
         d_scan, d_outgate, w_proj, tok, d_mid, mix_row, early_sums, sums, groups, chans
     )
     if by_hand:
-        flat = flat + swap(flat, "mp", 1, blocks)
-        out_tokens = from_rows(grad_tokens)
-        early_got, flat = tied(early_got, flat)
-        flat, out_tokens, grad_ffn = late.arrived(flat, out_tokens, grad_ffn)
+        one, two, three = (swap(flat, "dp", bit, layers_z) for bit in (1, 2, 3))
+        flat, early_got = tied((flat + one) + (two + three), early_got)
+        flat, grad_tokens, grad_ffn = late.arrived(flat, grad_tokens, grad_ffn)
         same, got = late.same, late.flying[0]
-    else:
-        early = lax.psum(reduce_mp(early.reshape(blocks, -1, width)), "dp").astype(F32)
-        late = lax.psum(reduce_mp(late.reshape(blocks, -1, width)), "dp").astype(F32)
-    if by_hand:
         finished = lax.cond(
             layer_index[0] > 0,
-            functools.partial(last_sums, finish, (1, 2), blocks, layers_z),
-            functools.partial(last_sums, finish, (2, 1), blocks, layers_z),
+            functools.partial(last_sums, finish, from_rows, (1, 2), blocks, layers_z),
+            functools.partial(last_sums, finish, from_rows, (2, 1), blocks, layers_z),
             flat,
             chip_one,
             same,
             got,
             early_share,
             early_got,
+            grad_tokens,
         )
     else:
+        early = lax.psum(reduce_mp(early.reshape(blocks, -1, width)), "dp").astype(F32)
+        late = lax.psum(reduce_mp(late.reshape(blocks, -1, width)), "dp").astype(F32)
         flat = lax.psum(flat, ("dp", "mp"))
-        out_tokens = from_rows(grad_tokens)
-    grad_ffn = lax.psum(grad_ffn, "dp")
+    grad_ffn = lax.psum(grad_ffn.reshape(3 * units_dev, width), "dp")
     if by_hand:
         *finished, grad_ffn = tied(*finished, grad_ffn)
+        *finished, g_output, g_outgate = finished
+        g_gate, g_up, g_down = unpack(grad_ffn)
     else:
-        finished = finish(flat, late, early)
-    grad_ffn = grad_ffn.astype(F32).reshape(3, units_dev, width)
+        finished = finish(flat, late)
+        g_gate, g_up, g_down = grad_ffn.astype(F32).reshape(3, units_dev, width)
+        g_output, g_outgate = early.reshape(2, 2, chans_dev, width)
+    gain_mix, g_input, g_forget, g_phase, g_lower, g_gain, gain_ffn, *moved = finished
+    out_tokens = moved[0] if moved else from_rows(grad_tokens)
     return (
         out_result,
         out_tokens,
-        *finished,
-        jnp.transpose(grad_ffn[0]),
-        jnp.transpose(grad_ffn[1]),
-        grad_ffn[2],
+        gain_mix,
+        g_input,
+        g_forget,
+        jnp.transpose(g_outgate, (2, 0, 1)),
+        g_phase,
+        g_lower,
+        g_gain,
+        g_output,
+        gain_ffn,
+        jnp.transpose(g_gate),
+        jnp.transpose(g_up),
+        g_down,
     )
 
 

time: 257 us -> 246 us (0.957)
  starting transfers between devices: 47.8 us -> 36.6 us
  Pallas kernels: 87 us -> 90.6 us
    ppermute x6 -> x3, waiting for transfers between devices: 26.1 us -> 8.27 us  [along_layers(): return lax.ppermute(share, 'dp', pairs)]
    ppermute x22 -> x25, waiting for transfers between devices: 31.2 us -> 46.5 us  [swap(): return lax.ppermute(values, axis, [(i, i ^ bit) for i in range(size)])]
    ppermute x6 -> x3, starting transfers between devices: 12.2 us -> 5.64 us  [along_layers(): return lax.ppermute(share, 'dp', pairs)]
    ppermute x22 -> x25, starting transfers between devices: 35.3 us -> 30.7 us  [swap(): return lax.ppermute(values, axis, [(i, i ^ bit) for i in range(size)])]
    reshape x0 -> x1, local copies, waits for them, and re-layouts: none -> 2.76 us  [from_rows(): values.reshape(groups, steps, CHUNKS, width)]
    transpose x2 -> x1, local copies, waits for them, and re-layouts: 5.52 us -> 2.76 us  [from_rows(): jnp.transpose(values.reshape(groups, steps, CHUNKS, width), (2, 1, 0, 3))]
    psum x1, waiting for transfers between devices: 0.01 us -> 2.63 us  [shards(): grad_ffn = lax.psum(grad_ffn.reshape(3 * units_dev, width), 'dp')]
    pallas_call x7 -> x8, Pallas kernels: 85.3 us -> 87.7 us  [kernel_call(): call(*(arg if at in free else placed(arg) for at, arg in enumerate(args)))]
  transfers between devices with their start and end apart: 31 -> 31, of which waited for: 11 -> 12; matrix products, arithmetic and copies ran while one was open for 7% -> 7% of each run, Pallas kernels for 26% -> 28%
where the time goes in v4:
time: 246 us; the launch traced here: 245 us
  Pallas kernels  90.6 us (37%)
  waiting for transfers between devices  57.4 us (23%)
  starting transfers between devices  36.6 us (15%)
  blocking collectives  19.2 us (8%)
  local copies, waits for them, and re-layouts  17.3 us (7%)
  between operations  14.8 us (6%)
  other arithmetic  9.13 us (4%)
    pallas_call x8, Pallas kernels, kernel_call(): call(*(arg if at in free else placed(arg) for at, arg in enumerate(args)))  87.7 us
    ppermute x25, waiting for transfers between devices, swap(): return lax.ppermute(values, axis, [(i, i ^ bit) for i in range(size)])  46.5 us
    ppermute x25, starting transfers between devices, swap(): return lax.ppermute(values, axis, [(i, i ^ bit) for i in range(size)])  30.7 us
    all_gather x1, blocking collectives, shards(): ends = lax.all_gather(totals, 'mp', axis=0)  9.82 us
    all_gather x1, blocking collectives, shards(): back_ends = lax.all_gather(back_totals, 'mp', axis=0)  9.37 us
    ppermute x3, waiting for transfers between devices, along_layers(): return lax.ppermute(share, 'dp', pairs)  8.27 us
    ppermute x3, starting transfers between devices, along_layers(): return lax.ppermute(share, 'dp', pairs)  5.64 us
    unnamed x49, local copies, waits for them, and re-layouts  5.25 us
  transfers between devices with their start and end apart: 31, of which 12 were waited for; matrix products, arithmetic and copies ran while one was open for 7% of the time, Pallas kernels for 28%

profile of v4, /device:TPU:0, one launch (start us, length us, event | category | flops | bytes accessed | tf_op | source)
XLA Modules:
  0.0 245.2 jit_solution(17824476823743052345)
XLA Ops:
  10.4 3.0 %collective-permute-start.22 = (bf16[384,768]{1,0:T(8,128)(2,1)S(1)}, bf16[384,768]{1,0:T(8,128)(2,1)S(1)}, u32[]{:S(2)}, u32[]{:S(2)}) collective-permute-start(bf16[384,768]{1,0:T(8,128)(2,1)S(1)} %fusion.15.refs_0_), channel_id=1, source_target_pairs={{0,2},{1,3},{2,0},{3,1},{4,6},{5,7},{6,4},{7,5},{8,10},{9,11},{10,... | collective-permute-start | bytes 1769480 | tf_op jit(solution)/shard_map/ppermute | solution.py:974
  19.0 12.6 %collective-permute-done.22.refs_2_ = bf16[384,768]{1,0:T(8,128)(2,1)S(1)} collective-permute-done((bf16[384,768]{1,0:T(8,128)(2,1)S(1)}, bf16[384,768]{1,0:T(8,128)(2,1)S(1)}, u32[]{:S(2)}, u32[]{:S(2)}) %collective-permute-start.22) | collective-permute-done | bytes 589856 | tf_op jit(solution)/shard_map/ppermute | solution.py:974
  31.6 2.8 %collective-permute-done.23.refs_4_ = bf16[384,768]{1,0:T(8,128)(2,1)S(1)} collective-permute-done((bf16[384,768]{1,0:T(8,128)(2,1)S(1)}, bf16[384,768]{1,0:T(8,128)(2,1)S(1)}, u32[]{:S(2)}, u32[]{:S(2)}) %collective-permute-start.23) | collective-permute-done | bytes 589856 | tf_op jit(solution)/shard_map/ppermute | solution.py:974
  37.8 6.2 %collective-permute-done.27 = bf16[192,768]{1,0:T(8,128)(2,1)S(1)} collective-permute-done((bf16[192,768]{1,0:T(8,128)(2,1)S(1)}, bf16[192,768]{1,0:T(8,128)(2,1)S(1)}, u32[]{:S(2)}, u32[]{:S(2)}) %collective-permute-start.27) | collective-permute-done | bytes 294944 | tf_op jit(solution)/shard_map/ppermute | solution.py:974
  47.5 11.6 %shard_map.263 = (bf16[1024,768]{1,0:T(8,128)(2,1)}, bf16[1024,1152]{1,0:T(8,128)(2,1)}, bf16[1024,768]{1,0:T(8,128)(2,1)}, f32[1024,768]{1,0:T(8,128)S(1)}, f32...) custom-call(s32[1]{0:T(128)} %bitcast.28.me, ...), custom_call_target="tpu_custom_call" | custom-call | flops 1 | bytes 1 | tf_op jit(solution)/shard_map/pallas_call | solution.py:47
  59.1 9.8 %all-gather = f32[16,8,384]{2,1,0:T(8,128)S(1)} all-gather(f32[2,8,384]{2,1,0:T(8,128)S(1)} %get-tuple-element.202), channel_id=2, replica_groups=mesh['dp'=4,'mp'=8] {'mp'}, dimensions={0}, use_global_device_ids=true | all-gather | bytes 221184 | tf_op jit(solution)/shard_map/all_gather | solution.py:1169
  69.0 7.8 %shard_map.264 = (bf16[1024,768]{1,0:T(8,128)(2,1)}, f32[2,2,8,384]{3,2,1,0:T(8,128)S(1)}, bf16[1024,768]{1,0:T(8,128)(2,1)}, f32[1024,768]{1,0:T(8,128)}, bf16[1024,768]{1,0:T(8,128)(2,1)}) custom-call(s32[1]{0:T(128)} %bitcast.28.me, f32[2,8]{1,0:T(2,128)S(1)} %compare_convert_fusion.2.keep, f32[8,2,8,384]{3,2,1,0:T(8,128)S(1)} %bitcast.100, ...), custom_call_target="tpu_custom_call" | custom-call | flops 1 | bytes 1 | tf_op jit(solution)/shard_map/pallas_call | solution.py:47
  76.7 20.7 %shard_map.265 = (bf16[1024,1536]{1,0:T(8,128)(2,1)}, bf16[1024,3072]{1,0:T(8,128)(2,1)}, bf16[8,576,768]{2,1,0:T(8,128)(2,1)}, bf16[3072,768]{1,0:T(8,128)(2,1)}) custom-call(bf16[1024,768]{1,0:T(8,128)(2,1)} %get-tuple-element.211.x, bf16[1024,768]{1,0:T(8,128)(2,1)} %bitcast.109, bf16[8,3,192,768]{3,2,1,0:T(8,128)(2,1)} %bitcast.107), custom_call_target="tpu_custom_call" | custom-call | flops 1 | bytes 1 | tf_op jit(solution)/shard_map/pallas_call | solution.py:47
  97.7 21.1 %shard_map.266 = (bf16[1024,768]{1,0:T(8,128)(2,1)}, bf16[1024,768]{1,0:T(8,128)(2,1)}, f32[1024,768]{1,0:T(8,128)S(1)}, f32[2,3,8,384]{3,2,1,0:T(8,128)S(1)}, f...) custom-call(s32[1]{0:T(128)} %bitcast.48.core, ...), custom_call_target="tpu_custom_call" | custom-call | flops 1 | bytes 1 | tf_op jit(solution)/shard_map/pallas_call | solution.py:47
  120.4 9.4 %all-gather.2 = f32[16,8,384]{2,1,0:T(8,128)S(1)} all-gather(f32[2,8,384]{2,1,0:T(8,128)} %copy-done.7), channel_id=4, replica_groups=mesh['dp'=4,'mp'=8] {'mp'}, dimensions={0}, use_global_device_ids=true | all-gather | bytes 221184 | tf_op jit(solution)/shard_map/all_gather | solution.py:1221
  136.1 6.1 %shard_map.268 = bf16[1024,768]{1,0:T(8,128)(2,1)S(1)} custom-call(bf16[1024,1536]{1,0:T(8,128)(2,1)} %get-tuple-element.231.act, bf16[8,3,192,768]{3,2,1,0:T(8,128)(2,1)} %bitcast.108, f32[1024,768]{1,0:T(8,128)} %get-tuple-element.232.mid), custom_call_target="tpu_custom_call" | custom-call | flops 1 | bytes 1 | tf_op jit(solution)/shard_map/pallas_call | solution.py:47
  142.2 2.8 %copy.39 = bf16[8,64,2,768]{3,2,1,0:T(2,128)(2,1)} copy(bf16[8,64,2,768]{3,0,1,2:T(8,128)(2,1)S(1)} %bitcast.98) | data formatting | bytes 3145728 | tf_op jit(solution)/shard_map/transpose | solution.py:1125
  145.0 10.2 %shard_map.269 = (bf16[1024,1152]{1,0:T(8,128)(2,1)}, f32[2,2,8,384]{3,2,1,0:T(8,128)S(1)}, bf16[4,144,768]{2,1,0:T(8,128)(2,1)}, bf16[4,144,768]{2,1,0:T(8,128)(2,1)}) custom-call(s32[1]{0:T(128)} %bitcast.28.me, s32[1]{0:T(128)} %bitcast.48.core, f32[2,8]{1,0:T(2,128)S(1)} %compare_convert_fusion.2.keep, f32[8,2,8,384]{3,2,1,0:T(8,128)S(1)} %bitcast.99, ...), custom_call_target="tpu_custom_call" | custom-call | flops 1 | bytes 1 | tf_op jit(solution)/shard_map/pallas_call | solution.py:47
  159.0 3.7 %collective-permute-start.38 = (bf16[192,768]{1,0:T(8,128)(2,1)S(1)}, bf16[192,768]{1,0:T(8,128)(2,1)S(1)}, u32[]{:S(2)}, u32[]{:S(2)}) collective-permute-start(bf16[192,768]{1,0:T(8,128)(2,1)S(1)} %fusion.18), channel_id=1, source_target_pairs={{0,8},{24,16},{1,9},{25,17},{2,10},{26,18},{3,11},{27,19},{4,12},{... | collective-permute-start | bytes 884744 | tf_op jit(solution)/shard_map/ppermute | solution.py:1065
  162.7 7.8 %shard_map.270 = (bf16[1024,768]{1,0:T(8,128)(2,1)S(1)}, f32[8,768]{1,0:T(8,128)S(1)}) custom-call(bf16[1024,1152]{1,0:T(8,128)(2,1)} %get-tuple-element.250.d_scan, bf16[1024,768]{1,0:T(8,128)(2,1)} %get-tuple-element.251.d_outgate, bf16[1920,768]{1,0:T(8,128)(2,1)} %bitcast.113, bf16[1024,768]{1,0:T(8,128)(2,1)} %bitcast.106, ...), custom_call_target="tpu_custom_call" | custom-call | flops 1 | bytes 1 | tf_op jit(solution)/shard_map/pallas_call | solution.py:47
  170.6 3.0 %collective-permute-start.36 = (f32[8,768]{1,0:T(8,128)S(1)}, f32[8,768]{1,0:T(8,128)S(1)}, u32[]{:S(2)}, u32[]{:S(2)}) collective-permute-start(f32[8,768]{1,0:T(8,128)S(1)} %get-tuple-element.256), channel_id=1, source_target_pairs={{0,16},{8,24},{16,0},{24,8},{1,17},{9,25},{17,1},{25,9},{2,18},{10... | collective-permute-start | bytes 73736 | tf_op jit(solution)/shard_map/ppermute | solution.py:974
  175.4 3.8 %collective-permute-done.37 = f32[8,768]{1,0:T(8,128)S(1)} collective-permute-done((f32[8,768]{1,0:T(8,128)S(1)}, f32[8,768]{1,0:T(8,128)S(1)}, u32[]{:S(2)}, u32[]{:S(2)}) %collective-permute-start.37) | collective-permute-done | bytes 24608 | tf_op jit(solution)/shard_map/ppermute | solution.py:974
  179.3 54.2 %conditional.1 = (f32[768]{0:T(1024)S(1)}, f32[768,2,48]{0,2,1:T(8,128)}, f32[768,48]{0,1:T(8,128)}, f32[48]{0:T(128)S(1)}, f32[12,48]{1,0:T(8,128)S(1)}, /*inde...) conditional(s32[]{:T(128)} %bitcast.54, (s32[]{:T(128)}, ...), branch_computations={%region_1.5_spmd, %region_5.9_spmd} | conditional | flops 3379962 | bytes 19026144 | solution.py:1283
  188.4 2.8 %copy.36 = bf16[2,64,8,768]{3,0,1,2:T(2,128)(2,1)} copy(bf16[2,64,8,768]{3,2,1,0:T(8,128)(2,1)S(1)} %bitcast.97) | data formatting | bytes 3145728 | tf_op jit(solution)/shard_map/cond/branch_1_fun/reshape | solution.py:1126
  191.1 3.8 %collective-permute-done.15 = f32[8,768]{1,0:T(8,128)S(1)} collective-permute-done((f32[8,768]{1,0:T(8,128)S(1)}, f32[8,768]{1,0:T(8,128)S(1)}, u32[]{:S(2)}, u32[]{:S(2)}) %collective-permute-start.15) | collective-permute-done | bytes 24608 | tf_op jit(solution)/shard_map/cond/branch_1_fun/ppermute | solution.py:974
  196.4 4.8 %collective-permute-start.18 = (bf16[144,768]{1,0:T(8,128)(2,1)S(1)}, bf16[144,768]{1,0:T(8,128)(2,1)S(1)}, u32[]{:S(2)}, u32[]{:S(2)}) collective-permute-start(bf16[144,768]{1,0:T(8,128)(2,1)S(1)} %fusion.9), channel_id=1, source_target_pairs={{0,8},{8,0},{16,24},{24,16},{1,9},{9,1},{17,25},{25,17},{2,10},{10... | collective-permute-start | bytes 663560 | tf_op jit(solution)/shard_map/cond/branch_1_fun/ppermute | solution.py:974
  201.2 3.0 %collective-permute-start.19 = (bf16[144,768]{1,0:T(8,128)(2,1)S(1)}, bf16[144,768]{1,0:T(8,128)(2,1)S(1)}, u32[]{:S(2)}, u32[]{:S(2)}) collective-permute-start(bf16[144,768]{1,0:T(8,128)(2,1)S(1)} %fusion.9), channel_id=1, source_target_pairs={{0,16},{8,24},{16,0},{24,8},{1,17},{9,25},{17,1},{25,9},{2,18},{10... | collective-permute-start | bytes 663560 | tf_op jit(solution)/shard_map/cond/branch_1_fun/ppermute | solution.py:974
  208.2 14.7 %collective-permute-done.19 = bf16[144,768]{1,0:T(8,128)(2,1)S(1)} collective-permute-done((bf16[144,768]{1,0:T(8,128)(2,1)S(1)}, bf16[144,768]{1,0:T(8,128)(2,1)S(1)}, u32[]{:S(2)}, u32[]{:S(2)}) %collective-permute-start.19) | collective-permute-done | bytes 221216 | tf_op jit(solution)/shard_map/cond/branch_1_fun/ppermute | solution.py:974
  224.4 8.3 %collective-permute-done.21 = bf16[192,768]{1,0:T(8,128)(2,1)S(1)} collective-permute-done((bf16[192,768]{1,0:T(8,128)(2,1)S(1)}, bf16[192,768]{1,0:T(8,128)(2,1)S(1)}, u32[]{:S(2)}, u32[]{:S(2)}) %collective-permute-start.21) | collective-permute-done | bytes 294944 | tf_op jit(solution)/shard_map/cond/branch_1_fun/ppermute | solution.py:1065
  (142 shorter events, 50.6 us)
Async XLA Ops:
  7.2 69.5 %all-gather.5.cloned.1.call-start = ((), (), s32[]{:S(2)}) async-start(), calls=%async_computation.3 | async-start | bytes 7962624 | tf_op jit(solution)/shard_map/all_gather | solution.py:1158
  10.4 168.9 %reduce-scatter.2.cloned.1.call-start = ((), (), s32[]{:S(2)}) async-start(), calls=%async_computation.1 | async-start | bytes 7962624 | tf_op jit(solution)/shard_map/reduce_scatter | solution.py:1001
  10.4 21.2 %collective-permute-start.22 = (bf16[384,768]{1,0:T(8,128)(2,1)S(1)}, bf16[384,768]{1,0:T(8,128)(2,1)S(1)}, u32[]{:S(2)}, u32[]{:S(2)}) collective-permute-start(bf16[384,768]{1,0:T(8,128)(2,1)S(1)} %fusion.15.refs_0_), channel_id=1, source_target_pairs={{0,2},{1,3},{2,0},{3,1},{4,6},{5,7},{6,4},{7,5},{8,10},{9,11},{10,... | collective-permute-start | bytes 1769480 | tf_op jit(solution)/shard_map/ppermute | solution.py:974
  13.4 21.0 %collective-permute-start.23 = (bf16[384,768]{1,0:T(8,128)(2,1)S(1)}, bf16[384,768]{1,0:T(8,128)(2,1)S(1)}, u32[]{:S(2)}, u32[]{:S(2)}) collective-permute-start(bf16[384,768]{1,0:T(8,128)(2,1)S(1)} %fusion.15.refs_0_), channel_id=1, source_target_pairs={{0,4},{1,5},{2,6},{3,7},{4,0},{5,1},{6,2},{7,3},{8,12},{9,13},{10,... | collective-permute-start | bytes 1769480 | tf_op jit(solution)/shard_map/ppermute | solution.py:974
  34.5 9.5 %collective-permute-start.27 = (bf16[192,768]{1,0:T(8,128)(2,1)S(1)}, bf16[192,768]{1,0:T(8,128)(2,1)S(1)}, u32[]{:S(2)}, u32[]{:S(2)}) collective-permute-start(bf16[192,768]{1,0:T(8,128)(2,1)S(1)} %slice.57), channel_id=1, source_target_pairs={{0,4},{1,5},{2,6},{3,7},{4,0},{5,1},{6,2},{7,3},{8,12},{9,13},{10,... | collective-permute-start | bytes 884744 | tf_op jit(solution)/shard_map/ppermute | solution.py:974
  37.1 8.1 %collective-permute-start.24 = (bf16[384,768]{1,0:T(8,128)(2,1)S(1)}, bf16[384,768]{1,0:T(8,128)(2,1)S(1)}, u32[]{:S(2)}, u32[]{:S(2)}) collective-permute-start(bf16[384,768]{1,0:T(8,128)(2,1)S(1)} %fusion.15.refs_0_), channel_id=1, source_target_pairs={{0,1},{1,0},{2,3},{3,2},{4,5},{5,4},{6,7},{7,6},{8,9},{9,8},{10,11... | collective-permute-start | bytes 1769480 | tf_op jit(solution)/shard_map/ppermute | solution.py:974
  37.2 8.0 %collective-permute-start.25 = (bf16[384,768]{1,0:T(8,128)(2,1)S(1)}, bf16[384,768]{1,0:T(8,128)(2,1)S(1)}, u32[]{:S(2)}, u32[]{:S(2)}) collective-permute-start(bf16[384,768]{1,0:T(8,128)(2,1)S(1)} %collective-permute-done.22.refs_2_), channel_id=1, source_target_pairs={{0,1},{1,0},{2,3},{3,2},{4,5},{5,4},{6,7},{7,6},{8,9},{9,8},{10,11... | collective-permute-start | bytes 1769480 | tf_op jit(solution)/shard_map/ppermute | solution.py:974
  37.7 8.3 %collective-permute-start.26 = (bf16[384,768]{1,0:T(8,128)(2,1)S(1)}, bf16[384,768]{1,0:T(8,128)(2,1)}, u32[]{:S(2)}, u32[]{:S(2)}) collective-permute-start(bf16[384,768]{1,0:T(8,128)(2,1)S(1)} %collective-permute-done.23.refs_4_), channel_id=1, source_target_pairs={{0,1},{1,0},{2,3},{3,2},{4,5},{5,4},{6,7},{7,6},{8,9},{9,8},{10,11... | collective-permute-start | bytes 1769480 | tf_op jit(solution)/shard_map/ppermute | solution.py:974
  97.4 138.8 %all-reduce.3.cloned.1.call-start = ((), (), s32[]{:S(2)}) async-start(), calls=%async_computation.2 | async-start | bytes 1769472 | tf_op jit(solution)/shard_map/psum | solution.py:1299
  120.0 9.7 %collective-permute-start.30 = (bf16[4,192,768]{2,1,0:T(8,128)(2,1)}, bf16[4,192,768]{2,1,0:T(8,128)(2,1)}, u32[]{:S(2)}, u32[]{:S(2)}) collective-permute-start(bf16[4,192,768]{2,1,0:T(8,128)(2,1)} %get-tuple-element.222), channel_id=1, source_target_pairs={{0,1},{1,0},{2,3},{3,2},{4,5},{5,4},{6,7},{7,6},{8,9},{9,8},{10,11... | collective-permute-start | bytes 3538952 | tf_op jit(solution)/shard_map/ppermute | solution.py:974
  132.6 23.2 %collective-permute-start.31 = (bf16[192,768]{1,0:T(8,128)(2,1)S(1)}, bf16[192,768]{1,0:T(8,128)(2,1)}, u32[]{:S(2)}, u32[]{:S(2)}) collective-permute-start(bf16[192,768]{1,0:T(8,128)(2,1)S(1)} %get-tuple-element.240), channel_id=1, source_target_pairs={{0,2},{1,3},{2,0},{3,1},{4,6},{5,7},{6,4},{7,5},{8,10},{9,11},{10,... | collective-permute-start | bytes 884744 | tf_op jit(solution)/shard_map/ppermute | solution.py:974
  133.5 22.3 %collective-permute-start.32 = (bf16[192,768]{1,0:T(8,128)(2,1)S(1)}, bf16[192,768]{1,0:T(8,128)(2,1)}, u32[]{:S(2)}, u32[]{:S(2)}) collective-permute-start(bf16[192,768]{1,0:T(8,128)(2,1)S(1)} %get-tuple-element.241), channel_id=1, source_target_pairs={{0,4},{1,5},{2,6},{3,7},{4,0},{5,1},{6,2},{7,3},{8,12},{9,13},{10,... | collective-permute-start | bytes 884744 | tf_op jit(solution)/shard_map/ppermute | solution.py:974
  134.7 22.8 %collective-permute-start.33 = (bf16[192,768]{1,0:T(8,128)(2,1)S(1)}, bf16[192,768]{1,0:T(8,128)(2,1)}, u32[]{:S(2)}, u32[]{:S(2)}) collective-permute-start(bf16[192,768]{1,0:T(8,128)(2,1)S(1)} %get-tuple-element.242), channel_id=1, source_target_pairs={{0,6},{1,7},{2,4},{3,5},{4,2},{5,3},{6,0},{7,1},{8,14},{9,15},{10,... | collective-permute-start | bytes 884744 | tf_op jit(solution)/shard_map/ppermute | solution.py:974
  157.4 21.8 %collective-permute-start.34 = (bf16[4,144,768]{2,1,0:T(8,128)(2,1)}, bf16[4,144,768]{2,1,0:T(8,128)(2,1)}, u32[]{:S(2)}, u32[]{:S(2)}) collective-permute-start(bf16[4,144,768]{2,1,0:T(8,128)(2,1)} %get-tuple-element.245), channel_id=1, source_target_pairs={{0,1},{1,0},{2,3},{3,2},{4,5},{5,4},{6,7},{7,6},{8,9},{9,8},{10,11... | collective-permute-start | bytes 2654216 | tf_op jit(solution)/shard_map/ppermute | solution.py:974
  159.0 20.3 %collective-permute-start.38 = (bf16[192,768]{1,0:T(8,128)(2,1)S(1)}, bf16[192,768]{1,0:T(8,128)(2,1)S(1)}, u32[]{:S(2)}, u32[]{:S(2)}) collective-permute-start(bf16[192,768]{1,0:T(8,128)(2,1)S(1)} %fusion.18), channel_id=1, source_target_pairs={{0,8},{24,16},{1,9},{25,17},{2,10},{26,18},{3,11},{27,19},{4,12},{... | collective-permute-start | bytes 884744 | tf_op jit(solution)/shard_map/ppermute | solution.py:1065
  181.0 15.4 %collective-permute-start.16 = (bf16[192,768]{1,0:T(8,128)(2,1)}, bf16[192,768]{1,0:T(8,128)(2,1)S(1)}, u32[]{:S(2)}, u32[]{:S(2)}) collective-permute-start(bf16[192,768]{1,0:T(8,128)(2,1)} %add_convert_fusion.3), channel_id=1, source_target_pairs={{8,16},{16,8},{9,17},{17,9},{10,18},{18,10},{11,19},{19,11},{12,20... | collective-permute-start | bytes 884744 | tf_op jit(solution)/shard_map/cond/branch_1_fun/ppermute | solution.py:1065
  183.3 11.7 %collective-permute-start.12 = (bf16[144,768]{1,0:T(8,128)(2,1)S(1)}, bf16[144,768]{1,0:T(8,128)(2,1)}, u32[]{:S(2)}, u32[]{:S(2)}) collective-permute-start(bf16[144,768]{1,0:T(8,128)(2,1)S(1)} %get-tuple-element.76), channel_id=1, source_target_pairs={{0,2},{1,3},{2,0},{3,1},{4,6},{5,7},{6,4},{7,5},{8,10},{9,11},{10,... | collective-permute-start | bytes 663560 | tf_op jit(solution)/shard_map/cond/branch_1_fun/ppermute | solution.py:974
  184.4 10.5 %collective-permute-start.13 = (bf16[144,768]{1,0:T(8,128)(2,1)S(1)}, bf16[144,768]{1,0:T(8,128)(2,1)}, u32[]{:S(2)}, u32[]{:S(2)}) collective-permute-start(bf16[144,768]{1,0:T(8,128)(2,1)S(1)} %get-tuple-element.77), channel_id=1, source_target_pairs={{0,4},{1,5},{2,6},{3,7},{4,0},{5,1},{6,2},{7,3},{8,12},{9,13},{10,... | collective-permute-start | bytes 663560 | tf_op jit(solution)/shard_map/cond/branch_1_fun/ppermute | solution.py:974
  185.2 9.8 %collective-permute-start.14 = (bf16[144,768]{1,0:T(8,128)(2,1)S(1)}, bf16[144,768]{1,0:T(8,128)(2,1)}, u32[]{:S(2)}, u32[]{:S(2)}) collective-permute-start(bf16[144,768]{1,0:T(8,128)(2,1)S(1)} %get-tuple-element.78), channel_id=1, source_target_pairs={{0,6},{1,7},{2,4},{3,5},{4,2},{5,3},{6,0},{7,1},{8,14},{9,15},{10,... | collective-permute-start | bytes 663560 | tf_op jit(solution)/shard_map/cond/branch_1_fun/ppermute | solution.py:974
  187.4 7.5 %collective-permute-start.15 = (f32[8,768]{1,0:T(8,128)S(1)}, f32[8,768]{1,0:T(8,128)S(1)}, u32[]{:S(2)}, u32[]{:S(2)}) collective-permute-start(f32[8,768]{1,0:T(8,128)S(1)} %add.135), channel_id=1, source_target_pairs={{0,4},{1,5},{2,6},{3,7},{4,0},{5,1},{6,2},{7,3},{8,12},{9,13},{10,... | collective-permute-start | bytes 73736 | tf_op jit(solution)/shard_map/cond/branch_1_fun/ppermute | solution.py:974
  196.4 11.8 %collective-permute-start.18 = (bf16[144,768]{1,0:T(8,128)(2,1)S(1)}, bf16[144,768]{1,0:T(8,128)(2,1)S(1)}, u32[]{:S(2)}, u32[]{:S(2)}) collective-permute-start(bf16[144,768]{1,0:T(8,128)(2,1)S(1)} %fusion.9), channel_id=1, source_target_pairs={{0,8},{8,0},{16,24},{24,16},{1,9},{9,1},{17,25},{25,17},{2,10},{10... | collective-permute-start | bytes 663560 | tf_op jit(solution)/shard_map/cond/branch_1_fun/ppermute | solution.py:974
  201.2 21.7 %collective-permute-start.19 = (bf16[144,768]{1,0:T(8,128)(2,1)S(1)}, bf16[144,768]{1,0:T(8,128)(2,1)S(1)}, u32[]{:S(2)}, u32[]{:S(2)}) collective-permute-start(bf16[144,768]{1,0:T(8,128)(2,1)S(1)} %fusion.9), channel_id=1, source_target_pairs={{0,16},{8,24},{16,0},{24,8},{1,17},{9,25},{17,1},{25,9},{2,18},{10... | collective-permute-start | bytes 663560 | tf_op jit(solution)/shard_map/cond/branch_1_fun/ppermute | solution.py:974
  204.2 18.7 %collective-permute-start.20 = (bf16[144,768]{1,0:T(8,128)(2,1)S(1)}, bf16[144,768]{1,0:T(8,128)(2,1)S(1)}, u32[]{:S(2)}, u32[]{:S(2)}) collective-permute-start(bf16[144,768]{1,0:T(8,128)(2,1)S(1)} %fusion.9), channel_id=1, source_target_pairs={{0,24},{8,16},{16,8},{24,0},{1,25},{9,17},{17,9},{25,1},{2,26},{10... | collective-permute-start | bytes 663560 | tf_op jit(solution)/shard_map/cond/branch_1_fun/ppermute | solution.py:974
  206.7 26.0 %collective-permute-start.21 = (bf16[192,768]{1,0:T(8,128)(2,1)S(1)}, bf16[192,768]{1,0:T(8,128)(2,1)S(1)}, u32[]{:S(2)}, u32[]{:S(2)}) collective-permute-start(bf16[192,768]{1,0:T(8,128)(2,1)S(1)} %add_convert_fusion.2), channel_id=1, source_target_pairs={{8,0},{16,24},{9,1},{17,25},{10,2},{18,26},{11,3},{19,27},{12,4},{... | collective-permute-start | bytes 884744 | tf_op jit(solution)/shard_map/cond/branch_1_fun/ppermute | solution.py:1065
  (30 other events, 198.8 us)
Sparse Core Ops, SparseCore 0:
  10.5 59.6 all-gather.4
  97.6 76.2 reduce-scatter.1
  179.4 56.7 all-reduce.2

commit v5 on v4

--- a/solution.py
+++ b/solution.py
@@ -234,7 +234,7 @@
 def project(me, layer, tokens, gain, pieces, kinds, w_proj, rows_all, groups, chans):
     rows, width = tokens.shape
     per = rows // groups
-    tile = min(TILE, per)
+    tile = min(2 * TILE, per)
     tiles = per // tile
     rowed = functools.partial(ahead, tiles, tile)
     made = [(5, 8, chans // 8, width), (2, 8, chans // 8, width)] if pieces else []
@@ -276,7 +276,6 @@
         ],
         [pltpu.VMEM((3, CHUNKS, chans), F32)],
         vmem=36,
-        free=range(4, 4 + len(pieces)),
     )(me, layer, tokens, gain, *given)
 
 
@@ -497,6 +496,10 @@
     )
 
 
+def gain_share(grads, w, gain):
+    return jnp.sum(grads * w[...].astype(F32), axis=0, keepdims=True) / gain[...]
+
+
 def mix_back_body(
     steps,
     chans,
@@ -513,6 +516,8 @@
     normed,
     decays,
     w_out,
+    w_proj,
+    mix_gain,
     out_gain,
     ffn_gain,
     angles,
@@ -529,6 +534,7 @@
     carry,
     gated_here,
     normed_here,
+    w_here,
     arrivals,
 ):
     rows_here = steps * CHUNKS
@@ -538,6 +544,7 @@
     fetches = [
         pltpu.make_async_copy(gated, gated_here, arrivals.at[0]),
         pltpu.make_async_copy(normed, normed_here, arrivals.at[1]),
+        pltpu.make_async_copy(w_proj.at[pl.ds(0, 2 * chans)], w_here, arrivals.at[2]),
     ]
 
     @pl.when(first_step())
@@ -602,6 +609,7 @@
         for fetch in fetches:
             fetch.wait()
         grads = [tn(gated_here[...], d_mixes[...]), tn(d_gates[...], normed_here[...])]
+        sums[2:3, :] = gain_share(grads[1], w_here, mix_gain)
         finish_grads(core, grads, 4, chans, unit_chans, same, other)
 
 
@@ -619,6 +627,8 @@
     normed,
     decays,
     w,
+    w_proj,
+    mix_gain,
     out_gain,
     ffn_gain,
     angles,
@@ -646,6 +656,8 @@
             pl.BlockSpec(memory_space=pl.ANY),
             rowed(chans),
             whole((2 * chans, width)),
+            pl.BlockSpec(memory_space=pl.ANY),
+            whole((1, width)),
             whole((1, 2 * chans)),
             whole((1, width)),
             whole(angles.shape),
@@ -674,9 +686,10 @@
             pltpu.VMEM((3, CHUNKS, chans), F32),
             pltpu.VMEM((rows, 2 * chans), BF16),
             pltpu.VMEM((rows, width), BF16),
-            pltpu.SemaphoreType.DMA((2,)),
-        ],
-        vmem=40,
+            pltpu.VMEM((2 * chans, width), BF16),
+            pltpu.SemaphoreType.DMA((3,)),
+        ],
+        vmem=42,
     )(
         core,
         d_pre,
@@ -690,6 +703,8 @@
         normed,
         decays,
         w,
+        w_proj,
+        mix_gain,
         out_gain,
         ffn_gain,
         angles,
@@ -719,19 +734,36 @@
     angles,
     table,
     normed,
+    w_proj,
+    mix_gain,
+    early,
     d_pre,
-    sums,
+    flat,
     same,
     other,
     leaving,
     full,
     d_pres,
     carry,
+    sums,
+    normed_here,
+    w_here,
+    arrivals,
 ):
     g, t = pl.program_id(0), pl.program_id(1)
     tiles = pl.num_programs(1)
     rows_here = steps * CHUNKS
     here = pl.ds(pl.multiple_of((g * tiles + tiles - 1 - t) * rows_here, rows_here), rows_here)
+    fetches = [
+        pltpu.make_async_copy(normed, normed_here, arrivals.at[0]),
+        pltpu.make_async_copy(w_proj.at[pl.ds(2 * chans, 3 * chans)], w_here, arrivals.at[1]),
+    ]
+
+    @pl.when(first_step())
+    def _():
+        sums[...] = jnp.zeros_like(sums)
+        for fetch in fetches:
+            fetch.start()
 
     @pl.when(t == 0)
     def _():
@@ -756,7 +788,6 @@
             leaving[1, s : s + 1, :] = run * flow_im + suffix[0, 2, s : s + 1, :]
             flow_re, flow_im = back_turn(cos_chunk, sin_chunk, flow_re, flow_im)
         carry[...] = jnp.ones_like(carry)
-        sums[...] = jnp.zeros_like(sums)
 
     low = angles[BOUND : BOUND + 1, :]
     cos_one, sin_one = angles[ONE : ONE + 1, :], angles[ONE + 1 : ONE + 2, :]
@@ -796,12 +827,20 @@
     d_all = jnp.concatenate([d_re, d_im, d_forget], axis=1)
     d_pre[...] = d_all
     d_pres[here, :] = d_all
-    sums[0, 0] += jnp.sum((decay * across).reshape(steps, CHUNKS, chans), axis=0)
-    sums[0, 1] += jnp.sum(d_low.reshape(steps, CHUNKS, chans), axis=0)
+    sums[0] += jnp.sum((decay * across).reshape(steps, CHUNKS, chans), axis=0)
+    sums[1] += jnp.sum(d_low.reshape(steps, CHUNKS, chans), axis=0)
 
     @pl.when(last_step())
     def _():
-        finish_grads(core, [tn(d_pres[...], normed[...])], 3, chans, unit_chans, same, other)
+        for fetch in fetches:
+            fetch.wait()
+        grads = tn(d_pres[...], normed_here[...])
+        finish_grads(core, [grads], 3, chans, unit_chans, same, other)
+        flat[...] = jnp.zeros_like(flat)
+        flat[0:1, :] = early[2:3, :] + gain_share(grads, w_here, mix_gain)
+        flat[1:3, :] = early[0:2, :]
+        flat[3:4, 0:chans] = jnp.sum(sums[0], axis=0, keepdims=True)
+        flat[3:4, chans:] = jnp.sum(sums[1], axis=0, keepdims=True)
 
 
 def adjoint_finish(
@@ -819,6 +858,9 @@
     angles,
     table,
     normed,
+    w_proj,
+    mix_gain,
+    early,
     groups,
     chans,
 ):
@@ -850,16 +892,19 @@
             per_group((1, 2, CHUNKS, chans)),
             whole(angles.shape),
             whole(table.shape),
-            whole((rows, width)),
+            pl.BlockSpec(memory_space=pl.ANY),
+            pl.BlockSpec(memory_space=pl.ANY),
+            whole((1, width)),
+            whole(early.shape),
         ],
         [
             rowed(3 * chans),
-            per_group((1, 2, CHUNKS, chans)),
+            kept((8, width)),
             *map(kept, grads_shapes(3, chans, unit_chans, width)),
         ],
         [
             shaped((rows, 3 * chans), BF16),
-            shaped((groups, 2, CHUNKS, chans)),
+            shaped((8, width)),
             *(shaped(shape, BF16) for shape in grads_shapes(3, chans, unit_chans, width)),
         ],
         [
@@ -867,6 +912,10 @@
             pltpu.VMEM((tile, 2 * chans), F32),
             pltpu.VMEM((rows, 3 * chans), BF16),
             pltpu.VMEM((CHUNKS, chans), F32),
+            pltpu.VMEM((2, CHUNKS, chans), F32),
+            pltpu.VMEM((rows, width), BF16),
+            pltpu.VMEM((3 * chans, width), BF16),
+            pltpu.SemaphoreType.DMA((2,)),
         ],
     )(
         me,
@@ -883,27 +932,23 @@
         angles,
         table,
         normed,
+        w_proj,
+        mix_gain,
+        early,
     )
 
 
-def tokens_back_body(chans, d_scan, d_outgate, w, tokens, d_mid, gain, early, scan, grad_tokens, sums):
-    @pl.when(first_step())
-    def _():
-        sums[...] = jnp.zeros_like(sums)
-        sums[1:3, :] = early[0:2, :]
-        sums[3:4, 0:chans] = jnp.sum(scan[:, 0], axis=(0, 1))[None]
-        sums[3:4, chans : 2 * chans] = jnp.sum(scan[:, 1], axis=(0, 1))[None]
-
+def tokens_back_body(chans, d_scan, d_outgate, w, tokens, d_mid, gain, grad_tokens):
     d_normed = nn(d_scan[...], w[2 * chans : 5 * chans, :])
     d_normed += nn(d_outgate[...], w[0 : 2 * chans, :])
     values = tokens[...].astype(F32)
     inv = rms_rows(values)
-    unit = values * inv
-    sums[0:1, :] += jnp.sum(d_normed * unit, axis=0, keepdims=True)
-    grad_tokens[...] = (d_mid[...].astype(F32) + rms_pull(unit, inv, gain[...], d_normed)).astype(BF16)
-
-
-def tokens_back(d_scan, d_outgate, w, tokens, d_mid, gain, early, scan, groups, chans):
+    grad_tokens[...] = (
+        d_mid[...].astype(F32) + rms_pull(values * inv, inv, gain[...], d_normed)
+    ).astype(BF16)
+
+
+def tokens_back(d_scan, d_outgate, w, tokens, d_mid, gain, groups, chans):
     rows, width = tokens.shape
     per = rows // groups
     tile = min(TILE, per)
@@ -919,13 +964,11 @@
             rowed(width),
             rowed(width),
             whole((1, width)),
-            whole(early.shape),
-            whole(scan.shape),
-        ],
-        [rowed(width), kept((8, width))],
-        [Near(shaped((rows, width), BF16)), shaped((8, width))],
+        ],
+        rowed(width),
+        Near(shaped((rows, width), BF16)),
         vmem=20,
-    )(d_scan, d_outgate, w, tokens, d_mid, gain, early, scan)
+    )(d_scan, d_outgate, w, tokens, d_mid, gain)
 
 
 def result_body(act, w_down, mid, result):
@@ -1208,6 +1251,8 @@
         normed,
         decays,
         w_out,
+        w_proj,
+        mix_row,
         gain_row,
         ffn_row,
         angles,
@@ -1225,7 +1270,7 @@
     out_result = from_rows(block_result(act, w_ffn, mid))
     if by_hand:
         back_ends, out_result = tied(back_ends, out_result)
-    d_scan, sums, same, other = adjoint_finish(
+    d_scan, flat, same, other = adjoint_finish(
         chans_dev,
         me_one,
         core_one,
@@ -1240,6 +1285,9 @@
         angles,
         lags,
         normed,
+        w_proj,
+        mix_row,
+        early_sums,
         groups,
         chans,
     )
@@ -1272,11 +1320,11 @@
             flat[1],
         )
 
-    grad_tokens, flat = tokens_back(
-        d_scan, d_outgate, w_proj, tok, d_mid, mix_row, early_sums, sums, groups, chans
-    )
     if by_hand:
         one, two, three = (swap(flat, "dp", bit, layers_z) for bit in (1, 2, 3))
+    grad_tokens = tokens_back(d_scan, d_outgate, w_proj, tok, d_mid, mix_row, groups, chans)
+    if by_hand:
+        grad_tokens, one, two, three = tied(grad_tokens, one, two, three)
         flat, early_got = tied((flat + one) + (two + three), early_got)
         flat, grad_tokens, grad_ffn = late.arrived(flat, grad_tokens, grad_ffn)
         same, got = late.same, late.flying[0]

time: 246 us -> 244 us (level)
  starting transfers between devices: 36.6 us -> 33.5 us
  waiting for transfers between devices: 57.4 us -> 60.3 us
    ppermute x25, starting transfers between devices: 30.7 us -> 26.9 us  [swap(): return lax.ppermute(values, axis, [(i, i ^ bit) for i in range(size)])]
    ppermute x3, waiting for transfers between devices: 8.27 us -> 11.5 us  [along_layers(): return lax.ppermute(share, 'dp', pairs)]
    unnamed x49 -> x53, local copies, waits for them, and re-layouts: 5.25 us -> 3.31 us
  transfers between devices with their start and end apart: 31 -> 31, of which waited for: 12 -> 11; matrix products, arithmetic and copies ran while one was open for 7% -> 7% of each run, Pallas kernels for 28% -> 28%
where the time goes in v5:
time: 244 us; the launch traced here: 243 us
  Pallas kernels  91.1 us (37%)
  waiting for transfers between devices  60.3 us (25%)
  starting transfers between devices  33.5 us (14%)
  blocking collectives  19.5 us (8%)
  local copies, waits for them, and re-layouts  15.4 us (6%)
  between operations  14.9 us (6%)
  other arithmetic  8.41 us (3%)
    pallas_call x8, Pallas kernels, kernel_call(): call(*(arg if at in free else placed(arg) for at, arg in enumerate(args)))  88.2 us
    ppermute x25, waiting for transfers between devices, swap(): return lax.ppermute(values, axis, [(i, i ^ bit) for i in range(size)])  44.4 us
    ppermute x25, starting transfers between devices, swap(): return lax.ppermute(values, axis, [(i, i ^ bit) for i in range(size)])  26.9 us
    ppermute x3, waiting for transfers between devices, along_layers(): return lax.ppermute(share, 'dp', pairs)  11.5 us
    all_gather x1, blocking collectives, shards(): ends = lax.all_gather(totals, 'mp', axis=0)  10.2 us
    all_gather x1, blocking collectives, shards(): back_ends = lax.all_gather(back_totals, 'mp', axis=0)  9.23 us
    ppermute x3, starting transfers between devices, along_layers(): return lax.ppermute(share, 'dp', pairs)  6.29 us
  transfers between devices with their start and end apart: 31, of which 11 were waited for; matrix products, arithmetic and copies ran while one was open for 7% of the time, Pallas kernels for 28%

profile of v5, /device:TPU:0, one launch (start us, length us, event | category | flops | bytes accessed | tf_op | source)
XLA Modules:
  0.0 243.2 jit_solution(2297748802369943399)
XLA Ops:
  10.4 3.0 %collective-permute-start.22 = (bf16[384,768]{1,0:T(8,128)(2,1)S(1)}, bf16[384,768]{1,0:T(8,128)(2,1)S(1)}, u32[]{:S(2)}, u32[]{:S(2)}) collective-permute-start(bf16[384,768]{1,0:T(8,128)(2,1)S(1)} %fusion.15.refs_0_), channel_id=1, source_target_pairs={{0,2},{1,3},{2,0},{3,1},{4,6},{5,7},{6,4},{7,5},{8,10},{9,11},{10,... | collective-permute-start | bytes 1769480 | tf_op jit(solution)/shard_map/ppermute | solution.py:1017
  19.0 12.6 %collective-permute-done.22.refs_2_ = bf16[384,768]{1,0:T(8,128)(2,1)S(1)} collective-permute-done((bf16[384,768]{1,0:T(8,128)(2,1)S(1)}, bf16[384,768]{1,0:T(8,128)(2,1)S(1)}, u32[]{:S(2)}, u32[]{:S(2)}) %collective-permute-start.22) | collective-permute-done | bytes 589856 | tf_op jit(solution)/shard_map/ppermute | solution.py:1017
  31.6 2.8 %collective-permute-done.23.refs_4_ = bf16[384,768]{1,0:T(8,128)(2,1)S(1)} collective-permute-done((bf16[384,768]{1,0:T(8,128)(2,1)S(1)}, bf16[384,768]{1,0:T(8,128)(2,1)S(1)}, u32[]{:S(2)}, u32[]{:S(2)}) %collective-permute-start.23) | collective-permute-done | bytes 589856 | tf_op jit(solution)/shard_map/ppermute | solution.py:1017
  34.5 2.5 %collective-permute-start.27 = (bf16[192,768]{1,0:T(8,128)(2,1)S(1)}, bf16[192,768]{1,0:T(8,128)(2,1)S(1)}, u32[]{:S(2)}, u32[]{:S(2)}) collective-permute-start(bf16[192,768]{1,0:T(8,128)(2,1)S(1)} %slice.57), channel_id=1, source_target_pairs={{0,4},{1,5},{2,6},{3,7},{4,0},{5,1},{6,2},{7,3},{8,12},{9,13},{10,... | collective-permute-start | bytes 884744 | tf_op jit(solution)/shard_map/ppermute | solution.py:1017
  37.8 6.2 %collective-permute-done.27 = bf16[192,768]{1,0:T(8,128)(2,1)S(1)} collective-permute-done((bf16[192,768]{1,0:T(8,128)(2,1)S(1)}, bf16[192,768]{1,0:T(8,128)(2,1)S(1)}, u32[]{:S(2)}, u32[]{:S(2)}) %collective-permute-start.27) | collective-permute-done | bytes 294944 | tf_op jit(solution)/shard_map/ppermute | solution.py:1017
  46.3 12.1 %shard_map.263 = (bf16[1024,768]{1,0:T(8,128)(2,1)}, bf16[1024,1152]{1,0:T(8,128)(2,1)}, bf16[1024,768]{1,0:T(8,128)(2,1)}, f32[1024,768]{1,0:T(8,128)S(1)}, f32...) custom-call(s32[1]{0:T(128)} %bitcast.28.me, ...), custom_call_target="tpu_custom_call" | custom-call | flops 1 | bytes 1 | tf_op jit(solution)/shard_map/pallas_call | solution.py:47
  58.5 10.2 %all-gather = f32[16,8,384]{2,1,0:T(8,128)S(1)} all-gather(f32[2,8,384]{2,1,0:T(8,128)S(1)} %get-tuple-element.204), channel_id=2, replica_groups=mesh['dp'=4,'mp'=8] {'mp'}, dimensions={0}, use_global_device_ids=true | all-gather | bytes 221184 | tf_op jit(solution)/shard_map/all_gather | solution.py:1212
  68.7 7.8 %shard_map.264 = (bf16[1024,768]{1,0:T(8,128)(2,1)}, f32[2,2,8,384]{3,2,1,0:T(8,128)S(1)}, bf16[1024,768]{1,0:T(8,128)(2,1)}, f32[1024,768]{1,0:T(8,128)}, bf16[1024,768]{1,0:T(8,128)(2,1)}) custom-call(s32[1]{0:T(128)} %bitcast.28.me, f32[2,8]{1,0:T(2,128)S(1)} %compare_convert_fusion.2.keep, f32[8,2,8,384]{3,2,1,0:T(8,128)S(1)} %bitcast.100, ...), custom_call_target="tpu_custom_call" | custom-call | flops 1 | bytes 1 | tf_op jit(solution)/shard_map/pallas_call | solution.py:47
  76.5 20.7 %shard_map.265 = (bf16[1024,1536]{1,0:T(8,128)(2,1)}, bf16[1024,3072]{1,0:T(8,128)(2,1)}, bf16[8,576,768]{2,1,0:T(8,128)(2,1)}, bf16[3072,768]{1,0:T(8,128)(2,1)}) custom-call(bf16[1024,768]{1,0:T(8,128)(2,1)} %get-tuple-element.213.x, bf16[1024,768]{1,0:T(8,128)(2,1)} %bitcast.112, bf16[8,3,192,768]{3,2,1,0:T(8,128)(2,1)} %bitcast.107), custom_call_target="tpu_custom_call" | custom-call | flops 1 | bytes 1 | tf_op jit(solution)/shard_map/pallas_call | solution.py:47
  97.5 21.2 %shard_map.266 = (bf16[1024,768]{1,0:T(8,128)(2,1)}, bf16[1024,768]{1,0:T(8,128)(2,1)}, f32[1024,768]{1,0:T(8,128)S(1)}, f32[2,3,8,384]{3,2,1,0:T(8,128)S(1)}, f...) custom-call(s32[1]{0:T(128)} %bitcast.48.core, ...), custom_call_target="tpu_custom_call" | custom-call | flops 1 | bytes 1 | tf_op jit(solution)/shard_map/pallas_call | solution.py:47
  119.6 9.2 %all-gather.2 = f32[16,8,384]{2,1,0:T(8,128)S(1)} all-gather(f32[2,8,384]{2,1,0:T(8,128)} %copy-done.1), channel_id=4, replica_groups=mesh['dp'=4,'mp'=8] {'mp'}, dimensions={0}, use_global_device_ids=true | all-gather | bytes 221184 | tf_op jit(solution)/shard_map/all_gather | solution.py:1266
  135.2 6.1 %shard_map.268 = bf16[1024,768]{1,0:T(8,128)(2,1)S(1)} custom-call(bf16[1024,1536]{1,0:T(8,128)(2,1)} %get-tuple-element.234.act, bf16[8,3,192,768]{3,2,1,0:T(8,128)(2,1)} %bitcast.108, f32[1024,768]{1,0:T(8,128)} %get-tuple-element.235.mid), custom_call_target="tpu_custom_call" | custom-call | flops 1 | bytes 1 | tf_op jit(solution)/shard_map/pallas_call | solution.py:47
  141.3 2.8 %copy.39 = bf16[8,64,2,768]{3,2,1,0:T(2,128)(2,1)} copy(bf16[8,64,2,768]{3,0,1,2:T(8,128)(2,1)S(1)} %bitcast.98) | data formatting | bytes 3145728 | tf_op jit(solution)/shard_map/transpose | solution.py:1168
  144.1 10.0 %shard_map.269 = (bf16[1024,1152]{1,0:T(8,128)(2,1)}, f32[8,768]{1,0:T(8,128)S(1)}, bf16[4,144,768]{2,1,0:T(8,128)(2,1)}, bf16[4,144,768]{2,1,0:T(8,128)(2,1)}) custom-call(s32[1]{0:T(128)} %bitcast.28.me, s32[1]{0:T(128)} %bitcast.48.core, f32[2,8]{1,0:T(2,128)S(1)} %compare_convert_fusion.2.keep, f32[8,2,8,384]{3,2,1,0:T(8,128)S(1)} %bitcast.99, ...), custom_call_target="tpu_custom_call" | custom-call | flops 1 | bytes 1 | tf_op jit(solution)/shard_map/pallas_call | solution.py:47
  159.1 3.6 %collective-permute-start.38 = (bf16[192,768]{1,0:T(8,128)(2,1)S(1)}, bf16[192,768]{1,0:T(8,128)(2,1)S(1)}, u32[]{:S(2)}, u32[]{:S(2)}) collective-permute-start(bf16[192,768]{1,0:T(8,128)(2,1)S(1)} %fusion.18), channel_id=1, source_target_pairs={{0,8},{24,16},{1,9},{25,17},{2,10},{26,18},{3,11},{27,19},{4,12},{... | collective-permute-start | bytes 884744 | tf_op jit(solution)/shard_map/ppermute | solution.py:1108
  162.8 2.9 %collective-permute-start.36 = (f32[8,768]{1,0:T(8,128)S(1)}, f32[8,768]{1,0:T(8,128)S(1)}, u32[]{:S(2)}, u32[]{:S(2)}) collective-permute-start(f32[8,768]{1,0:T(8,128)S(1)} %copy-done.3), channel_id=1, source_target_pairs={{0,16},{8,24},{16,0},{24,8},{1,17},{9,25},{17,1},{25,9},{2,18},{10... | collective-permute-start | bytes 73736 | tf_op jit(solution)/shard_map/ppermute | solution.py:1017
  167.2 7.9 %shard_map.270 = bf16[1024,768]{1,0:T(8,128)(2,1)S(1)} custom-call(bf16[1024,1152]{1,0:T(8,128)(2,1)} %get-tuple-element.255.d_scan, bf16[1024,768]{1,0:T(8,128)(2,1)} %get-tuple-element.256.d_outgate, bf16[1920,768]{1,0:T(8,128)(2,1)} %bitcast.111, bf16[1024,768]{1,0:T(8,128)(2,1)} %bitcast.106, bf16[1024,768]{1,0:T(8,128)(2,1)} %get-tuple-element.257.d_mid, ...), custom_call_target="tpu_custom_call" | custom-call | flops 1 | bytes 1 | tf_op jit(solution)/shard_map/pallas_call | solution.py:47
  175.2 54.7 %conditional.1 = (f32[768]{0:T(1024)S(1)}, f32[768,2,48]{0,2,1:T(8,128)}, f32[768,48]{0,1:T(8,128)}, f32[48]{0:T(128)S(1)}, f32[12,48]{1,0:T(8,128)S(1)}, /*inde...) conditional(s32[]{:T(128)} %bitcast.55, (s32[]{:T(128)}, ...), branch_computations={%region_1.5_spmd, %region_5.9_spmd} | conditional | flops 3379962 | bytes 19026144 | solution.py:1331
  184.1 2.8 %copy.36 = bf16[2,64,8,768]{3,0,1,2:T(2,128)(2,1)} copy(bf16[2,64,8,768]{3,2,1,0:T(8,128)(2,1)S(1)} %bitcast.97) | data formatting | bytes 3145728 | tf_op jit(solution)/shard_map/cond/branch_1_fun/reshape | solution.py:1169
  186.8 4.8 %collective-permute-done.15 = f32[8,768]{1,0:T(8,128)S(1)} collective-permute-done((f32[8,768]{1,0:T(8,128)S(1)}, f32[8,768]{1,0:T(8,128)S(1)}, u32[]{:S(2)}, u32[]{:S(2)}) %collective-permute-start.15) | collective-permute-done | bytes 24608 | tf_op jit(solution)/shard_map/cond/branch_1_fun/ppermute | solution.py:1017
  201.6 7.8 %collective-permute-done.18 = bf16[144,768]{1,0:T(8,128)(2,1)S(1)} collective-permute-done((bf16[144,768]{1,0:T(8,128)(2,1)S(1)}, bf16[144,768]{1,0:T(8,128)(2,1)S(1)}, u32[]{:S(2)}, u32[]{:S(2)}) %collective-permute-start.18) | collective-permute-done | bytes 221216 | tf_op jit(solution)/shard_map/cond/branch_1_fun/ppermute | solution.py:1017
  209.4 6.6 %collective-permute-done.19 = bf16[144,768]{1,0:T(8,128)(2,1)S(1)} collective-permute-done((bf16[144,768]{1,0:T(8,128)(2,1)S(1)}, bf16[144,768]{1,0:T(8,128)(2,1)S(1)}, u32[]{:S(2)}, u32[]{:S(2)}) %collective-permute-start.19) | collective-permute-done | bytes 221216 | tf_op jit(solution)/shard_map/cond/branch_1_fun/ppermute | solution.py:1017
  217.5 11.5 %collective-permute-done.21 = bf16[192,768]{1,0:T(8,128)(2,1)S(1)} collective-permute-done((bf16[192,768]{1,0:T(8,128)(2,1)S(1)}, bf16[192,768]{1,0:T(8,128)(2,1)S(1)}, u32[]{:S(2)}, u32[]{:S(2)}) %collective-permute-start.21) | collective-permute-done | bytes 294944 | tf_op jit(solution)/shard_map/cond/branch_1_fun/ppermute | solution.py:1108
  230.0 4.3 %all-reduce.3.cloned.1.call-done.ffn = bf16[576,768]{1,0:T(8,128)(2,1)} async-done(((bf16[576,768]{1,0:T(8,128)(2,1)}), bf16[576,768]{1,0:T(8,128)(2,1)}) %all-reduce.3.cloned.1.call-update) | async-done | bytes 884752 | tf_op jit(solution)/shard_map/psum | solution.py:1347
  (146 shorter events, 48.6 us)
Async XLA Ops:
  7.2 69.3 %all-gather.5.cloned.1.call-start = ((), (), s32[]{:S(2)}) async-start(), calls=%async_computation.3 | async-start | bytes 7962624 | tf_op jit(solution)/shard_map/all_gather | solution.py:1201
  10.4 164.8 %reduce-scatter.2.cloned.1.call-start = ((), (), s32[]{:S(2)}) async-start(), calls=%async_computation.1 | async-start | bytes 7962624 | tf_op jit(solution)/shard_map/reduce_scatter | solution.py:1044
  10.4 21.2 %collective-permute-start.22 = (bf16[384,768]{1,0:T(8,128)(2,1)S(1)}, bf16[384,768]{1,0:T(8,128)(2,1)S(1)}, u32[]{:S(2)}, u32[]{:S(2)}) collective-permute-start(bf16[384,768]{1,0:T(8,128)(2,1)S(1)} %fusion.15.refs_0_), channel_id=1, source_target_pairs={{0,2},{1,3},{2,0},{3,1},{4,6},{5,7},{6,4},{7,5},{8,10},{9,11},{10,... | collective-permute-start | bytes 1769480 | tf_op jit(solution)/shard_map/ppermute | solution.py:1017
  13.4 21.0 %collective-permute-start.23 = (bf16[384,768]{1,0:T(8,128)(2,1)S(1)}, bf16[384,768]{1,0:T(8,128)(2,1)S(1)}, u32[]{:S(2)}, u32[]{:S(2)}) collective-permute-start(bf16[384,768]{1,0:T(8,128)(2,1)S(1)} %fusion.15.refs_0_), channel_id=1, source_target_pairs={{0,4},{1,5},{2,6},{3,7},{4,0},{5,1},{6,2},{7,3},{8,12},{9,13},{10,... | collective-permute-start | bytes 1769480 | tf_op jit(solution)/shard_map/ppermute | solution.py:1017
  34.5 9.5 %collective-permute-start.27 = (bf16[192,768]{1,0:T(8,128)(2,1)S(1)}, bf16[192,768]{1,0:T(8,128)(2,1)S(1)}, u32[]{:S(2)}, u32[]{:S(2)}) collective-permute-start(bf16[192,768]{1,0:T(8,128)(2,1)S(1)} %slice.57), channel_id=1, source_target_pairs={{0,4},{1,5},{2,6},{3,7},{4,0},{5,1},{6,2},{7,3},{8,12},{9,13},{10,... | collective-permute-start | bytes 884744 | tf_op jit(solution)/shard_map/ppermute | solution.py:1017
  97.3 137.0 %all-reduce.3.cloned.1.call-start = ((), (), s32[]{:S(2)}) async-start(), calls=%async_computation.2 | async-start | bytes 1769472 | tf_op jit(solution)/shard_map/psum | solution.py:1347
  119.3 9.5 %collective-permute-start.30 = (bf16[4,192,768]{2,1,0:T(8,128)(2,1)}, bf16[4,192,768]{2,1,0:T(8,128)(2,1)}, u32[]{:S(2)}, u32[]{:S(2)}) collective-permute-start(bf16[4,192,768]{2,1,0:T(8,128)(2,1)} %get-tuple-element.225), channel_id=1, source_target_pairs={{0,1},{1,0},{2,3},{3,2},{4,5},{5,4},{6,7},{7,6},{8,9},{9,8},{10,11... | collective-permute-start | bytes 3538952 | tf_op jit(solution)/shard_map/ppermute | solution.py:1017
  131.6 23.0 %collective-permute-start.31 = (bf16[192,768]{1,0:T(8,128)(2,1)S(1)}, bf16[192,768]{1,0:T(8,128)(2,1)}, u32[]{:S(2)}, u32[]{:S(2)}) collective-permute-start(bf16[192,768]{1,0:T(8,128)(2,1)S(1)} %get-tuple-element.244), channel_id=1, source_target_pairs={{0,2},{1,3},{2,0},{3,1},{4,6},{5,7},{6,4},{7,5},{8,10},{9,11},{10,... | collective-permute-start | bytes 884744 | tf_op jit(solution)/shard_map/ppermute | solution.py:1017
  132.6 22.1 %collective-permute-start.32 = (bf16[192,768]{1,0:T(8,128)(2,1)S(1)}, bf16[192,768]{1,0:T(8,128)(2,1)}, u32[]{:S(2)}, u32[]{:S(2)}) collective-permute-start(bf16[192,768]{1,0:T(8,128)(2,1)S(1)} %get-tuple-element.245), channel_id=1, source_target_pairs={{0,4},{1,5},{2,6},{3,7},{4,0},{5,1},{6,2},{7,3},{8,12},{9,13},{10,... | collective-permute-start | bytes 884744 | tf_op jit(solution)/shard_map/ppermute | solution.py:1017
  133.7 23.1 %collective-permute-start.33 = (bf16[192,768]{1,0:T(8,128)(2,1)S(1)}, bf16[192,768]{1,0:T(8,128)(2,1)S(1)}, u32[]{:S(2)}, u32[]{:S(2)}) collective-permute-start(bf16[192,768]{1,0:T(8,128)(2,1)S(1)} %get-tuple-element.246), channel_id=1, source_target_pairs={{0,6},{1,7},{2,4},{3,5},{4,2},{5,3},{6,0},{7,1},{8,14},{9,15},{10,... | collective-permute-start | bytes 884744 | tf_op jit(solution)/shard_map/ppermute | solution.py:1017
  157.6 17.6 %collective-permute-start.34 = (bf16[4,144,768]{2,1,0:T(8,128)(2,1)}, bf16[4,144,768]{2,1,0:T(8,128)(2,1)}, u32[]{:S(2)}, u32[]{:S(2)}) collective-permute-start(bf16[4,144,768]{2,1,0:T(8,128)(2,1)} %get-tuple-element.249), channel_id=1, source_target_pairs={{0,1},{1,0},{2,3},{3,2},{4,5},{5,4},{6,7},{7,6},{8,9},{9,8},{10,11... | collective-permute-start | bytes 2654216 | tf_op jit(solution)/shard_map/ppermute | solution.py:1017
  159.1 16.1 %collective-permute-start.38 = (bf16[192,768]{1,0:T(8,128)(2,1)S(1)}, bf16[192,768]{1,0:T(8,128)(2,1)S(1)}, u32[]{:S(2)}, u32[]{:S(2)}) collective-permute-start(bf16[192,768]{1,0:T(8,128)(2,1)S(1)} %fusion.18), channel_id=1, source_target_pairs={{0,8},{24,16},{1,9},{25,17},{2,10},{26,18},{3,11},{27,19},{4,12},{... | collective-permute-start | bytes 884744 | tf_op jit(solution)/shard_map/ppermute | solution.py:1108
  162.7 12.4 %collective-permute-start.35 = (f32[8,768]{1,0:T(8,128)S(1)}, f32[8,768]{1,0:T(8,128)S(1)}, u32[]{:S(2)}, u32[]{:S(2)}) collective-permute-start(f32[8,768]{1,0:T(8,128)S(1)} %copy-done.3), channel_id=1, source_target_pairs={{0,8},{8,0},{16,24},{24,16},{1,9},{9,1},{17,25},{25,17},{2,10},{10... | collective-permute-start | bytes 73736 | tf_op jit(solution)/shard_map/ppermute | solution.py:1017
  162.8 12.3 %collective-permute-start.36 = (f32[8,768]{1,0:T(8,128)S(1)}, f32[8,768]{1,0:T(8,128)S(1)}, u32[]{:S(2)}, u32[]{:S(2)}) collective-permute-start(f32[8,768]{1,0:T(8,128)S(1)} %copy-done.3), channel_id=1, source_target_pairs={{0,16},{8,24},{16,0},{24,8},{1,17},{9,25},{17,1},{25,9},{2,18},{10... | collective-permute-start | bytes 73736 | tf_op jit(solution)/shard_map/ppermute | solution.py:1017
  165.7 9.4 %collective-permute-start.37 = (f32[8,768]{1,0:T(8,128)S(1)}, f32[8,768]{1,0:T(8,128)S(1)}, u32[]{:S(2)}, u32[]{:S(2)}) collective-permute-start(f32[8,768]{1,0:T(8,128)S(1)} %copy-done.3), channel_id=1, source_target_pairs={{0,24},{8,16},{16,8},{24,0},{1,25},{9,17},{17,9},{25,1},{2,26},{10... | collective-permute-start | bytes 73736 | tf_op jit(solution)/shard_map/ppermute | solution.py:1017
  176.0 17.1 %collective-permute-start.16 = (bf16[192,768]{1,0:T(8,128)(2,1)S(1)}, bf16[192,768]{1,0:T(8,128)(2,1)}, u32[]{:S(2)}, u32[]{:S(2)}) collective-permute-start(bf16[192,768]{1,0:T(8,128)(2,1)S(1)} %add_convert_fusion.3), channel_id=1, source_target_pairs={{8,16},{16,8},{9,17},{17,9},{10,18},{18,10},{11,19},{19,11},{12,20... | collective-permute-start | bytes 884744 | tf_op jit(solution)/shard_map/cond/branch_1_fun/ppermute | solution.py:1108
  179.2 12.5 %collective-permute-start.12 = (bf16[144,768]{1,0:T(8,128)(2,1)S(1)}, bf16[144,768]{1,0:T(8,128)(2,1)}, u32[]{:S(2)}, u32[]{:S(2)}) collective-permute-start(bf16[144,768]{1,0:T(8,128)(2,1)S(1)} %get-tuple-element.76), channel_id=1, source_target_pairs={{0,2},{1,3},{2,0},{3,1},{4,6},{5,7},{6,4},{7,5},{8,10},{9,11},{10,... | collective-permute-start | bytes 663560 | tf_op jit(solution)/shard_map/cond/branch_1_fun/ppermute | solution.py:1017
  180.3 11.4 %collective-permute-start.13 = (bf16[144,768]{1,0:T(8,128)(2,1)S(1)}, bf16[144,768]{1,0:T(8,128)(2,1)}, u32[]{:S(2)}, u32[]{:S(2)}) collective-permute-start(bf16[144,768]{1,0:T(8,128)(2,1)S(1)} %get-tuple-element.77), channel_id=1, source_target_pairs={{0,4},{1,5},{2,6},{3,7},{4,0},{5,1},{6,2},{7,3},{8,12},{9,13},{10,... | collective-permute-start | bytes 663560 | tf_op jit(solution)/shard_map/cond/branch_1_fun/ppermute | solution.py:1017
  180.9 10.8 %collective-permute-start.14 = (bf16[144,768]{1,0:T(8,128)(2,1)S(1)}, bf16[144,768]{1,0:T(8,128)(2,1)}, u32[]{:S(2)}, u32[]{:S(2)}) collective-permute-start(bf16[144,768]{1,0:T(8,128)(2,1)S(1)} %get-tuple-element.78), channel_id=1, source_target_pairs={{0,6},{1,7},{2,4},{3,5},{4,2},{5,3},{6,0},{7,1},{8,14},{9,15},{10,... | collective-permute-start | bytes 663560 | tf_op jit(solution)/shard_map/cond/branch_1_fun/ppermute | solution.py:1017
  183.3 8.3 %collective-permute-start.15 = (f32[8,768]{1,0:T(8,128)S(1)}, f32[8,768]{1,0:T(8,128)S(1)}, u32[]{:S(2)}, u32[]{:S(2)}) collective-permute-start(f32[8,768]{1,0:T(8,128)S(1)} %add.135), channel_id=1, source_target_pairs={{0,4},{1,5},{2,6},{3,7},{4,0},{5,1},{6,2},{7,3},{8,12},{9,13},{10,... | collective-permute-start | bytes 73736 | tf_op jit(solution)/shard_map/cond/branch_1_fun/ppermute | solution.py:1017
  193.1 16.3 %collective-permute-start.18 = (bf16[144,768]{1,0:T(8,128)(2,1)S(1)}, bf16[144,768]{1,0:T(8,128)(2,1)S(1)}, u32[]{:S(2)}, u32[]{:S(2)}) collective-permute-start(bf16[144,768]{1,0:T(8,128)(2,1)S(1)} %fusion.9), channel_id=1, source_target_pairs={{0,8},{8,0},{16,24},{24,16},{1,9},{9,1},{17,25},{25,17},{2,10},{10... | collective-permute-start | bytes 663560 | tf_op jit(solution)/shard_map/cond/branch_1_fun/ppermute | solution.py:1017
  195.1 20.9 %collective-permute-start.19 = (bf16[144,768]{1,0:T(8,128)(2,1)S(1)}, bf16[144,768]{1,0:T(8,128)(2,1)S(1)}, u32[]{:S(2)}, u32[]{:S(2)}) collective-permute-start(bf16[144,768]{1,0:T(8,128)(2,1)S(1)} %fusion.9), channel_id=1, source_target_pairs={{0,16},{8,24},{16,0},{24,8},{1,17},{9,25},{17,1},{25,9},{2,18},{10... | collective-permute-start | bytes 663560 | tf_op jit(solution)/shard_map/cond/branch_1_fun/ppermute | solution.py:1017
  197.6 18.4 %collective-permute-start.20 = (bf16[144,768]{1,0:T(8,128)(2,1)S(1)}, bf16[144,768]{1,0:T(8,128)(2,1)S(1)}, u32[]{:S(2)}, u32[]{:S(2)}) collective-permute-start(bf16[144,768]{1,0:T(8,128)(2,1)S(1)} %fusion.9), channel_id=1, source_target_pairs={{0,24},{8,16},{16,8},{24,0},{1,25},{9,17},{17,9},{25,1},{2,26},{10... | collective-permute-start | bytes 663560 | tf_op jit(solution)/shard_map/cond/branch_1_fun/ppermute | solution.py:1017
  200.1 28.9 %collective-permute-start.21 = (bf16[192,768]{1,0:T(8,128)(2,1)S(1)}, bf16[192,768]{1,0:T(8,128)(2,1)S(1)}, u32[]{:S(2)}, u32[]{:S(2)}) collective-permute-start(bf16[192,768]{1,0:T(8,128)(2,1)S(1)} %add_convert_fusion.2), channel_id=1, source_target_pairs={{8,0},{16,24},{9,1},{17,25},{10,2},{18,26},{11,3},{19,27},{12,4},{... | collective-permute-start | bytes 884744 | tf_op jit(solution)/shard_map/cond/branch_1_fun/ppermute | solution.py:1108
  (32 other events, 248.7 us)
Sparse Core Ops, SparseCore 0:
  10.5 59.6 all-gather.4
  97.4 75.9 reduce-scatter.1
  175.9 58.2 all-reduce.2

commit v6 on v5

--- a/solution.py
+++ b/solution.py
@@ -406,8 +406,13 @@
             other[chip, rows, :] = jnp.where(first, odd, even)
 
 
-def swiglu_body(unit, tile, x, up, w, act, d_pre, grads, w_out):
+def swiglu_body(unit, tile, x, up_all, w, act, d_pre, grads, w_out, up, arrival):
     devices = w.shape[0]
+    fetch = pltpu.make_async_copy(up_all, up, arrival)
+
+    @pl.when(pl.program_id(0) == 0)
+    def _():
+        fetch.start()
 
     def every(part):
         return jnp.concatenate([w[dev, part] for dev in range(devices)], axis=0)
@@ -419,6 +424,12 @@
     for start in range(0, x.shape[0], tile):
         rows = slice(start, start + tile)
         pre = nt(x[rows, :], w_pre)
+        if start == 0:
+
+            @pl.when(pl.program_id(0) == 0)
+            def _():
+                fetch.wait()
+
         d_hidden = nt(up[rows, :], w_down)
         gate, lift = pre[:, :span], pre[:, span:]
         sigma = sigmoid(gate)
@@ -452,7 +463,7 @@
         (blocks // devices,),
         [
             whole((rows, width)),
-            whole((rows, width)),
+            pl.BlockSpec(memory_space=pl.ANY),
             pl.BlockSpec((devices, 3, unit, width), lambda q: (q, 0, 0, 0)),
         ],
         [
@@ -467,6 +478,7 @@
             shaped((blocks, 3 * unit, width), BF16),
             shaped((2 * blocks * unit, width), BF16),
         ],
+        [pltpu.VMEM((rows, width), BF16), pltpu.SemaphoreType.DMA],
     )(x, up, w)
 
 

time: 244 us -> 246 us (level)
  no operation moved by 1% of the time
where the time goes in v6:
time: 246 us
  Pallas kernels  93.5 us (38%)
  waiting for transfers between devices  60.3 us (25%)
  starting transfers between devices  33.5 us (14%)
  blocking collectives  19.5 us (8%)
  local copies, waits for them, and re-layouts  15.4 us (6%)
  between operations  14.9 us (6%)
  other arithmetic  8.41 us (3%)
    pallas_call x8, Pallas kernels, kernel_call(): call(*(arg if at in free else placed(arg) for at, arg in enumerate(args)))  90.6 us
    ppermute x25, waiting for transfers between devices, swap(): return lax.ppermute(values, axis, [(i, i ^ bit) for i in range(size)])  46 us
    ppermute x25, starting transfers between devices, swap(): return lax.ppermute(values, axis, [(i, i ^ bit) for i in range(size)])  27 us
    all_gather x1, blocking collectives, shards(): ends = lax.all_gather(totals, 'mp', axis=0)  10.2 us
    ppermute x3, waiting for transfers between devices, along_layers(): return lax.ppermute(share, 'dp', pairs)  10.2 us
    all_gather x1, blocking collectives, shards(): back_ends = lax.all_gather(back_totals, 'mp', axis=0)  9.2 us
    ppermute x3, starting transfers between devices, along_layers(): return lax.ppermute(share, 'dp', pairs)  6.29 us
  transfers between devices with their start and end apart: 31, of which 11 were waited for; matrix products, arithmetic and copies ran while one was open for 7% of the time, Pallas kernels for 28%

profile of v6, /device:TPU:0, one launch (start us, length us, event | category | flops | bytes accessed | tf_op | source)
XLA Modules:
  0.0 245.6 jit_solution(1409529072529380043)
XLA Ops:
  10.4 3.0 %collective-permute-start.22 = (bf16[384,768]{1,0:T(8,128)(2,1)S(1)}, bf16[384,768]{1,0:T(8,128)(2,1)S(1)}, u32[]{:S(2)}, u32[]{:S(2)}) collective-permute-start(bf16[384,768]{1,0:T(8,128)(2,1)S(1)} %fusion.15.refs_0_), channel_id=1, source_target_pairs={{0,2},{1,3},{2,0},{3,1},{4,6},{5,7},{6,4},{7,5},{8,10},{9,11},{10,... | collective-permute-start | bytes 1769480 | tf_op jit(solution)/shard_map/ppermute | solution.py:1029
  19.0 12.6 %collective-permute-done.22.refs_2_ = bf16[384,768]{1,0:T(8,128)(2,1)S(1)} collective-permute-done((bf16[384,768]{1,0:T(8,128)(2,1)S(1)}, bf16[384,768]{1,0:T(8,128)(2,1)S(1)}, u32[]{:S(2)}, u32[]{:S(2)}) %collective-permute-start.22) | collective-permute-done | bytes 589856 | tf_op jit(solution)/shard_map/ppermute | solution.py:1029
  31.6 2.8 %collective-permute-done.23.refs_4_ = bf16[384,768]{1,0:T(8,128)(2,1)S(1)} collective-permute-done((bf16[384,768]{1,0:T(8,128)(2,1)S(1)}, bf16[384,768]{1,0:T(8,128)(2,1)S(1)}, u32[]{:S(2)}, u32[]{:S(2)}) %collective-permute-start.23) | collective-permute-done | bytes 589856 | tf_op jit(solution)/shard_map/ppermute | solution.py:1029
  34.5 2.5 %collective-permute-start.27 = (bf16[192,768]{1,0:T(8,128)(2,1)S(1)}, bf16[192,768]{1,0:T(8,128)(2,1)S(1)}, u32[]{:S(2)}, u32[]{:S(2)}) collective-permute-start(bf16[192,768]{1,0:T(8,128)(2,1)S(1)} %slice.57), channel_id=1, source_target_pairs={{0,4},{1,5},{2,6},{3,7},{4,0},{5,1},{6,2},{7,3},{8,12},{9,13},{10,... | collective-permute-start | bytes 884744 | tf_op jit(solution)/shard_map/ppermute | solution.py:1029
  37.8 6.2 %collective-permute-done.27 = bf16[192,768]{1,0:T(8,128)(2,1)S(1)} collective-permute-done((bf16[192,768]{1,0:T(8,128)(2,1)S(1)}, bf16[192,768]{1,0:T(8,128)(2,1)S(1)}, u32[]{:S(2)}, u32[]{:S(2)}) %collective-permute-start.27) | collective-permute-done | bytes 294944 | tf_op jit(solution)/shard_map/ppermute | solution.py:1029
  46.3 12.1 %shard_map.263 = (bf16[1024,768]{1,0:T(8,128)(2,1)}, bf16[1024,1152]{1,0:T(8,128)(2,1)}, bf16[1024,768]{1,0:T(8,128)(2,1)}, f32[1024,768]{1,0:T(8,128)S(1)}, f32...) custom-call(s32[1]{0:T(128)} %bitcast.28.me, ...), custom_call_target="tpu_custom_call" | custom-call | flops 1 | bytes 1 | tf_op jit(solution)/shard_map/pallas_call | solution.py:47
  58.5 10.2 %all-gather = f32[16,8,384]{2,1,0:T(8,128)S(1)} all-gather(f32[2,8,384]{2,1,0:T(8,128)S(1)} %get-tuple-element.204), channel_id=2, replica_groups=mesh['dp'=4,'mp'=8] {'mp'}, dimensions={0}, use_global_device_ids=true | all-gather | bytes 221184 | tf_op jit(solution)/shard_map/all_gather | solution.py:1224
  68.7 7.8 %shard_map.264 = (bf16[1024,768]{1,0:T(8,128)(2,1)}, f32[2,2,8,384]{3,2,1,0:T(8,128)S(1)}, bf16[1024,768]{1,0:T(8,128)(2,1)}, f32[1024,768]{1,0:T(8,128)}, bf16[1024,768]{1,0:T(8,128)(2,1)}) custom-call(s32[1]{0:T(128)} %bitcast.28.me, f32[2,8]{1,0:T(2,128)S(1)} %compare_convert_fusion.2.keep, f32[8,2,8,384]{3,2,1,0:T(8,128)S(1)} %bitcast.100, ...), custom_call_target="tpu_custom_call" | custom-call | flops 1 | bytes 1 | tf_op jit(solution)/shard_map/pallas_call | solution.py:47
  76.5 23.1 %shard_map.265 = (bf16[1024,1536]{1,0:T(8,128)(2,1)}, bf16[1024,3072]{1,0:T(8,128)(2,1)}, bf16[8,576,768]{2,1,0:T(8,128)(2,1)}, bf16[3072,768]{1,0:T(8,128)(2,1)}) custom-call(bf16[1024,768]{1,0:T(8,128)(2,1)} %get-tuple-element.213.x, bf16[1024,768]{1,0:T(8,128)(2,1)} %bitcast.112, bf16[8,3,192,768]{3,2,1,0:T(8,128)(2,1)} %bitcast.107), custom_call_target="tpu_custom_call" | custom-call | flops 1 | bytes 1 | tf_op jit(solution)/shard_map/pallas_call | solution.py:47
  99.9 21.2 %shard_map.266 = (bf16[1024,768]{1,0:T(8,128)(2,1)}, bf16[1024,768]{1,0:T(8,128)(2,1)}, f32[1024,768]{1,0:T(8,128)S(1)}, f32[2,3,8,384]{3,2,1,0:T(8,128)S(1)}, f...) custom-call(s32[1]{0:T(128)} %bitcast.48.core, ...), custom_call_target="tpu_custom_call" | custom-call | flops 1 | bytes 1 | tf_op jit(solution)/shard_map/pallas_call | solution.py:47
  122.0 9.2 %all-gather.2 = f32[16,8,384]{2,1,0:T(8,128)S(1)} all-gather(f32[2,8,384]{2,1,0:T(8,128)} %copy-done.1), channel_id=4, replica_groups=mesh['dp'=4,'mp'=8] {'mp'}, dimensions={0}, use_global_device_ids=true | all-gather | bytes 221184 | tf_op jit(solution)/shard_map/all_gather | solution.py:1278
  137.6 6.1 %shard_map.268 = bf16[1024,768]{1,0:T(8,128)(2,1)S(1)} custom-call(bf16[1024,1536]{1,0:T(8,128)(2,1)} %get-tuple-element.234.act, bf16[8,3,192,768]{3,2,1,0:T(8,128)(2,1)} %bitcast.108, f32[1024,768]{1,0:T(8,128)} %get-tuple-element.235.mid), custom_call_target="tpu_custom_call" | custom-call | flops 1 | bytes 1 | tf_op jit(solution)/shard_map/pallas_call | solution.py:47
  143.7 2.8 %copy.39 = bf16[8,64,2,768]{3,2,1,0:T(2,128)(2,1)} copy(bf16[8,64,2,768]{3,0,1,2:T(8,128)(2,1)S(1)} %bitcast.98) | data formatting | bytes 3145728 | tf_op jit(solution)/shard_map/transpose | solution.py:1180
  146.5 10.0 %shard_map.269 = (bf16[1024,1152]{1,0:T(8,128)(2,1)}, f32[8,768]{1,0:T(8,128)S(1)}, bf16[4,144,768]{2,1,0:T(8,128)(2,1)}, bf16[4,144,768]{2,1,0:T(8,128)(2,1)}) custom-call(s32[1]{0:T(128)} %bitcast.28.me, s32[1]{0:T(128)} %bitcast.48.core, f32[2,8]{1,0:T(2,128)S(1)} %compare_convert_fusion.2.keep, f32[8,2,8,384]{3,2,1,0:T(8,128)S(1)} %bitcast.99, ...), custom_call_target="tpu_custom_call" | custom-call | flops 1 | bytes 1 | tf_op jit(solution)/shard_map/pallas_call | solution.py:47
  161.5 3.6 %collective-permute-start.38 = (bf16[192,768]{1,0:T(8,128)(2,1)S(1)}, bf16[192,768]{1,0:T(8,128)(2,1)S(1)}, u32[]{:S(2)}, u32[]{:S(2)}) collective-permute-start(bf16[192,768]{1,0:T(8,128)(2,1)S(1)} %fusion.18), channel_id=1, source_target_pairs={{0,8},{24,16},{1,9},{25,17},{2,10},{26,18},{3,11},{27,19},{4,12},{... | collective-permute-start | bytes 884744 | tf_op jit(solution)/shard_map/ppermute | solution.py:1120
  165.2 2.9 %collective-permute-start.36 = (f32[8,768]{1,0:T(8,128)S(1)}, f32[8,768]{1,0:T(8,128)S(1)}, u32[]{:S(2)}, u32[]{:S(2)}) collective-permute-start(f32[8,768]{1,0:T(8,128)S(1)} %copy-done.3), channel_id=1, source_target_pairs={{0,16},{8,24},{16,0},{24,8},{1,17},{9,25},{17,1},{25,9},{2,18},{10... | collective-permute-start | bytes 73736 | tf_op jit(solution)/shard_map/ppermute | solution.py:1029
  169.6 7.9 %shard_map.270 = bf16[1024,768]{1,0:T(8,128)(2,1)S(1)} custom-call(bf16[1024,1152]{1,0:T(8,128)(2,1)} %get-tuple-element.255.d_scan, bf16[1024,768]{1,0:T(8,128)(2,1)} %get-tuple-element.256.d_outgate, bf16[1920,768]{1,0:T(8,128)(2,1)} %bitcast.111, bf16[1024,768]{1,0:T(8,128)(2,1)} %bitcast.106, bf16[1024,768]{1,0:T(8,128)(2,1)} %get-tuple-element.257.d_mid, ...), custom_call_target="tpu_custom_call" | custom-call | flops 1 | bytes 1 | tf_op jit(solution)/shard_map/pallas_call | solution.py:47
  177.7 54.9 %conditional.1 = (f32[768]{0:T(1024)S(1)}, f32[768,2,48]{0,2,1:T(8,128)}, f32[768,48]{0,1:T(8,128)}, f32[48]{0:T(128)S(1)}, f32[12,48]{1,0:T(8,128)S(1)}, /*inde...) conditional(s32[]{:T(128)} %bitcast.55, (s32[]{:T(128)}, ...), branch_computations={%region_1.5_spmd, %region_5.9_spmd} | conditional | flops 3379962 | bytes 19026144 | solution.py:1343
  186.5 2.8 %copy.36 = bf16[2,64,8,768]{3,0,1,2:T(2,128)(2,1)} copy(bf16[2,64,8,768]{3,2,1,0:T(8,128)(2,1)S(1)} %bitcast.97) | data formatting | bytes 3145728 | tf_op jit(solution)/shard_map/cond/branch_1_fun/reshape | solution.py:1181
  189.2 4.8 %collective-permute-done.15 = f32[8,768]{1,0:T(8,128)S(1)} collective-permute-done((f32[8,768]{1,0:T(8,128)S(1)}, f32[8,768]{1,0:T(8,128)S(1)}, u32[]{:S(2)}, u32[]{:S(2)}) %collective-permute-start.15) | collective-permute-done | bytes 24608 | tf_op jit(solution)/shard_map/cond/branch_1_fun/ppermute | solution.py:1029
  204.1 7.7 %collective-permute-done.18 = bf16[144,768]{1,0:T(8,128)(2,1)S(1)} collective-permute-done((bf16[144,768]{1,0:T(8,128)(2,1)S(1)}, bf16[144,768]{1,0:T(8,128)(2,1)S(1)}, u32[]{:S(2)}, u32[]{:S(2)}) %collective-permute-start.18) | collective-permute-done | bytes 221216 | tf_op jit(solution)/shard_map/cond/branch_1_fun/ppermute | solution.py:1029
  211.8 8.1 %collective-permute-done.19 = bf16[144,768]{1,0:T(8,128)(2,1)S(1)} collective-permute-done((bf16[144,768]{1,0:T(8,128)(2,1)S(1)}, bf16[144,768]{1,0:T(8,128)(2,1)S(1)}, u32[]{:S(2)}, u32[]{:S(2)}) %collective-permute-start.19) | collective-permute-done | bytes 221216 | tf_op jit(solution)/shard_map/cond/branch_1_fun/ppermute | solution.py:1029
  221.5 10.2 %collective-permute-done.21 = bf16[192,768]{1,0:T(8,128)(2,1)S(1)} collective-permute-done((bf16[192,768]{1,0:T(8,128)(2,1)S(1)}, bf16[192,768]{1,0:T(8,128)(2,1)S(1)}, u32[]{:S(2)}, u32[]{:S(2)}) %collective-permute-start.21) | collective-permute-done | bytes 294944 | tf_op jit(solution)/shard_map/cond/branch_1_fun/ppermute | solution.py:1120
  232.6 4.0 %all-reduce.3.cloned.1.call-done.ffn = bf16[576,768]{1,0:T(8,128)(2,1)} async-done(((bf16[576,768]{1,0:T(8,128)(2,1)}), bf16[576,768]{1,0:T(8,128)(2,1)}) %all-reduce.3.cloned.1.call-update) | async-done | bytes 884752 | tf_op jit(solution)/shard_map/psum | solution.py:1359
  (146 shorter events, 48.7 us)
Async XLA Ops:
  7.2 69.3 %all-gather.5.cloned.1.call-start = ((), (), s32[]{:S(2)}) async-start(), calls=%async_computation.3 | async-start | bytes 7962624 | tf_op jit(solution)/shard_map/all_gather | solution.py:1213
  10.4 167.2 %reduce-scatter.2.cloned.1.call-start = ((), (), s32[]{:S(2)}) async-start(), calls=%async_computation.1 | async-start | bytes 7962624 | tf_op jit(solution)/shard_map/reduce_scatter | solution.py:1056
  10.4 21.2 %collective-permute-start.22 = (bf16[384,768]{1,0:T(8,128)(2,1)S(1)}, bf16[384,768]{1,0:T(8,128)(2,1)S(1)}, u32[]{:S(2)}, u32[]{:S(2)}) collective-permute-start(bf16[384,768]{1,0:T(8,128)(2,1)S(1)} %fusion.15.refs_0_), channel_id=1, source_target_pairs={{0,2},{1,3},{2,0},{3,1},{4,6},{5,7},{6,4},{7,5},{8,10},{9,11},{10,... | collective-permute-start | bytes 1769480 | tf_op jit(solution)/shard_map/ppermute | solution.py:1029
  13.4 21.0 %collective-permute-start.23 = (bf16[384,768]{1,0:T(8,128)(2,1)S(1)}, bf16[384,768]{1,0:T(8,128)(2,1)S(1)}, u32[]{:S(2)}, u32[]{:S(2)}) collective-permute-start(bf16[384,768]{1,0:T(8,128)(2,1)S(1)} %fusion.15.refs_0_), channel_id=1, source_target_pairs={{0,4},{1,5},{2,6},{3,7},{4,0},{5,1},{6,2},{7,3},{8,12},{9,13},{10,... | collective-permute-start | bytes 1769480 | tf_op jit(solution)/shard_map/ppermute | solution.py:1029
  34.5 9.5 %collective-permute-start.27 = (bf16[192,768]{1,0:T(8,128)(2,1)S(1)}, bf16[192,768]{1,0:T(8,128)(2,1)S(1)}, u32[]{:S(2)}, u32[]{:S(2)}) collective-permute-start(bf16[192,768]{1,0:T(8,128)(2,1)S(1)} %slice.57), channel_id=1, source_target_pairs={{0,4},{1,5},{2,6},{3,7},{4,0},{5,1},{6,2},{7,3},{8,12},{9,13},{10,... | collective-permute-start | bytes 884744 | tf_op jit(solution)/shard_map/ppermute | solution.py:1029
  99.7 137.0 %all-reduce.3.cloned.1.call-start = ((), (), s32[]{:S(2)}) async-start(), calls=%async_computation.2 | async-start | bytes 1769472 | tf_op jit(solution)/shard_map/psum | solution.py:1359
  121.7 9.5 %collective-permute-start.30 = (bf16[4,192,768]{2,1,0:T(8,128)(2,1)}, bf16[4,192,768]{2,1,0:T(8,128)(2,1)}, u32[]{:S(2)}, u32[]{:S(2)}) collective-permute-start(bf16[4,192,768]{2,1,0:T(8,128)(2,1)} %get-tuple-element.225), channel_id=1, source_target_pairs={{0,1},{1,0},{2,3},{3,2},{4,5},{5,4},{6,7},{7,6},{8,9},{9,8},{10,11... | collective-permute-start | bytes 3538952 | tf_op jit(solution)/shard_map/ppermute | solution.py:1029
  134.0 23.0 %collective-permute-start.31 = (bf16[192,768]{1,0:T(8,128)(2,1)S(1)}, bf16[192,768]{1,0:T(8,128)(2,1)}, u32[]{:S(2)}, u32[]{:S(2)}) collective-permute-start(bf16[192,768]{1,0:T(8,128)(2,1)S(1)} %get-tuple-element.244), channel_id=1, source_target_pairs={{0,2},{1,3},{2,0},{3,1},{4,6},{5,7},{6,4},{7,5},{8,10},{9,11},{10,... | collective-permute-start | bytes 884744 | tf_op jit(solution)/shard_map/ppermute | solution.py:1029
  135.0 22.0 %collective-permute-start.32 = (bf16[192,768]{1,0:T(8,128)(2,1)S(1)}, bf16[192,768]{1,0:T(8,128)(2,1)}, u32[]{:S(2)}, u32[]{:S(2)}) collective-permute-start(bf16[192,768]{1,0:T(8,128)(2,1)S(1)} %get-tuple-element.245), channel_id=1, source_target_pairs={{0,4},{1,5},{2,6},{3,7},{4,0},{5,1},{6,2},{7,3},{8,12},{9,13},{10,... | collective-permute-start | bytes 884744 | tf_op jit(solution)/shard_map/ppermute | solution.py:1029
  136.1 23.2 %collective-permute-start.33 = (bf16[192,768]{1,0:T(8,128)(2,1)S(1)}, bf16[192,768]{1,0:T(8,128)(2,1)S(1)}, u32[]{:S(2)}, u32[]{:S(2)}) collective-permute-start(bf16[192,768]{1,0:T(8,128)(2,1)S(1)} %get-tuple-element.246), channel_id=1, source_target_pairs={{0,6},{1,7},{2,4},{3,5},{4,2},{5,3},{6,0},{7,1},{8,14},{9,15},{10,... | collective-permute-start | bytes 884744 | tf_op jit(solution)/shard_map/ppermute | solution.py:1029
  160.0 17.6 %collective-permute-start.34 = (bf16[4,144,768]{2,1,0:T(8,128)(2,1)}, bf16[4,144,768]{2,1,0:T(8,128)(2,1)}, u32[]{:S(2)}, u32[]{:S(2)}) collective-permute-start(bf16[4,144,768]{2,1,0:T(8,128)(2,1)} %get-tuple-element.249), channel_id=1, source_target_pairs={{0,1},{1,0},{2,3},{3,2},{4,5},{5,4},{6,7},{7,6},{8,9},{9,8},{10,11... | collective-permute-start | bytes 2654216 | tf_op jit(solution)/shard_map/ppermute | solution.py:1029
  161.5 16.1 %collective-permute-start.38 = (bf16[192,768]{1,0:T(8,128)(2,1)S(1)}, bf16[192,768]{1,0:T(8,128)(2,1)S(1)}, u32[]{:S(2)}, u32[]{:S(2)}) collective-permute-start(bf16[192,768]{1,0:T(8,128)(2,1)S(1)} %fusion.18), channel_id=1, source_target_pairs={{0,8},{24,16},{1,9},{25,17},{2,10},{26,18},{3,11},{27,19},{4,12},{... | collective-permute-start | bytes 884744 | tf_op jit(solution)/shard_map/ppermute | solution.py:1120
  165.1 12.4 %collective-permute-start.35 = (f32[8,768]{1,0:T(8,128)S(1)}, f32[8,768]{1,0:T(8,128)S(1)}, u32[]{:S(2)}, u32[]{:S(2)}) collective-permute-start(f32[8,768]{1,0:T(8,128)S(1)} %copy-done.3), channel_id=1, source_target_pairs={{0,8},{8,0},{16,24},{24,16},{1,9},{9,1},{17,25},{25,17},{2,10},{10... | collective-permute-start | bytes 73736 | tf_op jit(solution)/shard_map/ppermute | solution.py:1029
  165.2 12.3 %collective-permute-start.36 = (f32[8,768]{1,0:T(8,128)S(1)}, f32[8,768]{1,0:T(8,128)S(1)}, u32[]{:S(2)}, u32[]{:S(2)}) collective-permute-start(f32[8,768]{1,0:T(8,128)S(1)} %copy-done.3), channel_id=1, source_target_pairs={{0,16},{8,24},{16,0},{24,8},{1,17},{9,25},{17,1},{25,9},{2,18},{10... | collective-permute-start | bytes 73736 | tf_op jit(solution)/shard_map/ppermute | solution.py:1029
  168.1 9.4 %collective-permute-start.37 = (f32[8,768]{1,0:T(8,128)S(1)}, f32[8,768]{1,0:T(8,128)S(1)}, u32[]{:S(2)}, u32[]{:S(2)}) collective-permute-start(f32[8,768]{1,0:T(8,128)S(1)} %copy-done.3), channel_id=1, source_target_pairs={{0,24},{8,16},{16,8},{24,0},{1,25},{9,17},{17,9},{25,1},{2,26},{10... | collective-permute-start | bytes 73736 | tf_op jit(solution)/shard_map/ppermute | solution.py:1029
  178.4 17.1 %collective-permute-start.16 = (bf16[192,768]{1,0:T(8,128)(2,1)S(1)}, bf16[192,768]{1,0:T(8,128)(2,1)}, u32[]{:S(2)}, u32[]{:S(2)}) collective-permute-start(bf16[192,768]{1,0:T(8,128)(2,1)S(1)} %add_convert_fusion.3), channel_id=1, source_target_pairs={{8,16},{16,8},{9,17},{17,9},{10,18},{18,10},{11,19},{19,11},{12,20... | collective-permute-start | bytes 884744 | tf_op jit(solution)/shard_map/cond/branch_1_fun/ppermute | solution.py:1120
  181.6 12.5 %collective-permute-start.12 = (bf16[144,768]{1,0:T(8,128)(2,1)S(1)}, bf16[144,768]{1,0:T(8,128)(2,1)}, u32[]{:S(2)}, u32[]{:S(2)}) collective-permute-start(bf16[144,768]{1,0:T(8,128)(2,1)S(1)} %get-tuple-element.76), channel_id=1, source_target_pairs={{0,2},{1,3},{2,0},{3,1},{4,6},{5,7},{6,4},{7,5},{8,10},{9,11},{10,... | collective-permute-start | bytes 663560 | tf_op jit(solution)/shard_map/cond/branch_1_fun/ppermute | solution.py:1029
  182.7 11.4 %collective-permute-start.13 = (bf16[144,768]{1,0:T(8,128)(2,1)S(1)}, bf16[144,768]{1,0:T(8,128)(2,1)}, u32[]{:S(2)}, u32[]{:S(2)}) collective-permute-start(bf16[144,768]{1,0:T(8,128)(2,1)S(1)} %get-tuple-element.77), channel_id=1, source_target_pairs={{0,4},{1,5},{2,6},{3,7},{4,0},{5,1},{6,2},{7,3},{8,12},{9,13},{10,... | collective-permute-start | bytes 663560 | tf_op jit(solution)/shard_map/cond/branch_1_fun/ppermute | solution.py:1029
  183.3 10.8 %collective-permute-start.14 = (bf16[144,768]{1,0:T(8,128)(2,1)S(1)}, bf16[144,768]{1,0:T(8,128)(2,1)}, u32[]{:S(2)}, u32[]{:S(2)}) collective-permute-start(bf16[144,768]{1,0:T(8,128)(2,1)S(1)} %get-tuple-element.78), channel_id=1, source_target_pairs={{0,6},{1,7},{2,4},{3,5},{4,2},{5,3},{6,0},{7,1},{8,14},{9,15},{10,... | collective-permute-start | bytes 663560 | tf_op jit(solution)/shard_map/cond/branch_1_fun/ppermute | solution.py:1029
  185.7 8.3 %collective-permute-start.15 = (f32[8,768]{1,0:T(8,128)S(1)}, f32[8,768]{1,0:T(8,128)S(1)}, u32[]{:S(2)}, u32[]{:S(2)}) collective-permute-start(f32[8,768]{1,0:T(8,128)S(1)} %add.135), channel_id=1, source_target_pairs={{0,4},{1,5},{2,6},{3,7},{4,0},{5,1},{6,2},{7,3},{8,12},{9,13},{10,... | collective-permute-start | bytes 73736 | tf_op jit(solution)/shard_map/cond/branch_1_fun/ppermute | solution.py:1029
  195.5 16.3 %collective-permute-start.18 = (bf16[144,768]{1,0:T(8,128)(2,1)S(1)}, bf16[144,768]{1,0:T(8,128)(2,1)S(1)}, u32[]{:S(2)}, u32[]{:S(2)}) collective-permute-start(bf16[144,768]{1,0:T(8,128)(2,1)S(1)} %fusion.9), channel_id=1, source_target_pairs={{0,8},{8,0},{16,24},{24,16},{1,9},{9,1},{17,25},{25,17},{2,10},{10... | collective-permute-start | bytes 663560 | tf_op jit(solution)/shard_map/cond/branch_1_fun/ppermute | solution.py:1029
  197.5 22.4 %collective-permute-start.19 = (bf16[144,768]{1,0:T(8,128)(2,1)S(1)}, bf16[144,768]{1,0:T(8,128)(2,1)S(1)}, u32[]{:S(2)}, u32[]{:S(2)}) collective-permute-start(bf16[144,768]{1,0:T(8,128)(2,1)S(1)} %fusion.9), channel_id=1, source_target_pairs={{0,16},{8,24},{16,0},{24,8},{1,17},{9,25},{17,1},{25,9},{2,18},{10... | collective-permute-start | bytes 663560 | tf_op jit(solution)/shard_map/cond/branch_1_fun/ppermute | solution.py:1029
  200.0 19.9 %collective-permute-start.20 = (bf16[144,768]{1,0:T(8,128)(2,1)S(1)}, bf16[144,768]{1,0:T(8,128)(2,1)S(1)}, u32[]{:S(2)}, u32[]{:S(2)}) collective-permute-start(bf16[144,768]{1,0:T(8,128)(2,1)S(1)} %fusion.9), channel_id=1, source_target_pairs={{0,24},{8,16},{16,8},{24,0},{1,25},{9,17},{17,9},{25,1},{2,26},{10... | collective-permute-start | bytes 663560 | tf_op jit(solution)/shard_map/cond/branch_1_fun/ppermute | solution.py:1029
  202.6 29.1 %collective-permute-start.21 = (bf16[192,768]{1,0:T(8,128)(2,1)S(1)}, bf16[192,768]{1,0:T(8,128)(2,1)S(1)}, u32[]{:S(2)}, u32[]{:S(2)}) collective-permute-start(bf16[192,768]{1,0:T(8,128)(2,1)S(1)} %add_convert_fusion.2), channel_id=1, source_target_pairs={{8,0},{16,24},{9,1},{17,25},{10,2},{18,26},{11,3},{19,27},{12,4},{... | collective-permute-start | bytes 884744 | tf_op jit(solution)/shard_map/cond/branch_1_fun/ppermute | solution.py:1120
  (32 other events, 247.4 us)
Sparse Core Ops, SparseCore 0:
  10.5 59.6 all-gather.4
  99.8 75.9 reduce-scatter.1
  178.3 58.2 all-reduce.2
